TPU v7x, 256 devices: a whole 4x4x8 slice. The times are simulated.
256 devices in a mesh: inst: 4 (over y_lo, core), dom: 64 (over x, y_hi, z).
Axes of the slice: x: 4, y: 4 (y_hi: 2, y_lo: 2; y = y_hi * 2 + y_lo), z: 8, core: 2. Of those that a mesh axis runs over, the one named last changes fastest.
Arguments:
- state: float32 [8, 40, 8192], P('inst', None, 'dom'), may hold values from -6 to 6
- element_jacobian_blocks: float32 [8, 40, 40, 8192], P('inst', None, None, 'dom'), may hold values from -1 to 1
- face_blocks: float32 [8, 20, 20, 49152], P('inst', None, None, 'dom'), may hold values from -1.25 to 1.25
- mass: float32 [8, 8192], P(None, 'dom'), may hold values from 0.3 to 3
- counts: int32 [64], P('dom'), may hold values from 64 to 128, as said below
- face_owner: int32 [49152], P('dom'), may hold values from 0 to 127, as said below
- face_side: int32 [49152], P('dom'), may hold values from 0 to 5
- face_part: int32 [49152], P('dom'), may hold values from 0 to 63, as said below
- face_nbr: int32 [49152], P('dom'), may hold values from 0 to 127, as said below
Outputs:
- first: float32 [8, 40, 8192], P('inst', None, 'dom')
- second: float32 [8, 40, 8192], P('inst', None, 'dom')
Inputs may be any that keep to these rules, and one draw needn't show every extreme that they name: `counts`: some partition uses all 128 slots. `face_owner`: below the count of the entry's partition. `face_part`: differs from the entry's partition by -2, -1, 0, 1 or 2 around the closed loop of 64 partitions; of one partition's entries each of the four other partitions so reached is named by 64 to 128 of them, and in every partition one of them by exactly 128. `face_nbr`: below the count of the neighbour's partition.
All inputs are finite; a program needn't handle non-finite values.
Results may differ from a plain program's by a relative error of at most 0.00008.
Values sent between devices are 32-bit elements; how exact they have to be, the bound alone decides.
No kernel may reach another device: no remote copies, remote signals or barrier semaphores. Data moves between devices by JAX's collectives and lax.ppermute only.
A program may use at most 128 MiB of HBM per device.

v0:
```python
import math

import jax
import jax.numpy as jnp
from jax import lax
from jax.sharding import PartitionSpec as P

TOP_PRECISION = lax.Precision.HIGHEST
OMEGA = 1.0
OFFSETS = (-2, -1, 1, 2)


def from_behind(value, axis, by):
    length = lax.axis_size(axis)
    return lax.ppermute(value, axis, [(i, (i + by) % length) for i in range(length)])


def spectral_table(total):
    entries = []
    for target in range(total):
        row_values = []
        for source in range(total):
            spacing = target - source
            wrapped = spacing % total
            if wrapped != 0 and 2 * wrapped != total:
                row_values.append(
                    0.5 * OMEGA * (-1.0) ** spacing / math.tan(math.pi * spacing / total)
                )
            else:
                row_values.append(0.0)
        entries.append(row_values)
    return jnp.asarray(entries, dtype=jnp.float32)


def trace_rows():
    result = []
    for side in range(6):
        corners = [corner for corner in range(8) if corner >> side // 2 & 1 == side % 2]
        row_values = []
        for variable in range(5):
            for within in range(4):
                row_values.append(variable * 8 + corners[within])
        result.append(row_values)
    return result


def face_index(sides):
    lookup = jnp.asarray(trace_rows(), dtype=jnp.int32)
    matched = (sides[:, None] == jnp.arange(6, dtype=jnp.int32)[None, :]).astype(jnp.int32)
    return jnp.dot(matched, lookup)


def extract(states, columns, sides):
    picked = jnp.take(states, columns, axis=2)
    row_index = jnp.transpose(face_index(sides))[None, :, :]
    return jnp.take_along_axis(picked, row_index, axis=1)


def on_device(
    state,
    element_jacobian_blocks,
    face_blocks,
    mass,
    counts,
    face_owner,
    face_side,
    face_part,
    face_nbr,
):
    local_inst = state.shape[0]
    elements = state.shape[2]
    face_total = face_side.shape[0]
    part_total = lax.axis_size("dom")
    my_part = lax.axis_index("dom")
    inst_total = lax.axis_size("inst")
    my_inst = lax.axis_index("inst")
    live = (jnp.arange(elements, dtype=jnp.int32) < counts[0]).astype(jnp.float32)
    mass_rows = jnp.tile(mass, (5, 1))
    owner_rows = jnp.transpose(face_index(face_side))
    owner_grid = jnp.broadcast_to(face_owner[None, :], owner_rows.shape)
    far_sides = jnp.bitwise_xor(face_side, 1)
    offset_of = jnp.mod(face_part - my_part + 2, part_total) - 2
    full_table = spectral_table(local_inst * inst_total)
    coupling = lax.dynamic_slice_in_dim(full_table, my_inst * local_inst, local_inst, 0)
    pooled_index = 4 * elements + jnp.arange(face_total, dtype=jnp.int32)
    served_elements = []
    served_sides = []
    for bucket, offset in enumerate(OFFSETS):
        member = offset_of == offset
        ranking = jnp.cumsum(member.astype(jnp.int32)) - 1
        pooled_index = jnp.where(member, bucket * elements + ranking, pooled_index)
        target_slot = jnp.where(member, ranking, elements)
        wanted = (
            jnp.zeros((elements,), jnp.int32)
            .at[target_slot]
            .set(face_nbr * 6 + far_sides, mode="drop")
        )
        incoming = from_behind(wanted, "dom", offset)
        served_elements.append(incoming // 6)
        served_sides.append(incoming % 6)

    def neighbour_traces(vector):
        gathered = []
        for bucket, offset in enumerate(OFFSETS):
            outgoing = extract(vector, served_elements[bucket], served_sides[bucket])
            gathered.append(from_behind(outgoing, "dom", -offset))
        gathered.append(extract(vector, face_nbr, far_sides))
        return jnp.take(jnp.concatenate(gathered, axis=2), pooled_index, axis=2)

    def time_term(vector):
        summed = jnp.einsum(
            "ts,sre->tre",
            coupling,
            lax.all_gather(vector, "inst", axis=0, tiled=True),
            precision=TOP_PRECISION,
        )
        return mass_rows * summed

    def apply_jacobian(vector):
        element_term = jnp.einsum(
            "tije,tje->tie", element_jacobian_blocks, vector, precision=TOP_PRECISION
        )
        across = jnp.einsum(
            "tijf,tjf->tif", face_blocks, neighbour_traces(vector), precision=TOP_PRECISION
        )
        face_contribution = jnp.zeros_like(vector).at[:, owner_rows, owner_grid].add(across)
        return live * (element_term + face_contribution + time_term(vector))

    first = apply_jacobian(state * live)
    second = apply_jacobian(first)
    return (first, second)


def solution(mesh):
    placed = (
        P("inst", None, "dom"),
        P("inst", None, None, "dom"),
        P("inst", None, None, "dom"),
        P(None, "dom"),
        P("dom"),
        P("dom"),
        P("dom"),
        P("dom"),
        P("dom"),
    )
    return jax.shard_map(
        on_device,
        mesh=mesh,
        in_specs=placed,
        out_specs=(P("inst", None, "dom"), P("inst", None, "dom")),
        check_vma=False,
    )
```

profile of v0, /device:TPU:1, one launch (start us, length us, event | category | flops | bytes accessed | tf_op | source)
XLA Modules:
  0.0 1090.8 jit_solution(13469021113804710104)
XLA Ops:
  12.6 8.9 collective-permute-start.2
  41.0 7.2 all_gather.6
  48.5 3.9 select_bitcast_fusion.3
  53.7 13.2 %copy.96 = f32[2,40,768]{0,2,1:T(8,128)} copy(f32[2,40,768]{1,0,2:T(2,128)S(1)} %select_bitcast_fusion.3) | data formatting | bytes 491520 | tf_op jit(solution)/shard_map/jit(_take)/select_n | solution.py:54
  66.9 222.0 %gather_fusion.9 = f32[15360,2]{1,0:T(8,128)} fusion(f32[2,40,768]{0,2,1:T(8,128)} %copy.96, s32[15360]{0:T(1024)S(1)} %reshape.523), kind=kCustom, calls=%fused_computation.3.clone | custom fusion | bytes 368640 | tf_op jit(solution)/shard_map/jit(take_along_axis)/gather | solution.py:56
  289.0 5.0 copy.97
  297.8 3.5 copy.90
  301.3 37.4 %gather_fusion.3 = f32[2560,2]{1,0:T(8,128)} fusion(f32[2,40,128]{0,2,1:T(8,128)} %copy.90, s32[2560]{0:T(1024)S(1)} %fusion.16), kind=kCustom, calls=%fused_computation.12.clone | custom fusion | bytes 61440 | tf_op jit(solution)/shard_map/jit(take_along_axis)/gather | solution.py:56
  341.9 3.5 copy.88
  345.4 37.4 %gather_fusion.1 = f32[2560,2]{1,0:T(8,128)} fusion(f32[2,40,128]{0,2,1:T(8,128)} %copy.88, s32[2560]{0:T(1024)S(1)} %fusion.17), kind=kCustom, calls=%fused_computation.1.clone | custom fusion | bytes 61440 | tf_op jit(solution)/shard_map/jit(take_along_axis)/gather | solution.py:56
  386.1 3.5 copy.92
  389.5 37.4 %gather_fusion.5 = f32[2560,2]{1,0:T(8,128)} fusion(f32[2,40,128]{0,2,1:T(8,128)} %copy.92, s32[2560]{0:T(1024)S(1)} %fusion.15), kind=kCustom, calls=%fused_computation.13.clone | custom fusion | bytes 61440 | tf_op jit(solution)/shard_map/jit(take_along_axis)/gather | solution.py:56
  428.7 7.1 collective-permute-start.5
  436.9 3.5 copy.94
  440.4 37.4 %gather_fusion.7 = f32[2560,2]{1,0:T(8,128)} fusion(f32[2,40,128]{0,2,1:T(8,128)} %copy.94, s32[2560]{0:T(1024)S(1)} %fusion.14), kind=kCustom, calls=%fused_computation.14.clone | custom fusion | bytes 61440 | tf_op jit(solution)/shard_map/jit(take_along_axis)/gather | solution.py:56
  484.7 4.2 gather_fusion.10
  488.9 3.7 select_bitcast_fusion.2
  496.3 4.6 copy.135
  500.9 83.3 %scatter_fusion = f32[2,5120]{0,1:T(8,128)S(1)} fusion(f32[2,5120]{0,1:T(8,128)S(1)} %copy.99, s32[15360]{0:T(1024)S(1)} %copy-done.4, f32[15360,2]{1,0:T(8,128)} %bitcast.221), kind=kCustom, calls=%fused_computation.26 | custom fusion | flops 30720 | bytes 430080
  596.8 13.2 %copy.112 = f32[2,40,768]{0,2,1:T(8,128)} copy(f32[2,40,768]{1,0,2:T(2,128)S(1)} %select_bitcast_fusion.1) | data formatting | bytes 491520 | tf_op jit(solution)/shard_map/jit(_take)/select_n | solution.py:54
  610.1 222.0 %gather_fusion.20 = f32[15360,2]{1,0:T(8,128)} fusion(f32[2,40,768]{0,2,1:T(8,128)} %copy.112, s32[15360]{0:T(1024)S(1)} %reshape.523), kind=kCustom, calls=%fused_computation.20.clone | custom fusion | bytes 368640 | tf_op jit(solution)/shard_map/jit(take_along_axis)/gather | solution.py:56
  832.1 5.0 copy.113
  839.8 27.3 %gather_fusion.12 = f32[2560,2]{1,0:T(8,128)} fusion(f32[2,40,128]{0,2,1:T(8,128)S(1)} %copy.104, s32[2560]{0:T(1024)S(1)} %fusion.17), kind=kCustom, calls=%fused_computation.15.clone | custom fusion | bytes 61440 | tf_op jit(solution)/shard_map/jit(take_along_axis)/gather | solution.py:56
  872.3 27.3 %gather_fusion.14 = f32[2560,2]{1,0:T(8,128)} fusion(f32[2,40,128]{0,2,1:T(8,128)S(1)} %copy.106, s32[2560]{0:T(1024)S(1)} %fusion.16), kind=kCustom, calls=%fused_computation.16.clone | custom fusion | bytes 61440 | tf_op jit(solution)/shard_map/jit(take_along_axis)/gather | solution.py:56
  904.6 27.3 %gather_fusion.16 = f32[2560,2]{1,0:T(8,128)} fusion(f32[2,40,128]{0,2,1:T(8,128)S(1)} %copy.108, s32[2560]{0:T(1024)S(1)} %fusion.15), kind=kCustom, calls=%fused_computation.17.clone | custom fusion | bytes 61440 | tf_op jit(solution)/shard_map/jit(take_along_axis)/gather | solution.py:56
  934.3 7.1 collective-permute-start.10
  945.1 25.5 %gather_fusion.18 = f32[2560,2]{1,0:T(8,128)S(1)} fusion(f32[2,40,128]{0,2,1:T(8,128)} %copy.110, s32[2560]{0:T(1024)S(1)} %fusion.14), kind=kCustom, calls=%fused_computation.18.clone | custom fusion | bytes 61440 | tf_op jit(solution)/shard_map/jit(take_along_axis)/gather | solution.py:56
  973.7 8.4 all_gather.7
  988.0 4.2 gather_fusion.21
  992.2 3.9 select_bitcast_fusion
  999.9 4.6 copy.151
  1004.6 83.2 %scatter_fusion.1 = f32[2,5120]{0,1:T(8,128)S(1)} fusion(f32[2,5120]{0,1:T(8,128)S(1)} %copy.115, s32[15360]{0:T(1024)S(1)} %copy-done.4, f32[15360,2]{1,0:T(8,128)} %bitcast.220), kind=kCustom, calls=%fused_computation.27 | custom fusion | flops 30720 | bytes 430080
  (233 shorter events, 102.0 us)
Async XLA Ops:
  0.6 47.6 %copy-start = (f32[8,128]{1,0:T(8,128)S(1)}, f32[8,128]{1,0:T(8,128)}, u32[]{:S(2)}) copy-start(f32[8,128]{1,0:T(8,128)} %param.34) | copy-start | bytes 12292
  0.6 39.3 %copy-start.35 = (s32[6,20]{1,0:T(8,128)S(1)}, s32[6,20]{1,0:T(8,128)}, u32[]{:S(2)}) copy-start(s32[6,20]{1,0:T(8,128)} %constant.157.clone) | copy-start | bytes 1444
  0.7 39.3 %copy-start.24 = (s32[768]{0:T(1024)S(1)}, s32[768]{0:T(1024)}, u32[]{:S(2)}) copy-start(s32[768]{0:T(1024)} %param.37) | copy-start | bytes 9220
  0.7 47.6 %copy-start.10 = (s32[768]{0:T(1024)S(1)}, s32[768]{0:T(1024)}, u32[]{:S(2)}) copy-start(s32[768]{0:T(1024)} %param.36) | copy-start | bytes 9220
  2.0 46.3 %copy-start.34 = (s32[2]{0:T(128)S(1)}, s32[2]{0:T(128)}, u32[]{:S(2)}) copy-start(s32[2]{0:T(128)} %constant.163) | copy-start | bytes 28
  6.1 290.0 %collective-permute-start.4 = (s32[128]{0:T(128)S(1)}, s32[128]{0:T(128)S(1)}, u32[]{:S(2)}, u32[]{:S(2)}) collective-permute-start(s32[128]{0:T(128)S(1)} %scatter_custom_fusion.2), channel_id=1, source_target_pairs={{0,1},{1,2},{2,3},{3,4},{4,5},{5,6},{6,7},{7,8},{8,9},{9,10},{10,1... | collective-permute-start | bytes 1544 | tf_op jit(solution)/shard_map/ppermute | solution.py:15
  12.6 282.9 %collective-permute-start.2 = (s32[128]{0:T(128)S(1)}, s32[128]{0:T(128)S(1)}, u32[]{:S(2)}, u32[]{:S(2)}) collective-permute-start(s32[128]{0:T(128)S(1)} %scatter_custom_fusion.1), channel_id=1, source_target_pairs={{0,63},{1,0},{2,1},{3,2},{4,3},{5,4},{6,5},{7,6},{8,7},{9,8},{10,9... | collective-permute-start | bytes 1544 | tf_op jit(solution)/shard_map/ppermute | solution.py:15
  25.4 270.4 %collective-permute-start = (s32[128]{0:T(128)S(1)}, s32[128]{0:T(128)S(1)}, u32[]{:S(2)}, u32[]{:S(2)}) collective-permute-start(s32[128]{0:T(128)S(1)} %scatter_custom_fusion), channel_id=1, source_target_pairs={{0,62},{1,63},{2,0},{3,1},{4,2},{5,3},{6,4},{7,5},{8,6},{9,7},{10,... | collective-permute-start | bytes 1544 | tf_op jit(solution)/shard_map/ppermute | solution.py:15
  31.3 265.1 %collective-permute-start.6 = (s32[128]{0:T(128)S(1)}, s32[128]{0:T(128)S(1)}, u32[]{:S(2)}, u32[]{:S(2)}) collective-permute-start(s32[128]{0:T(128)S(1)} %scatter_custom_fusion.3), channel_id=1, source_target_pairs={{0,2},{1,3},{2,4},{3,5},{4,6},{5,7},{6,8},{7,9},{8,10},{9,11},{10,... | collective-permute-start | bytes 1544 | tf_op jit(solution)/shard_map/ppermute | solution.py:15
  33.2 15.3 %copy-start.18 = (pred[768]{0:T(1024)(128)(4,1)}, pred[768]{0:T(1024)(128)(4,1)S(1)}, u32[]{:S(2)}) copy-start(pred[768]{0:T(1024)(128)(4,1)S(1)} %compare_and_fusion.1) | copy-start | bytes 2308
  33.9 14.5 %copy-start.33 = (s32[2]{0:T(128)S(1)}, s32[2]{0:T(128)}, u32[]{:S(2)}) copy-start(s32[2]{0:T(128)} %constant.166) | copy-start | bytes 28
  40.9 442.2 %copy-start.7 = (pred[20,768]{1,0:T(8,128)(4,1)}, pred[20,768]{1,0:T(8,128)(4,1)S(1)}, u32[]{:S(2)}) copy-start(pred[20,768]{1,0:T(8,128)(4,1)S(1)} %and_bitcast_fusion) | copy-start | bytes 46084
  296.1 88.5 %copy-start.13 = (pred[20,128]{1,0:T(8,128)(4,1)}, pred[20,128]{1,0:T(8,128)(4,1)S(1)}, u32[]{:S(2)}) copy-start(pred[20,128]{1,0:T(8,128)(4,1)S(1)} %and_bitcast_fusion.4) | copy-start | bytes 7684
  296.4 132.3 %copy-start.11 = (pred[20,128]{1,0:T(8,128)(4,1)}, pred[20,128]{1,0:T(8,128)(4,1)S(1)}, u32[]{:S(2)}) copy-start(pred[20,128]{1,0:T(8,128)(4,1)S(1)} %and_bitcast_fusion.2) | copy-start | bytes 7684
  296.8 89.1 %copy-start.25 = (pred[128]{0:T(512)(128)(4,1)}, pred[128]{0:T(512)(128)(4,1)S(1)}, u32[]{:S(2)}) copy-start(pred[128]{0:T(512)(128)(4,1)S(1)} %get-tuple-element.20) | copy-start | bytes 388
  296.8 88.3 %copy-start.21 = (s32[1024]{0:T(1024)}, s32[1024]{0:T(1024)S(1)}, u32[]{:S(2)}) copy-start(s32[1024]{0:T(1024)S(1)} %get-tuple-element.43) | copy-start | bytes 12292
  340.5 141.6 %collective-permute-start.3 = (f32[2,20,128]{2,0,1:T(2,128)S(1)}, f32[2,20,128]{2,0,1:T(2,128)S(1)}, u32[]{:S(2)}, u32[]{:S(2)}) collective-permute-start(f32[2,20,128]{2,0,1:T(2,128)S(1)} %select_bitcast_fusion.18), channel_id=1, source_target_pairs={{0,1},{1,2},{2,3},{3,4},{4,5},{5,6},{6,7},{7,8},{8,9},{9,10},{10,1... | collective-permute-start | bytes 61448 | tf_op jit(solution)/shard_map/ppermute | solution.py:15
  384.6 97.4 %collective-permute-start.1 = (f32[2,20,128]{2,0,1:T(2,128)S(1)}, f32[2,20,128]{2,0,1:T(2,128)S(1)}, u32[]{:S(2)}, u32[]{:S(2)}) collective-permute-start(f32[2,20,128]{2,0,1:T(2,128)S(1)} %select_bitcast_fusion.19), channel_id=1, source_target_pairs={{0,2},{1,3},{2,4},{3,5},{4,6},{5,7},{6,8},{7,9},{8,10},{9,11},{10,... | collective-permute-start | bytes 61448 | tf_op jit(solution)/shard_map/ppermute | solution.py:15
  428.7 53.3 %collective-permute-start.5 = (f32[2,20,128]{2,0,1:T(2,128)S(1)}, f32[2,20,128]{2,0,1:T(2,128)S(1)}, u32[]{:S(2)}, u32[]{:S(2)}) collective-permute-start(f32[2,20,128]{2,0,1:T(2,128)S(1)} %select_bitcast_fusion.17), channel_id=1, source_target_pairs={{0,63},{1,0},{2,1},{3,2},{4,3},{5,4},{6,5},{7,6},{8,7},{9,8},{10,9... | collective-permute-start | bytes 61448 | tf_op jit(solution)/shard_map/ppermute | solution.py:15
  479.5 3.6 collective-permute-start.7
  593.8 379.9 %copy-start.9 = (f32[2,40,128]{2,1,0:T(8,128)}, f32[2,40,128]{2,1,0:T(8,128)S(1)}, u32[]{:S(2)}) copy-start(f32[2,40,128]{2,1,0:T(8,128)S(1)} %copy.118) | copy-start | bytes 122884
  839.7 29.1 %copy-start.14 = (pred[20,128]{1,0:T(8,128)(4,1)S(1)}, pred[20,128]{1,0:T(8,128)(4,1)}, u32[]{:S(2)}) copy-start(pred[20,128]{1,0:T(8,128)(4,1)} %copy-done.13) | copy-start | bytes 7684
  839.8 29.9 %copy-start.28 = (pred[128]{0:T(512)(128)(4,1)S(1)}, pred[128]{0:T(512)(128)(4,1)}, u32[]{:S(2)}) copy-start(pred[128]{0:T(512)(128)(4,1)} %copy-done.27) | copy-start | bytes 388
  869.4 114.8 %collective-permute-start.8 = (f32[2,20,128]{2,0,1:T(2,128)}, f32[2,20,128]{2,0,1:T(2,128)}, u32[]{:S(2)}, u32[]{:S(2)}) collective-permute-start(f32[2,20,128]{2,0,1:T(2,128)} %select_bitcast_fusion.15), channel_id=1, source_target_pairs={{0,2},{1,3},{2,4},{3,5},{4,6},{5,7},{6,8},{7,9},{8,10},{9,11},{10,... | collective-permute-start | bytes 61448 | tf_op jit(solution)/shard_map/ppermute | solution.py:15
  872.3 29.7 %copy-start.26 = (pred[128]{0:T(512)(128)(4,1)S(1)}, pred[128]{0:T(512)(128)(4,1)}, u32[]{:S(2)}) copy-start(pred[128]{0:T(512)(128)(4,1)} %copy-done.25) | copy-start | bytes 388
  901.9 83.1 %collective-permute-start.9 = (f32[2,20,128]{2,0,1:T(2,128)}, f32[2,20,128]{2,0,1:T(2,128)}, u32[]{:S(2)}, u32[]{:S(2)}) collective-permute-start(f32[2,20,128]{2,0,1:T(2,128)} %select_bitcast_fusion.14), channel_id=1, source_target_pairs={{0,1},{1,2},{2,3},{3,4},{4,5},{5,6},{6,7},{7,8},{8,9},{9,10},{10,1... | collective-permute-start | bytes 61448 | tf_op jit(solution)/shard_map/ppermute | solution.py:15
  904.6 29.0 %copy-start.12 = (pred[20,128]{1,0:T(8,128)(4,1)S(1)}, pred[20,128]{1,0:T(8,128)(4,1)}, u32[]{:S(2)}) copy-start(pred[20,128]{1,0:T(8,128)(4,1)} %copy-done.11) | copy-start | bytes 7684
  904.6 36.8 %copy-start.5 = (f32[128,2,40]{2,1,0:T(2,128)S(1)}, f32[128,2,40]{2,1,0:T(2,128)}, u32[]{:S(2)}) copy-start(f32[128,2,40]{2,1,0:T(2,128)} %gather_fusion.17) | copy-start | bytes 122884
  904.6 36.7 %copy-start.30 = (pred[128]{0:T(512)(128)(4,1)S(1)}, pred[128]{0:T(512)(128)(4,1)}, u32[]{:S(2)}) copy-start(pred[128]{0:T(512)(128)(4,1)} %copy-done.29) | copy-start | bytes 388
  934.3 51.4 %collective-permute-start.10 = (f32[2,20,128]{2,0,1:T(2,128)}, f32[2,20,128]{2,0,1:T(2,128)}, u32[]{:S(2)}, u32[]{:S(2)}) collective-permute-start(f32[2,20,128]{2,0,1:T(2,128)} %select_bitcast_fusion.13), channel_id=1, source_target_pairs={{0,63},{1,0},{2,1},{3,2},{4,3},{5,4},{6,5},{7,6},{8,7},{9,8},{10,9... | collective-permute-start | bytes 61448 | tf_op jit(solution)/shard_map/ppermute | solution.py:15
  945.1 37.1 %copy-start.3 = (f32[2,40,40,128]{3,2,1,0:T(8,128)S(1)}, f32[2,40,40,128]{3,2,1,0:T(8,128)}, u32[]{:S(2)}) copy-start(f32[2,40,40,128]{3,2,1,0:T(8,128)} %param.32) | copy-start | bytes 4915204
  971.0 15.4 %collective-permute-start.11 = (f32[2,20,128]{2,0,1:T(2,128)S(1)}, f32[2,20,128]{2,0,1:T(2,128)S(1)}, u32[]{:S(2)}, u32[]{:S(2)}) collective-permute-start(f32[2,20,128]{2,0,1:T(2,128)S(1)} %select_bitcast_fusion.12), channel_id=1, source_target_pairs={{0,62},{1,63},{2,0},{3,1},{4,2},{5,3},{6,4},{7,5},{8,6},{9,7},{10,... | collective-permute-start | bytes 61448 | tf_op jit(solution)/shard_map/ppermute | solution.py:15
  (16 other events, 75.2 us)
where the time goes:
time: 1100 us; the launch traced here: 1090 us
  local copies, waits for them, and re-layouts  835 us (76%)
  other arithmetic  198 us (18%)
  starting transfers between devices  34.5 us (3%)
  blocking collectives  15.6 us (1%)
    gather x21, local copies, waits for them, and re-layouts, extract(): return jnp.take_along_axis(picked, row_index, axis=1)  724 us
    unnamed x13, other arithmetic  181 us
    select_n x10, local copies, waits for them, and re-layouts, extract(): picked = jnp.take(states, columns, axis=2)  51.1 us
    ppermute x12, starting transfers between devices, from_behind(): lax.ppermute(value, axis, [(i, (i + by) % length) for i in range(length)])  34.5 us
  transfers between devices with their start and end apart: 12, of which 1 were waited for; matrix products, arithmetic and copies ran while one was open for 46% of the time, Pallas kernels for 0%

commit v1 on v0

v1 whole, which is shorter than its diff:
```python
import functools
import math

import jax
import jax.numpy as jnp
from jax import lax
from jax.experimental import pallas as pl
from jax.experimental.pallas import tpu as pltpu
from jax.sharding import PartitionSpec as P

OMEGA = 1.0
OFFSETS = (-2, -1, 1, 2)


def spectral(spacing, total):
    wrapped = spacing % total
    if wrapped == 0 or 2 * wrapped == total:
        return 0.0
    return 0.5 * OMEGA * (-1.0) ** wrapped / math.tan(math.pi * wrapped / total)


def pull(value, axis, offset):
    length = lax.axis_size(axis)
    return lax.ppermute(value, axis, [((i + offset) % length, i) for i in range(length)])


def sublanes():
    return lax.broadcasted_iota(jnp.int32, (8, 128), 0)


def fold_rows(tiles):
    row = sublanes()
    step = 1
    while len(tiles) > 1:
        keep = (row & step) == 0
        merged = []
        for first, second in zip(tiles[0::2], tiles[1::2]):
            own = jnp.where(keep, first, second)
            other = jnp.where(keep, second, first)
            merged.append(own + pltpu.roll(other, 8 - step, 0))
        tiles = merged
        step *= 2
    return tiles[0]


def element_kernel(vector_ref, blocks_ref, out_ref):
    insts, unknowns, _ = vector_ref.shape
    for t in range(insts):
        tiles = [vector_ref[t, 8 * g : 8 * g + 8, :] for g in range(unknowns // 8)]
        for group in range(unknowns // 8):
            partial = []
            for i in range(8 * group, 8 * group + 8):
                total = blocks_ref[t, i, 0:8, :] * tiles[0]
                for g in range(1, unknowns // 8):
                    total += blocks_ref[t, i, 8 * g : 8 * g + 8, :] * tiles[g]
                partial.append(total)
            out_ref[t, 8 * group : 8 * group + 8, :] = fold_rows(partial)


def element_term(vector, blocks):
    return pl.pallas_call(
        element_kernel,
        out_shape=jax.ShapeDtypeStruct(vector.shape, jnp.float32),
        in_specs=[pl.BlockSpec(memory_space=pltpu.VMEM)] * 2,
        out_specs=pl.BlockSpec(memory_space=pltpu.VMEM),
        cost_estimate=pl.CostEstimate(
            flops=2 * blocks.size, bytes_accessed=4 * blocks.size, transcendentals=0
        ),
        compiler_params=pltpu.CompilerParams(vmem_limit_bytes=32 * 2**20),
    )(vector, blocks)


def corner_of(side, within):
    axis, end = side >> 1, side & 1
    return jnp.where(
        axis == 0,
        2 * within + end,
        jnp.where(
            axis == 1,
            (within & 1) + 2 * end + 4 * (within >> 1),
            4 * end + within,
        ),
    )


def within_of(side, corner):
    axis, end = side >> 1, side & 1
    place = jnp.where(
        axis == 0,
        corner >> 1,
        jnp.where(axis == 1, (corner & 1) + 2 * (corner >> 2), corner & 3),
    )
    held = ((corner >> axis) & 1) == end
    return place, held


def face_kernel(
    instances,
    part_total,
    counts_ref,
    my_ref,
    owner_ref,
    side_ref,
    part_ref,
    nbr_ref,
    mass_ref,
    element_ref,
    blocks_ref,
    own_ref,
    *rest,
):
    neighbour_refs = rest[: len(OFFSETS)]
    instance_refs = rest[len(OFFSETS) : len(OFFSETS) + instances - 1]
    out_ref, trace_ref, across_ref, spread_ref = rest[len(OFFSETS) + instances - 1 :]
    insts, unknowns, elements = own_ref.shape
    variables = unknowns // 8
    width = 4 * variables
    lane_tiles = owner_ref.shape[0]
    stride = lane_tiles * insts
    row = sublanes()
    shape = (8, 128)

    def wide(ref, tile):
        return jnp.broadcast_to(ref[tile : tile + 1, :], shape)

    for tile in range(lane_tiles):
        column = wide(nbr_ref, tile)
        offset = wide(part_ref, tile) - my_ref[0]
        offset = jnp.where(offset > 2, offset - part_total, offset)
        offset = jnp.where(offset < -2, offset + part_total, offset)
        chosen = [offset == o for o in OFFSETS]
        corner = corner_of(wide(side_ref, tile) ^ 1, row & 3)
        for t in range(insts):
            traces = []
            for a in range(variables):
                rows = slice(8 * a, 8 * a + 8)
                picked = jnp.take_along_axis(
                    own_ref[t, rows, :], column, axis=1, mode="promise_in_bounds"
                )
                for mask, ref in zip(chosen, neighbour_refs):
                    picked = jnp.where(
                        mask,
                        jnp.take_along_axis(
                            ref[t, rows, :], column, axis=1, mode="promise_in_bounds"
                        ),
                        picked,
                    )
                traces.append(
                    jnp.take_along_axis(picked, corner, axis=0, mode="promise_in_bounds")
                )
            for a in range(0, variables, 2):
                start = 4 * a * stride + tile * insts + t
                if a + 1 < variables:
                    pair = jnp.where(row < 4, traces[a], traces[a + 1])
                    trace_ref[pl.ds(start, 8, stride=stride), :] = pair
                else:
                    trace_ref[pl.ds(start, 4, stride=stride), :] = traces[a][0:4, :]

    pair_rows = 2 * stride
    for i in range(width):
        total = None
        for p in range(width // 2):
            base = (i * width + 2 * p) * stride
            term = (
                blocks_ref[base : base + pair_rows, :]
                * trace_ref[p * pair_rows : (p + 1) * pair_rows, :]
            )
            total = term if total is None else total + term
        across_ref[i * pair_rows : (i + 1) * pair_rows, :] = total

    for tile in range(lane_tiles):
        place, held = within_of(wide(side_ref, tile), row)
        for t in range(insts):
            for a in range(variables):
                start = 4 * (a // 2) * 2 * pair_rows + tile * insts + t
                if a % 2 == 0:
                    here = across_ref[pl.ds(start, 8, stride=pair_rows), :]
                    here += across_ref[pl.ds(start + stride, 8, stride=pair_rows), :]
                moved = jnp.take_along_axis(
                    here, place + 4 * (a % 2), axis=0, mode="promise_in_bounds"
                )
                spread_ref[
                    (t * variables + a) * 8 : (t * variables + a) * 8 + 8,
                    tile * 128 : tile * 128 + 128,
                ] = jnp.where(held, moved, 0.0)

    slot = lax.broadcasted_iota(jnp.int32, (elements, 128), 0)
    owned = jnp.concatenate(
        [
            (jnp.broadcast_to(owner_ref[tile : tile + 1, :], slot.shape) == slot)
            for tile in range(lane_tiles)
        ],
        axis=1,
    )
    owned = jnp.where(owned, 1.0, 0.0).astype(jnp.bfloat16)
    spread = spread_ref[...]
    high = spread.astype(jnp.bfloat16)
    low = (spread - high.astype(jnp.float32)).astype(jnp.bfloat16)
    dims = (((1,), (1,)), ((), ()))
    landed = lax.dot_general(high, owned, dims, preferred_element_type=jnp.float32)
    landed += lax.dot_general(low, owned, dims, preferred_element_type=jnp.float32)

    live = lax.broadcasted_iota(jnp.int32, shape, 1) < counts_ref[0]
    mass = mass_ref[...]
    total_insts = insts * instances
    sources = (own_ref, *instance_refs)
    for t in range(insts):
        for a in range(variables):
            rows = slice(8 * a, 8 * a + 8)
            summed = None
            for k, ref in enumerate(sources):
                for s in range(insts):
                    weight = spectral(t - s - insts * k, total_insts)
                    if weight != 0.0:
                        term = weight * ref[s, rows, :]
                        summed = term if summed is None else summed + term
            base = (t * variables + a) * 8
            value = element_ref[t, rows, :] + landed[base : base + 8, :] + mass * summed
            out_ref[t, rows, :] = jnp.where(live, value, 0.0)


def face_and_time_term(
    counts, my_part, owner, side, part, nbr, mass, element, blocks, own, neighbours, others
):
    part_total = lax.axis_size("dom")
    instances = lax.axis_size("inst")
    insts, unknowns, _ = own.shape
    width = unknowns // 2
    stride = owner.shape[0] * insts
    vmem = pl.BlockSpec(memory_space=pltpu.VMEM)
    smem = pl.BlockSpec(memory_space=pltpu.SMEM)
    return pl.pallas_call(
        functools.partial(face_kernel, instances, part_total),
        out_shape=jax.ShapeDtypeStruct(own.shape, jnp.float32),
        in_specs=[smem, smem] + [vmem] * (8 + len(neighbours) + len(others)),
        out_specs=vmem,
        scratch_shapes=[
            pltpu.VMEM((width * stride, 128), jnp.float32),
            pltpu.VMEM(((width + 4) * 2 * stride, 128), jnp.float32),
            pltpu.VMEM((insts * unknowns, owner.shape[0] * 128), jnp.float32),
        ],
        cost_estimate=pl.CostEstimate(
            flops=2 * blocks.size, bytes_accessed=4 * blocks.size, transcendentals=0
        ),
        compiler_params=pltpu.CompilerParams(vmem_limit_bytes=32 * 2**20),
    )(counts, my_part, owner, side, part, nbr, mass, element, blocks, own, *neighbours, *others)


def on_device(
    state,
    element_jacobian_blocks,
    face_blocks,
    mass,
    counts,
    face_owner,
    face_side,
    face_part,
    face_nbr,
):
    insts, rows, columns, faces = face_blocks.shape
    tiles = faces // 128
    blocks = face_blocks.reshape(insts, rows, columns, tiles, 128)
    blocks = jnp.transpose(blocks, (1, 2, 3, 0, 4)).reshape(-1, 128)
    owner, side, part, nbr = (
        x.reshape(tiles, 128) for x in (face_owner, face_side, face_part, face_nbr)
    )
    my_part = lax.axis_index("dom").astype(jnp.int32).reshape(1)

    def apply_jacobian(vector):
        neighbours = [pull(vector, "dom", o) for o in OFFSETS]
        others = [pull(vector, "inst", k) for k in range(1, lax.axis_size("inst"))]
        element = element_term(vector, element_jacobian_blocks)
        return face_and_time_term(
            counts, my_part, owner, side, part, nbr, mass, element, blocks, vector,
            neighbours, others,
        )

    first = apply_jacobian(state)
    second = apply_jacobian(first)
    return first, second


def solution(mesh):
    placed = (
        P("inst", None, "dom"),
        P("inst", None, None, "dom"),
        P("inst", None, None, "dom"),
        P(None, "dom"),
        P("dom"),
        P("dom"),
        P("dom"),
        P("dom"),
        P("dom"),
    )
    return jax.shard_map(
        on_device,
        mesh=mesh,
        in_specs=placed,
        out_specs=(P("inst", None, "dom"), P("inst", None, "dom")),
        check_vma=False,
    )
```

time: 1100 us -> 48.2 us (0.04)
  local copies, waits for them, and re-layouts: 835 us -> 10.4 us
  other arithmetic: 198 us -> 0 us
  blocking collectives: 15.6 us -> 0 us
    gather x33 -> x0, local copies, waits for them, and re-layouts: 746 us -> none  [the longest x21 724 us: extract(): return jnp.take_along_axis(picked, row_index, axis=1)]
    unnamed x13 -> x0, other arithmetic: 181 us -> none
    select_n x10 -> x0, local copies, waits for them, and re-layouts: 51.1 us -> none  [extract(): picked = jnp.take(states, columns, axis=2)]
    all_gather x2 -> x0, blocking collectives: 15.6 us -> none  [time_term(): lax.all_gather(vector, 'inst', axis=0, tiled=True)]
    scatter x4 -> x0, local copies, waits for them, and re-layouts: 13.5 us -> none  [on_device(): wanted = jnp.zeros((elements,), jnp.int32).at[target_slot].set(face_nbr *...]
    ppermute x12 -> x14, starting transfers between devices: 34.5 us -> 29 us  [pull(): lax.ppermute(value, axis, [((i + offset) % length, i) for i in range(leng...]
  transfers between devices with their start and end apart: 12 -> 14, of which waited for: 1 -> 3; matrix products, arithmetic and copies ran while one was open for 46% -> 17% of each run, Pallas kernels for 0% -> 1%
where the time goes in v1:
time: 48.2 us; the launch traced here: 47.9 us
  starting transfers between devices  29 us (60%)
  local copies, waits for them, and re-layouts  10.4 us (22%)
  waiting for transfers between devices  3.79 us (8%)
  Pallas kernels  3.28 us (7%)
  between operations  1.43 us (3%)
    ppermute x14, starting transfers between devices, pull(): lax.ppermute(value, axis, [((i + offset) % length, i) for i in range(leng...  29 us
    reshape x1, local copies, waits for them, and re-layouts, on_device(): blocks = face_blocks.reshape(insts, rows, columns, tiles, 128)  4.91 us
    ppermute x14, waiting for transfers between devices, pull(): lax.ppermute(value, axis, [((i + offset) % length, i) for i in range(leng...  3.79 us
    transpose x1, local copies, waits for them, and re-layouts, on_device(): blocks = jnp.transpose(blocks, (1, 2, 3, 0, 4)).reshape(-1, 128)  3.25 us
    pallas_call x2, Pallas kernels, face_and_time_term(): pl.pallas_call(functools.partial(face_kernel, instances, part_total), out...  3 us
    unnamed x18, local copies, waits for them, and re-layouts  2.27 us
  transfers between devices with their start and end apart: 14, of which 3 were waited for; matrix products, arithmetic and copies ran while one was open for 17% of the time, Pallas kernels for 1%

profile of v1, /device:TPU:1, one launch (start us, length us, event | category | flops | bytes accessed | tf_op | source)
XLA Modules:
  0.0 47.9 jit_solution(9722243709461722278)
XLA Ops:
  0.6 3.9 %collective-permute-start = (f32[2,40,128]{2,1,0:T(8,128)}, f32[2,40,128]{2,1,0:T(8,128)S(1)}, u32[]{:S(2)}, u32[]{:S(2)}) collective-permute-start(f32[2,40,128]{2,1,0:T(8,128)} %own_ref.1), channel_id=1, source_target_pairs={{62,0},{63,1},{0,2},{1,3},{2,4},{3,5},{4,6},{5,7},{6,8},{7,9},{8,1... | collective-permute-start | bytes 122888 | tf_op jit(solution)/shard_map/ppermute | solution.py:24
  4.5 1.6 %collective-permute-start.1 = (f32[2,40,128]{2,1,0:T(8,128)}, f32[2,40,128]{2,1,0:T(8,128)S(1)}, u32[]{:S(2)}, u32[]{:S(2)}) collective-permute-start(f32[2,40,128]{2,1,0:T(8,128)} %own_ref.1), channel_id=1, source_target_pairs={{63,0},{0,1},{1,2},{2,3},{3,4},{4,5},{5,6},{6,7},{7,8},{8,9},{9,10... | collective-permute-start | bytes 122888 | tf_op jit(solution)/shard_map/ppermute | solution.py:24
  6.2 6.0 %collective-permute-start.2 = (f32[2,40,128]{2,1,0:T(8,128)}, f32[2,40,128]{2,1,0:T(8,128)S(1)}, u32[]{:S(2)}, u32[]{:S(2)}) collective-permute-start(f32[2,40,128]{2,1,0:T(8,128)} %own_ref.1), channel_id=1, source_target_pairs={{1,0},{2,1},{3,2},{4,3},{5,4},{6,5},{7,6},{8,7},{9,8},{10,9},{11,1... | collective-permute-start | bytes 122888 | tf_op jit(solution)/shard_map/ppermute | solution.py:24
  12.1 2.2 %collective-permute-start.3 = (f32[2,40,128]{2,1,0:T(8,128)}, f32[2,40,128]{2,1,0:T(8,128)S(1)}, u32[]{:S(2)}, u32[]{:S(2)}) collective-permute-start(f32[2,40,128]{2,1,0:T(8,128)} %own_ref.1), channel_id=1, source_target_pairs={{2,0},{3,1},{4,2},{5,3},{6,4},{7,5},{8,6},{9,7},{10,8},{11,9},{12,... | collective-permute-start | bytes 122888 | tf_op jit(solution)/shard_map/ppermute | solution.py:24
  14.3 1.5 %collective-permute-start.4 = (f32[2,40,128]{2,1,0:T(8,128)}, f32[2,40,128]{2,1,0:T(8,128)S(1)}, u32[]{:S(2)}, u32[]{:S(2)}) collective-permute-start(f32[2,40,128]{2,1,0:T(8,128)} %own_ref.1), channel_id=1, source_target_pairs={{64,0},{128,64},{192,128},{0,192},{65,1},{129,65},{193,129},{1,193... | collective-permute-start | bytes 122888 | tf_op jit(solution)/shard_map/ppermute | solution.py:24
  15.8 0.4 collective-permute-start.5
  16.2 1.4 %collective-permute-start.6 = (f32[2,40,128]{2,1,0:T(8,128)}, f32[2,40,128]{2,1,0:T(8,128)S(1)}, u32[]{:S(2)}, u32[]{:S(2)}) collective-permute-start(f32[2,40,128]{2,1,0:T(8,128)} %own_ref.1), channel_id=1, source_target_pairs={{192,0},{0,64},{64,128},{128,192},{193,1},{1,65},{65,129},{129,193... | collective-permute-start | bytes 122888 | tf_op jit(solution)/shard_map/ppermute | solution.py:24
  17.6 4.9 %reshape.30 = f32[2,20,20,6,128]{4,3,0,2,1:T(8,128)} reshape(f32[2,20,20,768]{3,0,2,1:T(2,128)} %param.11) | data formatting | bytes 4915200 | tf_op jit(solution)/shard_map/reshape | solution.py:262
  22.5 0.0 copy-start.7
  22.5 0.0 copy-start.8
  22.6 3.2 %copy.12 = f32[20,20,6,2,128]{4,3,2,1,0:T(2,128)S(1)} copy(f32[20,20,6,2,128]{4,2,3,1,0:T(8,128)} %bitcast.19) | data formatting | bytes 4915200 | tf_op jit(solution)/shard_map/transpose | solution.py:263
  26.5 0.0 copy-start
  26.5 1.4 %copy-done = f32[2,40,40,128]{3,2,1,0:T(8,128)S(1)} copy-done((f32[2,40,40,128]{3,2,1,0:T(8,128)S(1)}, f32[2,40,40,128]{3,2,1,0:T(8,128)}, u32[]{:S(2)}) %copy-start) | copy-done | bytes 1638424
  27.9 0.1 shard_map.104.element_ref
  28.0 0.0 collective-permute-done.2.rest_2_
  28.1 0.0 collective-permute-done.3.rest_3_
  28.1 0.0 collective-permute-done.5.rest_5_
  28.1 0.0 collective-permute-done.6.rest_6_
  28.1 1.5 %shard_map.105.vector_ref.own_ref = f32[2,40,128]{2,1,0:T(8,128)} custom-call(s32[1]{0:T(128)S(6)} %copy.13.counts_ref, s32[1]{0:T(128)} %bitcast.my_ref, s32[6,128]{1,0:T(8,128)S(1)} %bitcast.11, s32[6,128]{1,0:T(8,128)S(1)} %bitcast.13, s32[6,128]{1,0:T(8,128)S(1)} %bitcast.15, s32[6,128]{1,0:T(8,128)S(1)} %bitcast.17, f32[8,128]{1,0:T(8,128)S(1)} %copy-done.8, ...), custom_call_target="tpu_custom_call" | custom-call | flops 1228800 | bytes 2457600 | tf_op jit(solution)/shard_map/pallas_call | solution.py:232
  29.7 3.3 %collective-permute-start.10 = (f32[2,40,128]{2,1,0:T(8,128)}, f32[2,40,128]{2,1,0:T(8,128)S(1)}, u32[]{:S(2)}, u32[]{:S(2)}) collective-permute-start(f32[2,40,128]{2,1,0:T(8,128)} %shard_map.105.vector_ref.own_ref), channel_id=1, source_target_pairs={{2,0},{3,1},{4,2},{5,3},{6,4},{7,5},{8,6},{9,7},{10,8},{11,9},{12,... | collective-permute-start | bytes 122888 | tf_op jit(solution)/shard_map/ppermute | solution.py:24
  32.9 0.2 collective-permute-start.11
  33.1 0.3 collective-permute-start.12
  33.3 2.0 %collective-permute-start.13 = (f32[2,40,128]{2,1,0:T(8,128)}, f32[2,40,128]{2,1,0:T(8,128)S(1)}, u32[]{:S(2)}, u32[]{:S(2)}) collective-permute-start(f32[2,40,128]{2,1,0:T(8,128)} %shard_map.105.vector_ref.own_ref), channel_id=1, source_target_pairs={{192,0},{0,64},{64,128},{128,192},{193,1},{1,65},{65,129},{129,193... | collective-permute-start | bytes 122888 | tf_op jit(solution)/shard_map/ppermute | solution.py:24
  35.3 0.0 collective-permute-start.7
  35.3 0.3 collective-permute-start.8
  35.6 0.9 %collective-permute-done.11.rest_4_ = f32[2,40,128]{2,1,0:T(8,128)S(1)} collective-permute-done((f32[2,40,128]{2,1,0:T(8,128)}, f32[2,40,128]{2,1,0:T(8,128)S(1)}, u32[]{:S(2)}, u32[]{:S(2)}) %collective-permute-start.11) | collective-permute-done | bytes 40992 | tf_op jit(solution)/shard_map/ppermute | solution.py:24
  36.6 6.1 %collective-permute-start.9 = (f32[2,40,128]{2,1,0:T(8,128)}, f32[2,40,128]{2,1,0:T(8,128)S(1)}, u32[]{:S(2)}, u32[]{:S(2)}) collective-permute-start(f32[2,40,128]{2,1,0:T(8,128)} %shard_map.105.vector_ref.own_ref), channel_id=1, source_target_pairs={{1,0},{2,1},{3,2},{4,3},{5,4},{6,5},{7,6},{8,7},{9,8},{10,9},{11,1... | collective-permute-start | bytes 122888 | tf_op jit(solution)/shard_map/ppermute | solution.py:24
  42.6 0.8 %copy-done.2 = f32[2,40,128]{2,1,0:T(8,128)S(1)} copy-done((f32[2,40,128]{2,1,0:T(8,128)S(1)}, f32[2,40,128]{2,1,0:T(8,128)}, u32[]{:S(2)}) %copy-start.2) | copy-done | bytes 40984
  43.4 0.1 shard_map.106.element_ref
  43.6 2.0 %collective-permute-done.7.rest_0_ = f32[2,40,128]{2,1,0:T(8,128)S(1)} collective-permute-done((f32[2,40,128]{2,1,0:T(8,128)}, f32[2,40,128]{2,1,0:T(8,128)S(1)}, u32[]{:S(2)}, u32[]{:S(2)}) %collective-permute-start.7) | collective-permute-done | bytes 40992 | tf_op jit(solution)/shard_map/ppermute | solution.py:24
  45.6 0.9 %collective-permute-done.8.rest_1_ = f32[2,40,128]{2,1,0:T(8,128)S(1)} collective-permute-done((f32[2,40,128]{2,1,0:T(8,128)}, f32[2,40,128]{2,1,0:T(8,128)S(1)}, u32[]{:S(2)}, u32[]{:S(2)}) %collective-permute-start.8) | collective-permute-done | bytes 40992 | tf_op jit(solution)/shard_map/ppermute | solution.py:24
  46.4 1.5 %shard_map.107 = f32[2,40,128]{2,1,0:T(8,128)} custom-call(s32[1]{0:T(128)S(6)} %copy.13.counts_ref, s32[1]{0:T(128)} %bitcast.my_ref, s32[6,128]{1,0:T(8,128)S(1)} %bitcast.12, s32[6,128]{1,0:T(8,128)S(1)} %bitcast.14, s32[6,128]{1,0:T(8,128)S(1)} %bitcast.16, s32[6,128]{1,0:T(8,128)S(1)} %bitcast.18, f32[8,128]{1,0:T(8,128)S(1)} %copy-done.8, ...), custom_call_target="tpu_custom_call" | custom-call | flops 1228800 | bytes 2457600 | tf_op jit(solution)/shard_map/pallas_call | solution.py:232
  (20 shorter events, 0.0 us)
Async XLA Ops:
  0.6 15.2 %collective-permute-start = (f32[2,40,128]{2,1,0:T(8,128)}, f32[2,40,128]{2,1,0:T(8,128)S(1)}, u32[]{:S(2)}, u32[]{:S(2)}) collective-permute-start(f32[2,40,128]{2,1,0:T(8,128)} %own_ref.1), channel_id=1, source_target_pairs={{62,0},{63,1},{0,2},{1,3},{2,4},{3,5},{4,6},{5,7},{6,8},{7,9},{8,1... | collective-permute-start | bytes 122888 | tf_op jit(solution)/shard_map/ppermute | solution.py:24
  4.5 11.7 %collective-permute-start.1 = (f32[2,40,128]{2,1,0:T(8,128)}, f32[2,40,128]{2,1,0:T(8,128)S(1)}, u32[]{:S(2)}, u32[]{:S(2)}) collective-permute-start(f32[2,40,128]{2,1,0:T(8,128)} %own_ref.1), channel_id=1, source_target_pairs={{63,0},{0,1},{1,2},{2,3},{3,4},{4,5},{5,6},{6,7},{7,8},{8,9},{9,10... | collective-permute-start | bytes 122888 | tf_op jit(solution)/shard_map/ppermute | solution.py:24
  6.2 21.9 %collective-permute-start.2 = (f32[2,40,128]{2,1,0:T(8,128)}, f32[2,40,128]{2,1,0:T(8,128)S(1)}, u32[]{:S(2)}, u32[]{:S(2)}) collective-permute-start(f32[2,40,128]{2,1,0:T(8,128)} %own_ref.1), channel_id=1, source_target_pairs={{1,0},{2,1},{3,2},{4,3},{5,4},{6,5},{7,6},{8,7},{9,8},{10,9},{11,1... | collective-permute-start | bytes 122888 | tf_op jit(solution)/shard_map/ppermute | solution.py:24
  12.1 15.9 %collective-permute-start.3 = (f32[2,40,128]{2,1,0:T(8,128)}, f32[2,40,128]{2,1,0:T(8,128)S(1)}, u32[]{:S(2)}, u32[]{:S(2)}) collective-permute-start(f32[2,40,128]{2,1,0:T(8,128)} %own_ref.1), channel_id=1, source_target_pairs={{2,0},{3,1},{4,2},{5,3},{6,4},{7,5},{8,6},{9,7},{10,8},{11,9},{12,... | collective-permute-start | bytes 122888 | tf_op jit(solution)/shard_map/ppermute | solution.py:24
  14.3 13.8 %collective-permute-start.4 = (f32[2,40,128]{2,1,0:T(8,128)}, f32[2,40,128]{2,1,0:T(8,128)S(1)}, u32[]{:S(2)}, u32[]{:S(2)}) collective-permute-start(f32[2,40,128]{2,1,0:T(8,128)} %own_ref.1), channel_id=1, source_target_pairs={{64,0},{128,64},{192,128},{0,192},{65,1},{129,65},{193,129},{1,193... | collective-permute-start | bytes 122888 | tf_op jit(solution)/shard_map/ppermute | solution.py:24
  15.8 12.3 %collective-permute-start.5 = (f32[2,40,128]{2,1,0:T(8,128)}, f32[2,40,128]{2,1,0:T(8,128)S(1)}, u32[]{:S(2)}, u32[]{:S(2)}) collective-permute-start(f32[2,40,128]{2,1,0:T(8,128)} %own_ref.1), channel_id=1, source_target_pairs={{128,0},{192,64},{0,128},{64,192},{129,1},{193,65},{1,129},{65,193... | collective-permute-start | bytes 122888 | tf_op jit(solution)/shard_map/ppermute | solution.py:24
  16.2 11.9 %collective-permute-start.6 = (f32[2,40,128]{2,1,0:T(8,128)}, f32[2,40,128]{2,1,0:T(8,128)S(1)}, u32[]{:S(2)}, u32[]{:S(2)}) collective-permute-start(f32[2,40,128]{2,1,0:T(8,128)} %own_ref.1), channel_id=1, source_target_pairs={{192,0},{0,64},{64,128},{128,192},{193,1},{1,65},{65,129},{129,193... | collective-permute-start | bytes 122888 | tf_op jit(solution)/shard_map/ppermute | solution.py:24
  22.5 3.9 %copy-start.3 = (f32[2,40,128]{2,1,0:T(8,128)S(1)}, f32[2,40,128]{2,1,0:T(8,128)}, u32[]{:S(2)}) copy-start(f32[2,40,128]{2,1,0:T(8,128)} %own_ref.1) | copy-start | bytes 122884
  22.5 5.6 %copy-start.4 = (s32[768]{0:T(1024)S(1)}, s32[768]{0:T(1024)}, u32[]{:S(2)}) copy-start(s32[768]{0:T(1024)} %param.14) | copy-start | bytes 9220
  22.5 5.6 %copy-start.5 = (s32[768]{0:T(1024)S(1)}, s32[768]{0:T(1024)}, u32[]{:S(2)}) copy-start(s32[768]{0:T(1024)} %param.15) | copy-start | bytes 9220
  22.5 5.6 %copy-start.6 = (s32[768]{0:T(1024)S(1)}, s32[768]{0:T(1024)}, u32[]{:S(2)}) copy-start(s32[768]{0:T(1024)} %param.16) | copy-start | bytes 9220
  22.5 5.6 %copy-start.7 = (s32[768]{0:T(1024)S(1)}, s32[768]{0:T(1024)}, u32[]{:S(2)}) copy-start(s32[768]{0:T(1024)} %param.17) | copy-start | bytes 9220
  22.5 5.6 %copy-start.8 = (f32[8,128]{1,0:T(8,128)S(1)}, f32[8,128]{1,0:T(8,128)}, u32[]{:S(2)}) copy-start(f32[8,128]{1,0:T(8,128)} %mass_ref.3) | copy-start | bytes 12292
  26.5 1.4 %copy-start = (f32[2,40,40,128]{3,2,1,0:T(8,128)S(1)}, f32[2,40,40,128]{3,2,1,0:T(8,128)}, u32[]{:S(2)}) copy-start(f32[2,40,40,128]{3,2,1,0:T(8,128)} %blocks_ref.3) | copy-start | bytes 4915204
  27.9 14.7 %copy-start.1 = (f32[2,40,40,128]{3,2,1,0:T(8,128)S(1)}, f32[2,40,40,128]{3,2,1,0:T(8,128)}, u32[]{:S(2)}) copy-start(f32[2,40,40,128]{3,2,1,0:T(8,128)} %blocks_ref.3) | copy-start | bytes 4915204
  29.7 5.7 %collective-permute-start.10 = (f32[2,40,128]{2,1,0:T(8,128)}, f32[2,40,128]{2,1,0:T(8,128)S(1)}, u32[]{:S(2)}, u32[]{:S(2)}) collective-permute-start(f32[2,40,128]{2,1,0:T(8,128)} %shard_map.105.vector_ref.own_ref), channel_id=1, source_target_pairs={{2,0},{3,1},{4,2},{5,3},{6,4},{7,5},{8,6},{9,7},{10,8},{11,9},{12,... | collective-permute-start | bytes 122888 | tf_op jit(solution)/shard_map/ppermute | solution.py:24
  32.9 3.7 %collective-permute-start.11 = (f32[2,40,128]{2,1,0:T(8,128)}, f32[2,40,128]{2,1,0:T(8,128)S(1)}, u32[]{:S(2)}, u32[]{:S(2)}) collective-permute-start(f32[2,40,128]{2,1,0:T(8,128)} %shard_map.105.vector_ref.own_ref), channel_id=1, source_target_pairs={{64,0},{128,64},{192,128},{0,192},{65,1},{129,65},{193,129},{1,193... | collective-permute-start | bytes 122888 | tf_op jit(solution)/shard_map/ppermute | solution.py:24
  33.1 10.5 %collective-permute-start.12 = (f32[2,40,128]{2,1,0:T(8,128)}, f32[2,40,128]{2,1,0:T(8,128)S(1)}, u32[]{:S(2)}, u32[]{:S(2)}) collective-permute-start(f32[2,40,128]{2,1,0:T(8,128)} %shard_map.105.vector_ref.own_ref), channel_id=1, source_target_pairs={{128,0},{192,64},{0,128},{64,192},{129,1},{193,65},{1,129},{65,193... | collective-permute-start | bytes 122888 | tf_op jit(solution)/shard_map/ppermute | solution.py:24
  33.3 10.3 %collective-permute-start.13 = (f32[2,40,128]{2,1,0:T(8,128)}, f32[2,40,128]{2,1,0:T(8,128)S(1)}, u32[]{:S(2)}, u32[]{:S(2)}) collective-permute-start(f32[2,40,128]{2,1,0:T(8,128)} %shard_map.105.vector_ref.own_ref), channel_id=1, source_target_pairs={{192,0},{0,64},{64,128},{128,192},{193,1},{1,65},{65,129},{129,193... | collective-permute-start | bytes 122888 | tf_op jit(solution)/shard_map/ppermute | solution.py:24
  35.3 10.2 %collective-permute-start.7 = (f32[2,40,128]{2,1,0:T(8,128)}, f32[2,40,128]{2,1,0:T(8,128)S(1)}, u32[]{:S(2)}, u32[]{:S(2)}) collective-permute-start(f32[2,40,128]{2,1,0:T(8,128)} %shard_map.105.vector_ref.own_ref), channel_id=1, source_target_pairs={{62,0},{63,1},{0,2},{1,3},{2,4},{3,5},{4,6},{5,7},{6,8},{7,9},{8,1... | collective-permute-start | bytes 122888 | tf_op jit(solution)/shard_map/ppermute | solution.py:24
  35.3 11.1 %collective-permute-start.8 = (f32[2,40,128]{2,1,0:T(8,128)}, f32[2,40,128]{2,1,0:T(8,128)S(1)}, u32[]{:S(2)}, u32[]{:S(2)}) collective-permute-start(f32[2,40,128]{2,1,0:T(8,128)} %shard_map.105.vector_ref.own_ref), channel_id=1, source_target_pairs={{63,0},{0,1},{1,2},{2,3},{3,4},{4,5},{5,6},{6,7},{7,8},{8,9},{9,10... | collective-permute-start | bytes 122888 | tf_op jit(solution)/shard_map/ppermute | solution.py:24
  36.6 9.9 %collective-permute-start.9 = (f32[2,40,128]{2,1,0:T(8,128)}, f32[2,40,128]{2,1,0:T(8,128)S(1)}, u32[]{:S(2)}, u32[]{:S(2)}) collective-permute-start(f32[2,40,128]{2,1,0:T(8,128)} %shard_map.105.vector_ref.own_ref), channel_id=1, source_target_pairs={{1,0},{2,1},{3,2},{4,3},{5,4},{6,5},{7,6},{8,7},{9,8},{10,9},{11,1... | collective-permute-start | bytes 122888 | tf_op jit(solution)/shard_map/ppermute | solution.py:24
  42.6 0.8 %copy-start.2 = (f32[2,40,128]{2,1,0:T(8,128)S(1)}, f32[2,40,128]{2,1,0:T(8,128)}, u32[]{:S(2)}) copy-start(f32[2,40,128]{2,1,0:T(8,128)} %shard_map.105.vector_ref.own_ref) | copy-start | bytes 122884

commit v2 on v1

--- a/solution.py
+++ b/solution.py
@@ -9,7 +9,6 @@
 from jax.sharding import PartitionSpec as P
 
 OMEGA = 1.0
-OFFSETS = (-2, -1, 1, 2)
 
 
 def spectral(spacing, total):
@@ -19,9 +18,55 @@
     return 0.5 * OMEGA * (-1.0) ** wrapped / math.tan(math.pi * wrapped / total)
 
 
-def pull(value, axis, offset):
-    length = lax.axis_size(axis)
-    return lax.ppermute(value, axis, [((i + offset) % length, i) for i in range(length)])
+def joint(rule):
+    insts, parts = lax.axis_size("inst"), lax.axis_size("dom")
+    pairs = []
+    for inst in range(insts):
+        for part in range(parts):
+            to_inst, to_part = rule(inst, part)
+            pairs.append((inst * parts + part, to_inst * parts + to_part % parts))
+    return pairs
+
+
+def send(value, rule):
+    return lax.ppermute(value, ("inst", "dom"), joint(rule))
+
+
+def to_core(inst, part):
+    return inst ^ 1, part
+
+
+def to_chip(inst, part):
+    return inst ^ 2, part
+
+
+def near_step(part, reach):
+    return -reach if part & reach else reach
+
+
+def to_near(inst, part):
+    return inst, part + near_step(part, 1 + inst % 2)
+
+
+def to_far(inst, part):
+    return inst, part - near_step(part, 1 + inst % 2)
+
+
+def pack_kernel(own_ref, other_ref, out_ref):
+    insts = own_ref.shape[0]
+    out_ref[:insts] = own_ref[...]
+    out_ref[insts:] = other_ref[...]
+
+
+def pack(own, other):
+    return pl.pallas_call(
+        pack_kernel,
+        out_shape=jax.ShapeDtypeStruct((2 * own.shape[0],) + own.shape[1:], jnp.float32),
+        in_specs=[pl.BlockSpec(memory_space=pltpu.VMEM)] * 2,
+        out_specs=pl.BlockSpec(memory_space=pltpu.VMEM),
+        cost_estimate=pl.CostEstimate(flops=0, bytes_accessed=16 * own.size, transcendentals=0),
+        compiler_params=pltpu.CompilerParams(vmem_limit_bytes=2**20),
+    )(own, other)
 
 
 def sublanes():
@@ -43,31 +88,49 @@
     return tiles[0]
 
 
-def element_kernel(vector_ref, blocks_ref, out_ref):
-    insts, unknowns, _ = vector_ref.shape
-    for t in range(insts):
-        tiles = [vector_ref[t, 8 * g : 8 * g + 8, :] for g in range(unknowns // 8)]
-        for group in range(unknowns // 8):
-            partial = []
-            for i in range(8 * group, 8 * group + 8):
-                total = blocks_ref[t, i, 0:8, :] * tiles[0]
-                for g in range(1, unknowns // 8):
-                    total += blocks_ref[t, i, 8 * g : 8 * g + 8, :] * tiles[g]
-                partial.append(total)
-            out_ref[t, 8 * group : 8 * group + 8, :] = fold_rows(partial)
-
-
-def element_term(vector, blocks):
+def element_term(vector_ref, blocks_ref, t):
+    unknowns = vector_ref.shape[1]
+    tiles = [vector_ref[t, 8 * g : 8 * g + 8, :] for g in range(unknowns // 8)]
+    groups = []
+    for group in range(unknowns // 8):
+        partial = []
+        for i in range(8 * group, 8 * group + 8):
+            total = blocks_ref[t, i, 0:8, :] * tiles[0]
+            for g in range(1, unknowns // 8):
+                total += blocks_ref[t, i, 8 * g : 8 * g + 8, :] * tiles[g]
+            partial.append(total)
+        groups.append(fold_rows(partial))
+    return groups
+
+
+def regroup_kernel(blocks_ref, out_ref):
+    rows, columns, insts, faces = blocks_ref.shape
+    lane_tiles = faces // 128
+    stride = lane_tiles * insts
+
+    def one_row(i, carry):
+        base = pl.multiple_of(i * columns * stride, 8)
+        for p in range(columns):
+            for tile in range(lane_tiles):
+                out_ref[pl.ds(base + p * stride + tile * insts, insts), :] = blocks_ref[
+                    i, p, :, tile * 128 : tile * 128 + 128
+                ]
+        return carry
+
+    lax.fori_loop(0, rows, one_row, 0)
+
+
+def regroup(blocks):
     return pl.pallas_call(
-        element_kernel,
-        out_shape=jax.ShapeDtypeStruct(vector.shape, jnp.float32),
-        in_specs=[pl.BlockSpec(memory_space=pltpu.VMEM)] * 2,
+        regroup_kernel,
+        out_shape=jax.ShapeDtypeStruct((blocks.size // 128, 128), jnp.float32),
+        in_specs=[pl.BlockSpec(memory_space=pltpu.VMEM)],
         out_specs=pl.BlockSpec(memory_space=pltpu.VMEM),
         cost_estimate=pl.CostEstimate(
-            flops=2 * blocks.size, bytes_accessed=4 * blocks.size, transcendentals=0
+            flops=0, bytes_accessed=8 * blocks.size, transcendentals=0
         ),
-        compiler_params=pltpu.CompilerParams(vmem_limit_bytes=32 * 2**20),
-    )(vector, blocks)
+        compiler_params=pltpu.CompilerParams(vmem_limit_bytes=16 * 2**20),
+    )(blocks)
 
 
 def corner_of(side, within):
@@ -94,24 +157,42 @@
     return place, held
 
 
-def face_kernel(
+def jacobian_kernel(
     instances,
     part_total,
     counts_ref,
-    my_ref,
+    place_ref,
     owner_ref,
     side_ref,
     part_ref,
     nbr_ref,
     mass_ref,
-    element_ref,
+    element_blocks_ref,
     blocks_ref,
     own_ref,
-    *rest,
+    core_ref,
+    chip_ref,
+    far_ref,
+    near_ref,
+    other_far_ref,
+    other_near_ref,
+    out_ref,
+    trace_ref,
+    across_ref,
+    spread_ref,
 ):
-    neighbour_refs = rest[: len(OFFSETS)]
-    instance_refs = rest[len(OFFSETS) : len(OFFSETS) + instances - 1]
-    out_ref, trace_ref, across_ref, spread_ref = rest[len(OFFSETS) + instances - 1 :]
+    my_part = place_ref[0]
+    on_first = place_ref[1] == 0
+    step_one = jnp.where((my_part & 1) == 0, 1, -1)
+    step_two = jnp.where((my_part & 2) == 0, 2, -2)
+    mine = jnp.where(on_first, step_one, step_two)
+    others = jnp.where(on_first, step_two, step_one)
+    neighbours = (
+        (-mine, far_ref, 0),
+        (mine, near_ref, 0),
+        (-others, other_far_ref, 1),
+        (others, other_near_ref, 1),
+    )
     insts, unknowns, elements = own_ref.shape
     variables = unknowns // 8
     width = 4 * variables
@@ -125,10 +206,10 @@
 
     for tile in range(lane_tiles):
         column = wide(nbr_ref, tile)
-        offset = wide(part_ref, tile) - my_ref[0]
+        offset = wide(part_ref, tile) - my_part
         offset = jnp.where(offset > 2, offset - part_total, offset)
         offset = jnp.where(offset < -2, offset + part_total, offset)
-        chosen = [offset == o for o in OFFSETS]
+        chosen = [offset == o for o, _, _ in neighbours]
         corner = corner_of(wide(side_ref, tile) ^ 1, row & 3)
         for t in range(insts):
             traces = []
@@ -137,14 +218,14 @@
                 picked = jnp.take_along_axis(
                     own_ref[t, rows, :], column, axis=1, mode="promise_in_bounds"
                 )
-                for mask, ref in zip(chosen, neighbour_refs):
-                    picked = jnp.where(
-                        mask,
-                        jnp.take_along_axis(
-                            ref[t, rows, :], column, axis=1, mode="promise_in_bounds"
-                        ),
-                        picked,
+                for mask, (_, ref, half) in zip(chosen, neighbours):
+                    there = jnp.take_along_axis(
+                        ref[half * insts + t, rows, :],
+                        column,
+                        axis=1,
+                        mode="promise_in_bounds",
                     )
+                    picked = jnp.where(mask, there, picked)
                 traces.append(
                     jnp.take_along_axis(picked, corner, axis=0, mode="promise_in_bounds")
                 )
@@ -203,24 +284,33 @@
     live = lax.broadcasted_iota(jnp.int32, shape, 1) < counts_ref[0]
     mass = mass_ref[...]
     total_insts = insts * instances
-    sources = (own_ref, *instance_refs)
+    sources = (
+        (own_ref, 0, 0, 0),
+        (core_ref, 0, -1, 1),
+        (chip_ref, 0, 2, 2),
+        (chip_ref, insts, 1, -1),
+    )
     for t in range(insts):
+        element = element_term(own_ref, element_blocks_ref, t)
         for a in range(variables):
             rows = slice(8 * a, 8 * a + 8)
             summed = None
-            for k, ref in enumerate(sources):
+            for ref, base, ahead_first, ahead_second in sources:
                 for s in range(insts):
-                    weight = spectral(t - s - insts * k, total_insts)
-                    if weight != 0.0:
-                        term = weight * ref[s, rows, :]
-                        summed = term if summed is None else summed + term
+                    even = spectral(t - s + insts * ahead_first, total_insts)
+                    odd = spectral(t - s + insts * ahead_second, total_insts)
+                    if even == 0.0 and odd == 0.0:
+                        continue
+                    weight = even if even == odd else jnp.where(on_first, even, odd)
+                    term = weight * ref[base + s, rows, :]
+                    summed = term if summed is None else summed + term
             base = (t * variables + a) * 8
-            value = element_ref[t, rows, :] + landed[base : base + 8, :] + mass * summed
+            value = element[a] + landed[base : base + 8, :] + mass * summed
             out_ref[t, rows, :] = jnp.where(live, value, 0.0)
 
 
-def face_and_time_term(
-    counts, my_part, owner, side, part, nbr, mass, element, blocks, own, neighbours, others
+def jacobian_rows(
+    keep, counts, place, owner, side, part, nbr, mass, element_blocks, blocks, own, *fields
 ):
     part_total = lax.axis_size("dom")
     instances = lax.axis_size("inst")
@@ -230,9 +320,9 @@
     vmem = pl.BlockSpec(memory_space=pltpu.VMEM)
     smem = pl.BlockSpec(memory_space=pltpu.SMEM)
     return pl.pallas_call(
-        functools.partial(face_kernel, instances, part_total),
-        out_shape=jax.ShapeDtypeStruct(own.shape, jnp.float32),
-        in_specs=[smem, smem] + [vmem] * (8 + len(neighbours) + len(others)),
+        functools.partial(jacobian_kernel, instances, part_total),
+        out_shape=(pltpu.VMEM if keep else jax.ShapeDtypeStruct)(own.shape, jnp.float32),
+        in_specs=[smem, smem] + [vmem] * (8 + len(fields)),
         out_specs=vmem,
         scratch_shapes=[
             pltpu.VMEM((width * stride, 128), jnp.float32),
@@ -240,10 +330,10 @@
             pltpu.VMEM((insts * unknowns, owner.shape[0] * 128), jnp.float32),
         ],
         cost_estimate=pl.CostEstimate(
-            flops=2 * blocks.size, bytes_accessed=4 * blocks.size, transcendentals=0
+            flops=4 * blocks.size, bytes_accessed=4 * blocks.size, transcendentals=0
         ),
-        compiler_params=pltpu.CompilerParams(vmem_limit_bytes=32 * 2**20),
-    )(counts, my_part, owner, side, part, nbr, mass, element, blocks, own, *neighbours, *others)
+        compiler_params=pltpu.CompilerParams(vmem_limit_bytes=16 * 2**20),
+    )(counts, place, owner, side, part, nbr, mass, element_blocks, blocks, own, *fields)
 
 
 def on_device(
@@ -257,26 +347,30 @@
     face_part,
     face_nbr,
 ):
-    insts, rows, columns, faces = face_blocks.shape
-    tiles = faces // 128
-    blocks = face_blocks.reshape(insts, rows, columns, tiles, 128)
-    blocks = jnp.transpose(blocks, (1, 2, 3, 0, 4)).reshape(-1, 128)
+    tiles = face_blocks.shape[-1] // 128
+    blocks = regroup(jnp.transpose(face_blocks, (1, 2, 0, 3)))
     owner, side, part, nbr = (
         x.reshape(tiles, 128) for x in (face_owner, face_side, face_part, face_nbr)
     )
-    my_part = lax.axis_index("dom").astype(jnp.int32).reshape(1)
-
-    def apply_jacobian(vector):
-        neighbours = [pull(vector, "dom", o) for o in OFFSETS]
-        others = [pull(vector, "inst", k) for k in range(1, lax.axis_size("inst"))]
-        element = element_term(vector, element_jacobian_blocks)
-        return face_and_time_term(
-            counts, my_part, owner, side, part, nbr, mass, element, blocks, vector,
-            neighbours, others,
+    place = jnp.stack(
+        [lax.axis_index("dom"), lax.axis_index("inst") % 2]
+    ).astype(jnp.int32)
+
+    def apply_jacobian(vector, keep):
+        other = send(vector, to_core)
+        both = pack(vector, other)
+        far = send(both, to_far)
+        near = send(both, to_near)
+        chip = send(both, to_chip)
+        other_near = send(near, to_core)
+        other_far = send(far, to_core)
+        return jacobian_rows(
+            keep, counts, place, owner, side, part, nbr, mass, element_jacobian_blocks, blocks, vector,
+            other, chip, far, near, other_far, other_near,
         )
 
-    first = apply_jacobian(state)
-    second = apply_jacobian(first)
+    first = apply_jacobian(state, True)
+    second = apply_jacobian(first, False)
     return first, second
 
 

time: 48.2 us -> 42.2 us (0.88)
  starting transfers between devices: 29 us -> 22.9 us
  local copies, waits for them, and re-layouts: 10.4 us -> 4.54 us
  waiting for transfers between devices: 3.79 us -> 9.16 us
  Pallas kernels: 3.28 us -> 3.84 us
    ppermute x14 -> x12, starting transfers between devices: 29 us -> 22.9 us  [send(): return lax.ppermute(value, ('inst', 'dom'), joint(rule))]
    ppermute x14 -> x12, waiting for transfers between devices: 3.79 us -> 9.16 us  [send(): return lax.ppermute(value, ('inst', 'dom'), joint(rule))]
    reshape x1 -> x0, local copies, waits for them, and re-layouts: 4.91 us -> none  [on_device(): blocks = face_blocks.reshape(insts, rows, columns, tiles, 128)]
    transpose x1 -> x0, local copies, waits for them, and re-layouts: 3.25 us -> none  [on_device(): blocks = jnp.transpose(blocks, (1, 2, 3, 0, 4)).reshape(-1, 128)]
    unnamed x18 -> x21, local copies, waits for them, and re-layouts: 2.27 us -> 4.54 us
    pallas_call x4 -> x5, Pallas kernels: 3.28 us -> 3.84 us  [the longest x2 3.62 us: jacobian_rows(): pl.pallas_call(functools.partial(jacobian_kernel, instances, part_total),...]
  transfers between devices with their start and end apart: 14 -> 12, of which waited for: 3 -> 7; matrix products, arithmetic and copies ran while one was open for 17% -> 2% of each run, Pallas kernels for 1% -> 0%
where the time goes in v2:
time: 42.2 us; the launch traced here: 41.9 us
  starting transfers between devices  22.9 us (54%)
  waiting for transfers between devices  9.16 us (22%)
  local copies, waits for them, and re-layouts  4.54 us (11%)
  Pallas kernels  3.84 us (9%)
  between operations  1.4 us (3%)
    ppermute x12, starting transfers between devices, send(): return lax.ppermute(value, ('inst', 'dom'), joint(rule))  22.9 us
    ppermute x12, waiting for transfers between devices, send(): return lax.ppermute(value, ('inst', 'dom'), joint(rule))  9.16 us
    unnamed x21, local copies, waits for them, and re-layouts  4.54 us
    pallas_call x2, Pallas kernels, jacobian_rows(): pl.pallas_call(functools.partial(jacobian_kernel, instances, part_total),...  3.62 us
  transfers between devices with their start and end apart: 12, of which 7 were waited for; matrix products, arithmetic and copies ran while one was open for 2% of the time, Pallas kernels for 0%

profile of v2, /device:TPU:1, one launch (start us, length us, event | category | flops | bytes accessed | tf_op | source)
XLA Modules:
  0.0 41.9 jit_solution(6279159986865569969)
XLA Ops:
  0.6 3.3 %collective-permute-start = (f32[2,40,128]{2,1,0:T(8,128)}, f32[2,40,128]{2,1,0:T(8,128)S(1)}, u32[]{:S(2)}, u32[]{:S(2)}) collective-permute-start(f32[2,40,128]{2,1,0:T(8,128)} %own_ref.3), channel_id=1, source_target_pairs={{0,64},{1,65},{2,66},{3,67},{4,68},{5,69},{6,70},{7,71},{8,72},{9,... | collective-permute-start | bytes 122888 | tf_op jit(solution)/shard_map/ppermute | solution.py:32
  4.0 1.1 %collective-permute-done.other_ref.core_ref = f32[2,40,128]{2,1,0:T(8,128)S(1)} collective-permute-done((f32[2,40,128]{2,1,0:T(8,128)}, f32[2,40,128]{2,1,0:T(8,128)S(1)}, u32[]{:S(2)}, u32[]{:S(2)}) %collective-permute-start) | collective-permute-done | bytes 40992 | tf_op jit(solution)/shard_map/ppermute | solution.py:32
  5.0 0.8 %copy-done.3 = f32[2,40,128]{2,1,0:T(8,128)S(1)} copy-done((f32[2,40,128]{2,1,0:T(8,128)S(1)}, f32[2,40,128]{2,1,0:T(8,128)}, u32[]{:S(2)}) %copy-start.3) | copy-done | bytes 40984
  5.8 9.1 %collective-permute-start.2 = (f32[4,40,128]{2,1,0:T(8,128)S(1)}, f32[4,40,128]{2,1,0:T(8,128)S(1)}, u32[]{:S(2)}, u32[]{:S(2)}) collective-permute-start(f32[4,40,128]{2,1,0:T(8,128)S(1)} %shard_map.105), channel_id=1, source_target_pairs={{0,63},{1,2},{2,1},{3,4},{4,3},{5,6},{6,5},{7,8},{8,7},{9,10},{10,... | collective-permute-start | bytes 245768 | tf_op jit(solution)/shard_map/ppermute | solution.py:32
  15.6 0.0 copy-start.2
  15.6 1.7 %copy-done.2 = f32[2,20,20,768]{3,0,2,1:T(2,128)S(1)} copy-done((f32[2,20,20,768]{3,0,2,1:T(2,128)S(1)}, f32[2,20,20,768]{3,0,2,1:T(2,128)}, u32[]{:S(2)}) %copy-start.2) | copy-done | bytes 2457624
  17.3 0.0 copy-start.8
  17.3 0.0 copy-start.9
  17.3 0.2 shard_map.104.blocks_ref
  17.5 0.5 %collective-permute-start.1 = (f32[4,40,128]{2,1,0:T(8,128)S(1)}, f32[4,40,128]{2,1,0:T(8,128)S(1)}, u32[]{:S(2)}, u32[]{:S(2)}) collective-permute-start(f32[4,40,128]{2,1,0:T(8,128)S(1)} %shard_map.105), channel_id=1, source_target_pairs={{0,128},{1,129},{2,130},{3,131},{4,132},{5,133},{6,134},{7,135},{8... | collective-permute-start | bytes 245768 | tf_op jit(solution)/shard_map/ppermute | solution.py:32
  18.0 0.0 collective-permute-done.2.far_ref
  18.0 0.7 %collective-permute-start.4 = (f32[4,40,128]{2,1,0:T(8,128)S(1)}, f32[4,40,128]{2,1,0:T(8,128)S(1)}, u32[]{:S(2)}, u32[]{:S(2)}) collective-permute-start(f32[4,40,128]{2,1,0:T(8,128)S(1)} %collective-permute-done.2.far_ref), channel_id=1, source_target_pairs={{0,64},{1,65},{2,66},{3,67},{4,68},{5,69},{6,70},{7,71},{8,72},{9,... | collective-permute-start | bytes 245768 | tf_op jit(solution)/shard_map/ppermute | solution.py:32
  18.8 1.2 %collective-permute-done.3.near_ref = f32[4,40,128]{2,1,0:T(8,128)S(1)} collective-permute-done((f32[4,40,128]{2,1,0:T(8,128)S(1)}, f32[4,40,128]{2,1,0:T(8,128)S(1)}, u32[]{:S(2)}, u32[]{:S(2)}) %collective-permute-start.3) | collective-permute-done | bytes 81952 | tf_op jit(solution)/shard_map/ppermute | solution.py:32
  20.0 0.1 collective-permute-start.5
  20.1 0.1 pad_add_fusion.place_ref
  20.2 1.3 %collective-permute-done.1.chip_ref = f32[4,40,128]{2,1,0:T(8,128)S(1)} collective-permute-done((f32[4,40,128]{2,1,0:T(8,128)S(1)}, f32[4,40,128]{2,1,0:T(8,128)S(1)}, u32[]{:S(2)}, u32[]{:S(2)}) %collective-permute-start.1) | collective-permute-done | bytes 81952 | tf_op jit(solution)/shard_map/ppermute | solution.py:32
  21.5 0.0 collective-permute-done.4.other_far_ref
  21.5 0.0 collective-permute-done.5.other_near_ref
  21.6 0.0 copy-start
  21.6 1.4 %copy-done = f32[2,40,40,128]{3,2,1,0:T(8,128)S(1)} copy-done((f32[2,40,40,128]{3,2,1,0:T(8,128)S(1)}, f32[2,40,40,128]{3,2,1,0:T(8,128)}, u32[]{:S(2)}) %copy-start) | copy-done | bytes 1638424
  23.0 1.5 %shard_map.106.own_ref = f32[2,40,128]{2,1,0:T(8,128)S(1)} custom-call(s32[1]{0:T(128)S(6)} %copy.12.counts_ref, s32[2]{0:T(128)S(1)} %pad_add_fusion.place_ref, s32[6,128]{1,0:T(8,128)S(1)} %bitcast.8, s32[6,128]{1,0:T(8,128)S(1)} %bitcast.10, s32[6,128]{1,0:T(8,128)S(1)} %bitcast.12, s32[6,128]{1,0:T(8,128)S(1)} %bitcast.14, f32[8,128]{1,0:T(8,128)S(1)} %copy-done.9, ...), custom_call_target="tpu_custom_call" | custom-call | flops 2457600 | bytes 2457600 | tf_op jit(solution)/shard_map/pallas_call | solution.py:322
  24.5 1.1 %collective-permute-start.6 = (f32[2,40,128]{2,1,0:T(8,128)S(1)}, f32[2,40,128]{2,1,0:T(8,128)S(1)}, u32[]{:S(2)}, u32[]{:S(2)}) collective-permute-start(f32[2,40,128]{2,1,0:T(8,128)S(1)} %shard_map.106.own_ref), channel_id=1, source_target_pairs={{0,64},{1,65},{2,66},{3,67},{4,68},{5,69},{6,70},{7,71},{8,72},{9,... | collective-permute-start | bytes 122888 | tf_op jit(solution)/shard_map/ppermute | solution.py:32
  25.6 0.9 %collective-permute-done.6.other_ref.core_ref = f32[2,40,128]{2,1,0:T(8,128)S(1)} collective-permute-done((f32[2,40,128]{2,1,0:T(8,128)S(1)}, f32[2,40,128]{2,1,0:T(8,128)S(1)}, u32[]{:S(2)}, u32[]{:S(2)}) %collective-permute-start.6) | collective-permute-done | bytes 40992 | tf_op jit(solution)/shard_map/ppermute | solution.py:32
  26.5 5.6 %collective-permute-start.8 = (f32[4,40,128]{2,1,0:T(8,128)S(1)}, f32[4,40,128]{2,1,0:T(8,128)S(1)}, u32[]{:S(2)}, u32[]{:S(2)}) collective-permute-start(f32[4,40,128]{2,1,0:T(8,128)S(1)} %shard_map.107), channel_id=1, source_target_pairs={{0,63},{1,2},{2,1},{3,4},{4,3},{5,6},{6,5},{7,8},{8,7},{9,10},{10,... | collective-permute-start | bytes 245768 | tf_op jit(solution)/shard_map/ppermute | solution.py:32
  32.1 0.4 collective-permute-start.7
  32.5 4.0 %collective-permute-done.8.far_ref = f32[4,40,128]{2,1,0:T(8,128)S(1)} collective-permute-done((f32[4,40,128]{2,1,0:T(8,128)S(1)}, f32[4,40,128]{2,1,0:T(8,128)S(1)}, u32[]{:S(2)}, u32[]{:S(2)}) %collective-permute-start.8) | collective-permute-done | bytes 81952 | tf_op jit(solution)/shard_map/ppermute | solution.py:32
  36.5 2.1 %collective-permute-start.10 = (f32[4,40,128]{2,1,0:T(8,128)S(1)}, f32[4,40,128]{2,1,0:T(8,128)S(1)}, u32[]{:S(2)}, u32[]{:S(2)}) collective-permute-start(f32[4,40,128]{2,1,0:T(8,128)S(1)} %collective-permute-done.8.far_ref), channel_id=1, source_target_pairs={{0,64},{1,65},{2,66},{3,67},{4,68},{5,69},{6,70},{7,71},{8,72},{9,... | collective-permute-start | bytes 245768 | tf_op jit(solution)/shard_map/ppermute | solution.py:32
  38.5 0.0 collective-permute-start.11
  38.5 0.6 %copy.11 = f32[2,40,128]{2,1,0:T(8,128)} copy(f32[2,40,128]{2,1,0:T(8,128)S(1)} %shard_map.106.own_ref) | data formatting | bytes 81920
  39.2 0.3 collective-permute-done.10.other_far_ref
  39.5 0.4 collective-permute-done.11.other_near_ref
  39.8 2.1 %shard_map.108 = f32[2,40,128]{2,1,0:T(8,128)} custom-call(s32[1]{0:T(128)S(6)} %copy.12.counts_ref, s32[2]{0:T(128)S(1)} %pad_add_fusion.place_ref, s32[6,128]{1,0:T(8,128)S(1)} %bitcast.9, s32[6,128]{1,0:T(8,128)S(1)} %bitcast.11, s32[6,128]{1,0:T(8,128)S(1)} %bitcast.13, s32[6,128]{1,0:T(8,128)S(1)} %bitcast.15, f32[8,128]{1,0:T(8,128)S(1)} %copy-done.9, ...), custom_call_target="tpu_custom_call" | custom-call | flops 2457600 | bytes 2457600 | tf_op jit(solution)/shard_map/pallas_call | solution.py:322
  (19 shorter events, 0.0 us)
Async XLA Ops:
  0.6 4.4 %collective-permute-start = (f32[2,40,128]{2,1,0:T(8,128)}, f32[2,40,128]{2,1,0:T(8,128)S(1)}, u32[]{:S(2)}, u32[]{:S(2)}) collective-permute-start(f32[2,40,128]{2,1,0:T(8,128)} %own_ref.3), channel_id=1, source_target_pairs={{0,64},{1,65},{2,66},{3,67},{4,68},{5,69},{6,70},{7,71},{8,72},{9,... | collective-permute-start | bytes 122888 | tf_op jit(solution)/shard_map/ppermute | solution.py:32
  5.0 0.8 %copy-start.3 = (f32[2,40,128]{2,1,0:T(8,128)S(1)}, f32[2,40,128]{2,1,0:T(8,128)}, u32[]{:S(2)}) copy-start(f32[2,40,128]{2,1,0:T(8,128)} %own_ref.3) | copy-start | bytes 122884
  5.8 12.2 %collective-permute-start.2 = (f32[4,40,128]{2,1,0:T(8,128)S(1)}, f32[4,40,128]{2,1,0:T(8,128)S(1)}, u32[]{:S(2)}, u32[]{:S(2)}) collective-permute-start(f32[4,40,128]{2,1,0:T(8,128)S(1)} %shard_map.105), channel_id=1, source_target_pairs={{0,63},{1,2},{2,1},{3,4},{4,3},{5,6},{6,5},{7,8},{8,7},{9,10},{10,... | collective-permute-start | bytes 245768 | tf_op jit(solution)/shard_map/ppermute | solution.py:32
  14.9 5.1 %collective-permute-start.3 = (f32[4,40,128]{2,1,0:T(8,128)S(1)}, f32[4,40,128]{2,1,0:T(8,128)S(1)}, u32[]{:S(2)}, u32[]{:S(2)}) collective-permute-start(f32[4,40,128]{2,1,0:T(8,128)S(1)} %shard_map.105), channel_id=1, source_target_pairs={{0,1},{1,0},{2,3},{3,2},{4,5},{5,4},{6,7},{7,6},{8,9},{9,8},{10,11... | collective-permute-start | bytes 245768 | tf_op jit(solution)/shard_map/ppermute | solution.py:32
  15.6 1.7 %copy-start.2 = (f32[2,20,20,768]{3,0,2,1:T(2,128)S(1)}, f32[2,20,20,768]{3,0,2,1:T(2,128)}, u32[]{:S(2)}) copy-start(f32[2,20,20,768]{3,0,2,1:T(2,128)} %param.11) | copy-start | bytes 7372804
  17.3 4.2 %copy-start.4 = (f32[2,40,128]{2,1,0:T(8,128)S(1)}, f32[2,40,128]{2,1,0:T(8,128)}, u32[]{:S(2)}) copy-start(f32[2,40,128]{2,1,0:T(8,128)} %own_ref.3) | copy-start | bytes 122884
  17.3 4.2 %copy-start.5 = (s32[768]{0:T(1024)S(1)}, s32[768]{0:T(1024)}, u32[]{:S(2)}) copy-start(s32[768]{0:T(1024)} %param.14) | copy-start | bytes 9220
  17.3 4.2 %copy-start.6 = (s32[768]{0:T(1024)S(1)}, s32[768]{0:T(1024)}, u32[]{:S(2)}) copy-start(s32[768]{0:T(1024)} %param.15) | copy-start | bytes 9220
  17.3 4.2 %copy-start.7 = (s32[768]{0:T(1024)S(1)}, s32[768]{0:T(1024)}, u32[]{:S(2)}) copy-start(s32[768]{0:T(1024)} %param.16) | copy-start | bytes 9220
  17.3 4.2 %copy-start.8 = (s32[768]{0:T(1024)S(1)}, s32[768]{0:T(1024)}, u32[]{:S(2)}) copy-start(s32[768]{0:T(1024)} %param.17) | copy-start | bytes 9220
  17.3 4.2 %copy-start.9 = (f32[8,128]{1,0:T(8,128)S(1)}, f32[8,128]{1,0:T(8,128)}, u32[]{:S(2)}) copy-start(f32[8,128]{1,0:T(8,128)} %mass_ref.3) | copy-start | bytes 12292
  17.5 4.0 %collective-permute-start.1 = (f32[4,40,128]{2,1,0:T(8,128)S(1)}, f32[4,40,128]{2,1,0:T(8,128)S(1)}, u32[]{:S(2)}, u32[]{:S(2)}) collective-permute-start(f32[4,40,128]{2,1,0:T(8,128)S(1)} %shard_map.105), channel_id=1, source_target_pairs={{0,128},{1,129},{2,130},{3,131},{4,132},{5,133},{6,134},{7,135},{8... | collective-permute-start | bytes 245768 | tf_op jit(solution)/shard_map/ppermute | solution.py:32
  18.0 3.5 %collective-permute-start.4 = (f32[4,40,128]{2,1,0:T(8,128)S(1)}, f32[4,40,128]{2,1,0:T(8,128)S(1)}, u32[]{:S(2)}, u32[]{:S(2)}) collective-permute-start(f32[4,40,128]{2,1,0:T(8,128)S(1)} %collective-permute-done.2.far_ref), channel_id=1, source_target_pairs={{0,64},{1,65},{2,66},{3,67},{4,68},{5,69},{6,70},{7,71},{8,72},{9,... | collective-permute-start | bytes 245768 | tf_op jit(solution)/shard_map/ppermute | solution.py:32
  20.0 1.5 %collective-permute-start.5 = (f32[4,40,128]{2,1,0:T(8,128)S(1)}, f32[4,40,128]{2,1,0:T(8,128)S(1)}, u32[]{:S(2)}, u32[]{:S(2)}) collective-permute-start(f32[4,40,128]{2,1,0:T(8,128)S(1)} %collective-permute-done.3.near_ref), channel_id=1, source_target_pairs={{0,64},{1,65},{2,66},{3,67},{4,68},{5,69},{6,70},{7,71},{8,72},{9,... | collective-permute-start | bytes 245768 | tf_op jit(solution)/shard_map/ppermute | solution.py:32
  21.6 1.4 %copy-start = (f32[2,40,40,128]{3,2,1,0:T(8,128)S(1)}, f32[2,40,40,128]{3,2,1,0:T(8,128)}, u32[]{:S(2)}) copy-start(f32[2,40,40,128]{3,2,1,0:T(8,128)} %element_blocks_ref.3) | copy-start | bytes 4915204
  23.0 16.8 %copy-start.1 = (f32[2,40,40,128]{3,2,1,0:T(8,128)S(1)}, f32[2,40,40,128]{3,2,1,0:T(8,128)}, u32[]{:S(2)}) copy-start(f32[2,40,40,128]{3,2,1,0:T(8,128)} %element_blocks_ref.3) | copy-start | bytes 4915204
  24.5 1.9 %collective-permute-start.6 = (f32[2,40,128]{2,1,0:T(8,128)S(1)}, f32[2,40,128]{2,1,0:T(8,128)S(1)}, u32[]{:S(2)}, u32[]{:S(2)}) collective-permute-start(f32[2,40,128]{2,1,0:T(8,128)S(1)} %shard_map.106.own_ref), channel_id=1, source_target_pairs={{0,64},{1,65},{2,66},{3,67},{4,68},{5,69},{6,70},{7,71},{8,72},{9,... | collective-permute-start | bytes 122888 | tf_op jit(solution)/shard_map/ppermute | solution.py:32
  26.5 10.0 %collective-permute-start.8 = (f32[4,40,128]{2,1,0:T(8,128)S(1)}, f32[4,40,128]{2,1,0:T(8,128)S(1)}, u32[]{:S(2)}, u32[]{:S(2)}) collective-permute-start(f32[4,40,128]{2,1,0:T(8,128)S(1)} %shard_map.107), channel_id=1, source_target_pairs={{0,63},{1,2},{2,1},{3,4},{4,3},{5,6},{6,5},{7,8},{8,7},{9,10},{10,... | collective-permute-start | bytes 245768 | tf_op jit(solution)/shard_map/ppermute | solution.py:32
  32.1 6.5 %collective-permute-start.9 = (f32[4,40,128]{2,1,0:T(8,128)S(1)}, f32[4,40,128]{2,1,0:T(8,128)S(1)}, u32[]{:S(2)}, u32[]{:S(2)}) collective-permute-start(f32[4,40,128]{2,1,0:T(8,128)S(1)} %shard_map.107), channel_id=1, source_target_pairs={{0,1},{1,0},{2,3},{3,2},{4,5},{5,4},{6,7},{7,6},{8,9},{9,8},{10,11... | collective-permute-start | bytes 245768 | tf_op jit(solution)/shard_map/ppermute | solution.py:32
  32.1 7.1 %collective-permute-start.7 = (f32[4,40,128]{2,1,0:T(8,128)S(1)}, f32[4,40,128]{2,1,0:T(8,128)S(1)}, u32[]{:S(2)}, u32[]{:S(2)}) collective-permute-start(f32[4,40,128]{2,1,0:T(8,128)S(1)} %shard_map.107), channel_id=1, source_target_pairs={{0,128},{1,129},{2,130},{3,131},{4,132},{5,133},{6,134},{7,135},{8... | collective-permute-start | bytes 245768 | tf_op jit(solution)/shard_map/ppermute | solution.py:32
  36.5 3.0 %collective-permute-start.10 = (f32[4,40,128]{2,1,0:T(8,128)S(1)}, f32[4,40,128]{2,1,0:T(8,128)S(1)}, u32[]{:S(2)}, u32[]{:S(2)}) collective-permute-start(f32[4,40,128]{2,1,0:T(8,128)S(1)} %collective-permute-done.8.far_ref), channel_id=1, source_target_pairs={{0,64},{1,65},{2,66},{3,67},{4,68},{5,69},{6,70},{7,71},{8,72},{9,... | collective-permute-start | bytes 245768 | tf_op jit(solution)/shard_map/ppermute | solution.py:32
  38.5 1.3 %collective-permute-start.11 = (f32[4,40,128]{2,1,0:T(8,128)S(1)}, f32[4,40,128]{2,1,0:T(8,128)S(1)}, u32[]{:S(2)}, u32[]{:S(2)}) collective-permute-start(f32[4,40,128]{2,1,0:T(8,128)S(1)} %collective-permute-done.9.near_ref), channel_id=1, source_target_pairs={{0,64},{1,65},{2,66},{3,67},{4,68},{5,69},{6,70},{7,71},{8,72},{9,... | collective-permute-start | bytes 245768 | tf_op jit(solution)/shard_map/ppermute | solution.py:32

commit v3 on v2

--- a/solution.py
+++ b/solution.py
@@ -52,21 +52,24 @@
     return inst, part - near_step(part, 1 + inst % 2)
 
 
-def pack_kernel(own_ref, other_ref, out_ref):
-    insts = own_ref.shape[0]
-    out_ref[:insts] = own_ref[...]
-    out_ref[insts:] = other_ref[...]
-
-
-def pack(own, other):
+def join_kernel(base, first_ref, second_ref, out_ref):
+    insts = out_ref.shape[0] // 2
+    out_ref[:insts] = first_ref[base : base + insts]
+    out_ref[insts:] = second_ref[base : base + insts]
+
+
+def join(first, second, base):
+    insts = first.shape[0] - base
     return pl.pallas_call(
-        pack_kernel,
-        out_shape=jax.ShapeDtypeStruct((2 * own.shape[0],) + own.shape[1:], jnp.float32),
+        functools.partial(join_kernel, base),
+        out_shape=jax.ShapeDtypeStruct((2 * insts,) + first.shape[1:], jnp.float32),
         in_specs=[pl.BlockSpec(memory_space=pltpu.VMEM)] * 2,
         out_specs=pl.BlockSpec(memory_space=pltpu.VMEM),
-        cost_estimate=pl.CostEstimate(flops=0, bytes_accessed=16 * own.size, transcendentals=0),
+        cost_estimate=pl.CostEstimate(
+            flops=0, bytes_accessed=8 * first.size, transcendentals=0
+        ),
         compiler_params=pltpu.CompilerParams(vmem_limit_bytes=2**20),
-    )(own, other)
+    )(first, second)
 
 
 def sublanes():
@@ -103,34 +106,81 @@
     return groups
 
 
-def regroup_kernel(blocks_ref, out_ref):
-    rows, columns, insts, faces = blocks_ref.shape
+CHUNKS = 4
+
+
+def stage_kernel(
+    state_ref,
+    element_ref,
+    faces_ref,
+    own_ref,
+    element_out_ref,
+    out_ref,
+    held_ref,
+    state_sem,
+    element_sem,
+    face_sems,
+):
+    rows, columns, insts, faces = faces_ref.shape
     lane_tiles = faces // 128
     stride = lane_tiles * insts
+    depth = rows // CHUNKS
+    copies = []
+    for c in range(CHUNKS):
+        part = pl.ds(c * depth, depth)
+        copies.append(
+            pltpu.make_async_copy(faces_ref.at[part], held_ref.at[part], face_sems.at[c])
+        )
+        copies[-1].start()
+    state_copy = pltpu.make_async_copy(state_ref, own_ref, state_sem)
+    state_copy.start()
+    element_copy = pltpu.make_async_copy(element_ref, element_out_ref, element_sem)
+    element_copy.start()
 
     def one_row(i, carry):
         base = pl.multiple_of(i * columns * stride, 8)
         for p in range(columns):
             for tile in range(lane_tiles):
-                out_ref[pl.ds(base + p * stride + tile * insts, insts), :] = blocks_ref[
+                out_ref[pl.ds(base + p * stride + tile * insts, insts), :] = held_ref[
                     i, p, :, tile * 128 : tile * 128 + 128
                 ]
         return carry
 
-    lax.fori_loop(0, rows, one_row, 0)
-
-
-def regroup(blocks):
+    for c in range(CHUNKS):
+        copies[c].wait()
+        lax.fori_loop(c * depth, (c + 1) * depth, one_row, 0)
+    state_copy.wait()
+    element_copy.wait()
+
+
+def stage(state, element_blocks, face_blocks):
+    anywhere = pl.BlockSpec(memory_space=pltpu.HBM)
+    vmem = pl.BlockSpec(memory_space=pltpu.VMEM)
     return pl.pallas_call(
-        regroup_kernel,
-        out_shape=jax.ShapeDtypeStruct((blocks.size // 128, 128), jnp.float32),
-        in_specs=[pl.BlockSpec(memory_space=pltpu.VMEM)],
-        out_specs=pl.BlockSpec(memory_space=pltpu.VMEM),
+        stage_kernel,
+        out_shape=(
+            pltpu.VMEM(state.shape, jnp.float32),
+            pltpu.VMEM(element_blocks.shape, jnp.float32),
+            pltpu.VMEM((face_blocks.size // 128, 128), jnp.float32),
+        ),
+        in_specs=[anywhere] * 3,
+        out_specs=(vmem, vmem, vmem),
+        scratch_shapes=[
+            pltpu.VMEM(face_blocks.shape, jnp.float32),
+            pltpu.SemaphoreType.DMA,
+            pltpu.SemaphoreType.DMA,
+            pltpu.SemaphoreType.DMA((CHUNKS,)),
+        ],
         cost_estimate=pl.CostEstimate(
-            flops=0, bytes_accessed=8 * blocks.size, transcendentals=0
+            flops=0, bytes_accessed=4 * element_blocks.size, transcendentals=0
         ),
-        compiler_params=pltpu.CompilerParams(vmem_limit_bytes=16 * 2**20),
-    )(blocks)
+        compiler_params=pltpu.CompilerParams(vmem_limit_bytes=4 * 2**20),
+    )(
+        *(
+            pltpu.with_memory_space_constraint(x, pltpu.HBM)
+            for x in (state, element_blocks, face_blocks)
+        )
+    )
 
 
 def corner_of(side, within):
@@ -160,8 +210,8 @@
 def jacobian_kernel(
     instances,
     part_total,
+    keep,
     counts_ref,
-    place_ref,
     owner_ref,
     side_ref,
     part_ref,
@@ -174,15 +224,16 @@
     chip_ref,
     far_ref,
     near_ref,
-    other_far_ref,
-    other_near_ref,
+    passed_ref,
     out_ref,
-    trace_ref,
-    across_ref,
-    spread_ref,
+    *rest,
 ):
-    my_part = place_ref[0]
-    on_first = place_ref[1] == 0
+    trace_ref, across_ref, spread_ref = rest[-3:] if keep else rest[1:4]
+    if not keep:
+        save = pltpu.make_async_copy(own_ref, rest[0], rest[4])
+        save.start()
+    my_part = lax.axis_index("dom")
+    on_first = (lax.axis_index("inst") & 1) == 0
     step_one = jnp.where((my_part & 1) == 0, 1, -1)
     step_two = jnp.where((my_part & 2) == 0, 2, -2)
     mine = jnp.where(on_first, step_one, step_two)
@@ -190,8 +241,8 @@
     neighbours = (
         (-mine, far_ref, 0),
         (mine, near_ref, 0),
-        (-others, other_far_ref, 1),
-        (others, other_near_ref, 1),
+        (-others, passed_ref, 0),
+        (others, passed_ref, 1),
     )
     insts, unknowns, elements = own_ref.shape
     variables = unknowns // 8
@@ -281,7 +332,7 @@
     landed = lax.dot_general(high, owned, dims, preferred_element_type=jnp.float32)
     landed += lax.dot_general(low, owned, dims, preferred_element_type=jnp.float32)
 
-    live = lax.broadcasted_iota(jnp.int32, shape, 1) < counts_ref[0]
+    live = lax.broadcasted_iota(jnp.int32, shape, 1) < counts_ref[...]
     mass = mass_ref[...]
     total_insts = insts * instances
     sources = (
@@ -307,10 +358,12 @@
             base = (t * variables + a) * 8
             value = element[a] + landed[base : base + 8, :] + mass * summed
             out_ref[t, rows, :] = jnp.where(live, value, 0.0)
+    if not keep:
+        save.wait()
 
 
 def jacobian_rows(
-    keep, counts, place, owner, side, part, nbr, mass, element_blocks, blocks, own, *fields
+    keep, counts, owner, side, part, nbr, mass, element_blocks, blocks, own, *fields
 ):
     part_total = lax.axis_size("dom")
     instances = lax.axis_size("inst")
@@ -318,22 +371,23 @@
     width = unknowns // 2
     stride = owner.shape[0] * insts
     vmem = pl.BlockSpec(memory_space=pltpu.VMEM)
-    smem = pl.BlockSpec(memory_space=pltpu.SMEM)
+    result = jax.ShapeDtypeStruct(own.shape, jnp.float32)
     return pl.pallas_call(
-        functools.partial(jacobian_kernel, instances, part_total),
-        out_shape=(pltpu.VMEM if keep else jax.ShapeDtypeStruct)(own.shape, jnp.float32),
-        in_specs=[smem, smem] + [vmem] * (8 + len(fields)),
-        out_specs=vmem,
+        functools.partial(jacobian_kernel, instances, part_total, keep),
+        out_shape=pltpu.VMEM(own.shape, jnp.float32) if keep else (result, result),
+        in_specs=[vmem] * (9 + len(fields)),
+        out_specs=vmem if keep else (vmem, pl.BlockSpec(memory_space=pl.ANY)),
         scratch_shapes=[
             pltpu.VMEM((width * stride, 128), jnp.float32),
             pltpu.VMEM(((width + 4) * 2 * stride, 128), jnp.float32),
             pltpu.VMEM((insts * unknowns, owner.shape[0] * 128), jnp.float32),
-        ],
+        ]
+        + ([] if keep else [pltpu.SemaphoreType.DMA]),
         cost_estimate=pl.CostEstimate(
             flops=4 * blocks.size, bytes_accessed=4 * blocks.size, transcendentals=0
         ),
-        compiler_params=pltpu.CompilerParams(vmem_limit_bytes=16 * 2**20),
-    )(counts, place, owner, side, part, nbr, mass, element_blocks, blocks, own, *fields)
+        compiler_params=pltpu.CompilerParams(vmem_limit_bytes=8 * 2**20),
+    )(counts, owner, side, part, nbr, mass, element_blocks, blocks, own, *fields)
 
 
 def on_device(
@@ -348,29 +402,27 @@
     face_nbr,
 ):
     tiles = face_blocks.shape[-1] // 128
-    blocks = regroup(jnp.transpose(face_blocks, (1, 2, 0, 3)))
     owner, side, part, nbr = (
         x.reshape(tiles, 128) for x in (face_owner, face_side, face_part, face_nbr)
     )
-    place = jnp.stack(
-        [lax.axis_index("dom"), lax.axis_index("inst") % 2]
-    ).astype(jnp.int32)
-
-    def apply_jacobian(vector, keep):
-        other = send(vector, to_core)
-        both = pack(vector, other)
+    live_count = counts.reshape(1, 1)
+    own, element_blocks, blocks = stage(
+        state, element_jacobian_blocks, jnp.transpose(face_blocks, (1, 2, 0, 3))
+    )
+
+    def apply_jacobian(vector, core, keep):
+        both = join(vector, core, 0)
         far = send(both, to_far)
         near = send(both, to_near)
         chip = send(both, to_chip)
-        other_near = send(near, to_core)
-        other_far = send(far, to_core)
+        passed = send(join(far, near, vector.shape[0]), to_core)
         return jacobian_rows(
-            keep, counts, place, owner, side, part, nbr, mass, element_jacobian_blocks, blocks, vector,
-            other, chip, far, near, other_far, other_near,
+            keep, live_count, owner, side, part, nbr, mass, element_blocks,
+            blocks, vector, core, chip, far, near, passed,
         )
 
-    first = apply_jacobian(state, True)
-    second = apply_jacobian(first, False)
+    first = apply_jacobian(own, send(state, to_core), True)
+    second, first = apply_jacobian(first, send(first, to_core), False)
     return first, second
 
 

time: 42.2 us -> 38.2 us (0.905)
  local copies, waits for them, and re-layouts: 4.54 us -> 0.02 us
  Pallas kernels: 3.84 us -> 4.94 us
  waiting for transfers between devices: 9.16 us -> 8.07 us
  starting transfers between devices: 22.9 us -> 23.7 us
    unnamed x21 -> x10, local copies, waits for them, and re-layouts: 4.54 us -> 0.02 us
    pallas_call x5 -> x7, Pallas kernels: 3.84 us -> 4.94 us  [the longest x2 2.66 us: jacobian_rows(): pl.pallas_call(functools.partial(jacobian_kernel, instances, part_total,...]
    ppermute x12 -> x10, waiting for transfers between devices: 9.16 us -> 8.07 us  [send(): return lax.ppermute(value, ('inst', 'dom'), joint(rule))]
    ppermute x12 -> x10, starting transfers between devices: 22.9 us -> 23.7 us  [send(): return lax.ppermute(value, ('inst', 'dom'), joint(rule))]
  transfers between devices with their start and end apart: 12 -> 10, of which waited for: 7 -> 6; matrix products, arithmetic and copies ran while one was open for 2% -> 0% of each run, Pallas kernels for 0% -> 6%
where the time goes in v3:
time: 38.2 us; the launch traced here: 38.1 us
  starting transfers between devices  23.7 us (62%)
  waiting for transfers between devices  8.07 us (21%)
  Pallas kernels  4.94 us (13%)
  between operations  1.39 us (4%)
    ppermute x10, starting transfers between devices, send(): return lax.ppermute(value, ('inst', 'dom'), joint(rule))  23.7 us
    ppermute x10, waiting for transfers between devices, send(): return lax.ppermute(value, ('inst', 'dom'), joint(rule))  8.07 us
    pallas_call x2, Pallas kernels, jacobian_rows(): pl.pallas_call(functools.partial(jacobian_kernel, instances, part_total,...  2.66 us
    pallas_call x1, Pallas kernels, stage(): pl.pallas_call(stage_kernel, out_shape=(pltpu.VMEM(state.shape, jnp.float...  2.25 us
  transfers between devices with their start and end apart: 10, of which 6 were waited for; matrix products, arithmetic and copies ran while one was open for 0% of the time, Pallas kernels for 6%

profile of v3, /device:TPU:1, one launch (start us, length us, event | category | flops | bytes accessed | tf_op | source)
XLA Modules:
  0.0 38.1 jit_solution(18359667002213547588)
XLA Ops:
  0.6 0.0 copy-start.4
  0.6 0.0 copy-start.3
  0.7 0.0 copy-start.2
  0.7 0.0 copy-start.1
  0.7 0.0 copy-start
  0.7 3.3 %collective-permute-start = (f32[2,40,128]{2,1,0:T(8,128)}, f32[2,40,128]{2,1,0:T(8,128)S(1)}, u32[]{:S(2)}, u32[]{:S(2)}) collective-permute-start(f32[2,40,128]{2,1,0:T(8,128)} %state_ref.1), channel_id=1, source_target_pairs={{0,64},{1,65},{2,66},{3,67},{4,68},{5,69},{6,70},{7,71},{8,72},{9,... | collective-permute-start | bytes 122888 | tf_op jit(solution)/shard_map/ppermute | solution.py:32
  4.0 2.2 %shard_map.104 = (f32[2,40,128]{2,1,0:T(8,128)S(1)}, f32[2,40,40,128]{3,2,1,0:T(8,128)S(1)}, f32[4800,128]{1,0:T(8,128)S(1)}) custom-call(f32[2,40,128]{2,1,0:T(8,128)} %state_ref.1, f32[2,40,40,128]{3,2,1,0:T(8,128)} %element_ref.1, f32[20,20,2,768]{3,2,1,0:T(2,128)} %bitcast.16), custom_call_target="tpu_custom_call" | custom-call | bytes 1638400 | tf_op jit(solution)/shard_map/pallas_call | solution.py:159
  6.3 0.0 collective-permute-done.second_ref.core_ref
  6.3 1.3 %collective-permute-start.3 = (f32[4,40,128]{2,1,0:T(8,128)S(1)}, f32[4,40,128]{2,1,0:T(8,128)S(1)}, u32[]{:S(2)}, u32[]{:S(2)}) collective-permute-start(f32[4,40,128]{2,1,0:T(8,128)S(1)} %shard_map.105), channel_id=1, source_target_pairs={{0,1},{1,0},{2,3},{3,2},{4,5},{5,4},{6,7},{7,6},{8,9},{9,8},{10,11... | collective-permute-start | bytes 245768 | tf_op jit(solution)/shard_map/ppermute | solution.py:32
  7.6 9.0 %collective-permute-start.2 = (f32[4,40,128]{2,1,0:T(8,128)S(1)}, f32[4,40,128]{2,1,0:T(8,128)S(1)}, u32[]{:S(2)}, u32[]{:S(2)}) collective-permute-start(f32[4,40,128]{2,1,0:T(8,128)S(1)} %shard_map.105), channel_id=1, source_target_pairs={{0,63},{1,2},{2,1},{3,4},{4,3},{5,6},{6,5},{7,8},{8,7},{9,10},{10,... | collective-permute-start | bytes 245768 | tf_op jit(solution)/shard_map/ppermute | solution.py:32
  16.7 0.4 %collective-permute-start.1 = (f32[4,40,128]{2,1,0:T(8,128)S(1)}, f32[4,40,128]{2,1,0:T(8,128)S(1)}, u32[]{:S(2)}, u32[]{:S(2)}) collective-permute-start(f32[4,40,128]{2,1,0:T(8,128)S(1)} %shard_map.105), channel_id=1, source_target_pairs={{0,128},{1,129},{2,130},{3,131},{4,132},{5,133},{6,134},{7,135},{8... | collective-permute-start | bytes 245768 | tf_op jit(solution)/shard_map/ppermute | solution.py:32
  17.1 0.0 collective-permute-done.3.second_ref.near_ref
  17.1 3.1 %collective-permute-done.2.first_ref.far_ref = f32[4,40,128]{2,1,0:T(8,128)S(1)} collective-permute-done((f32[4,40,128]{2,1,0:T(8,128)S(1)}, f32[4,40,128]{2,1,0:T(8,128)S(1)}, u32[]{:S(2)}, u32[]{:S(2)}) %collective-permute-start.2) | collective-permute-done | bytes 81952 | tf_op jit(solution)/shard_map/ppermute | solution.py:32
  20.2 0.0 collective-permute-start.4
  20.9 0.1 collective-permute-done.1.chip_ref
  21.0 0.5 %collective-permute-done.4.passed_ref = f32[4,40,128]{2,1,0:T(8,128)S(1)} collective-permute-done((f32[4,40,128]{2,1,0:T(8,128)S(1)}, f32[4,40,128]{2,1,0:T(8,128)S(1)}, u32[]{:S(2)}, u32[]{:S(2)}) %collective-permute-start.4) | collective-permute-done | bytes 81952 | tf_op jit(solution)/shard_map/ppermute | solution.py:32
  21.5 0.0 copy-done.4
  21.5 0.0 copy-done.3
  21.5 0.0 copy-done.2
  21.5 0.0 copy-done.1
  21.5 1.0 %shard_map.107.first_ref.own_ref = f32[2,40,128]{2,1,0:T(8,128)S(1)} custom-call(s32[1,1]{1,0:T(1,128)} %bitcast.6.counts_ref, s32[6,128]{1,0:T(8,128)S(1)} %bitcast.8, s32[6,128]{1,0:T(8,128)S(1)} %bitcast.10, s32[6,128]{1,0:T(8,128)S(1)} %bitcast.12, s32[6,128]{1,0:T(8,128)S(1)} %bitcast.14, f32[8,128]{1,0:T(8,128)S(1)} %copy-done.4, ...), custom_call_target="tpu_custom_call" | custom-call | flops 2457600 | bytes 2457600 | tf_op jit(solution)/shard_map/pallas_call | solution.py:375
  22.6 0.2 collective-permute-start.5
  22.8 1.1 %collective-permute-done.5.second_ref.core_ref = f32[2,40,128]{2,1,0:T(8,128)S(1)} collective-permute-done((f32[2,40,128]{2,1,0:T(8,128)S(1)}, f32[2,40,128]{2,1,0:T(8,128)S(1)}, u32[]{:S(2)}, u32[]{:S(2)}) %collective-permute-start.5) | collective-permute-done | bytes 40992 | tf_op jit(solution)/shard_map/ppermute | solution.py:32
  23.9 0.0 collective-permute-start.8
  23.9 8.1 %collective-permute-start.7 = (f32[4,40,128]{2,1,0:T(8,128)S(1)}, f32[4,40,128]{2,1,0:T(8,128)S(1)}, u32[]{:S(2)}, u32[]{:S(2)}) collective-permute-start(f32[4,40,128]{2,1,0:T(8,128)S(1)} %shard_map.108), channel_id=1, source_target_pairs={{0,63},{1,2},{2,1},{3,4},{4,3},{5,6},{6,5},{7,8},{8,7},{9,10},{10,... | collective-permute-start | bytes 245768 | tf_op jit(solution)/shard_map/ppermute | solution.py:32
  32.0 0.4 %collective-permute-start.6 = (f32[4,40,128]{2,1,0:T(8,128)S(1)}, f32[4,40,128]{2,1,0:T(8,128)S(1)}, u32[]{:S(2)}, u32[]{:S(2)}) collective-permute-start(f32[4,40,128]{2,1,0:T(8,128)S(1)} %shard_map.108), channel_id=1, source_target_pairs={{0,128},{1,129},{2,130},{3,131},{4,132},{5,133},{6,134},{7,135},{8... | collective-permute-start | bytes 245768 | tf_op jit(solution)/shard_map/ppermute | solution.py:32
  32.4 0.0 collective-permute-done.8.second_ref.near_ref
  32.4 2.3 %collective-permute-done.7.first_ref.far_ref = f32[4,40,128]{2,1,0:T(8,128)S(1)} collective-permute-done((f32[4,40,128]{2,1,0:T(8,128)S(1)}, f32[4,40,128]{2,1,0:T(8,128)S(1)}, u32[]{:S(2)}, u32[]{:S(2)}) %collective-permute-start.7) | collective-permute-done | bytes 81952 | tf_op jit(solution)/shard_map/ppermute | solution.py:32
  34.7 0.9 %collective-permute-start.9 = (f32[4,40,128]{2,1,0:T(8,128)S(1)}, f32[4,40,128]{2,1,0:T(8,128)S(1)}, u32[]{:S(2)}, u32[]{:S(2)}) collective-permute-start(f32[4,40,128]{2,1,0:T(8,128)S(1)} %shard_map.109), channel_id=1, source_target_pairs={{0,64},{1,65},{2,66},{3,67},{4,68},{5,69},{6,70},{7,71},{8,72},{9,... | collective-permute-start | bytes 245768 | tf_op jit(solution)/shard_map/ppermute | solution.py:32
  35.5 0.0 collective-permute-done.6.chip_ref
  35.5 0.9 %collective-permute-done.9.passed_ref = f32[4,40,128]{2,1,0:T(8,128)S(1)} collective-permute-done((f32[4,40,128]{2,1,0:T(8,128)S(1)}, f32[4,40,128]{2,1,0:T(8,128)S(1)}, u32[]{:S(2)}, u32[]{:S(2)}) %collective-permute-start.9) | collective-permute-done | bytes 81952 | tf_op jit(solution)/shard_map/ppermute | solution.py:32
  36.5 1.6 %shard_map.110 = (f32[2,40,128]{2,1,0:T(8,128)}, f32[2,40,128]{2,1,0:T(8,128)}) custom-call(s32[1,1]{1,0:T(1,128)} %bitcast.7.counts_ref, s32[6,128]{1,0:T(8,128)S(1)} %bitcast.9, s32[6,128]{1,0:T(8,128)S(1)} %bitcast.11, s32[6,128]{1,0:T(8,128)S(1)} %bitcast.13, s32[6,128]{1,0:T(8,128)S(1)} %bitcast.15, f32[8,128]{1,0:T(8,128)S(1)} %copy-done.4, ...), custom_call_target="tpu_custom_call" | custom-call | flops 2457600 | bytes 2457600 | tf_op jit(solution)/shard_map/pallas_call | solution.py:375
  (5 shorter events, 0.0 us)
Async XLA Ops:
  0.6 20.9 %copy-start.4 = (f32[8,128]{1,0:T(8,128)S(1)}, f32[8,128]{1,0:T(8,128)}, u32[]{:S(2)}) copy-start(f32[8,128]{1,0:T(8,128)} %mass_ref.3) | copy-start | bytes 12292
  0.6 20.9 %copy-start.3 = (s32[768]{0:T(1024)S(1)}, s32[768]{0:T(1024)}, u32[]{:S(2)}) copy-start(s32[768]{0:T(1024)} %param.17) | copy-start | bytes 9220
  0.7 20.9 %copy-start.2 = (s32[768]{0:T(1024)S(1)}, s32[768]{0:T(1024)}, u32[]{:S(2)}) copy-start(s32[768]{0:T(1024)} %param.16) | copy-start | bytes 9220
  0.7 20.8 %copy-start.1 = (s32[768]{0:T(1024)S(1)}, s32[768]{0:T(1024)}, u32[]{:S(2)}) copy-start(s32[768]{0:T(1024)} %param.15) | copy-start | bytes 9220
  0.7 20.8 %copy-start = (s32[768]{0:T(1024)S(1)}, s32[768]{0:T(1024)}, u32[]{:S(2)}) copy-start(s32[768]{0:T(1024)} %param.14) | copy-start | bytes 9220
  0.7 5.6 %collective-permute-start = (f32[2,40,128]{2,1,0:T(8,128)}, f32[2,40,128]{2,1,0:T(8,128)S(1)}, u32[]{:S(2)}, u32[]{:S(2)}) collective-permute-start(f32[2,40,128]{2,1,0:T(8,128)} %state_ref.1), channel_id=1, source_target_pairs={{0,64},{1,65},{2,66},{3,67},{4,68},{5,69},{6,70},{7,71},{8,72},{9,... | collective-permute-start | bytes 122888 | tf_op jit(solution)/shard_map/ppermute | solution.py:32
  6.3 10.8 %collective-permute-start.3 = (f32[4,40,128]{2,1,0:T(8,128)S(1)}, f32[4,40,128]{2,1,0:T(8,128)S(1)}, u32[]{:S(2)}, u32[]{:S(2)}) collective-permute-start(f32[4,40,128]{2,1,0:T(8,128)S(1)} %shard_map.105), channel_id=1, source_target_pairs={{0,1},{1,0},{2,3},{3,2},{4,5},{5,4},{6,7},{7,6},{8,9},{9,8},{10,11... | collective-permute-start | bytes 245768 | tf_op jit(solution)/shard_map/ppermute | solution.py:32
  7.6 12.6 %collective-permute-start.2 = (f32[4,40,128]{2,1,0:T(8,128)S(1)}, f32[4,40,128]{2,1,0:T(8,128)S(1)}, u32[]{:S(2)}, u32[]{:S(2)}) collective-permute-start(f32[4,40,128]{2,1,0:T(8,128)S(1)} %shard_map.105), channel_id=1, source_target_pairs={{0,63},{1,2},{2,1},{3,4},{4,3},{5,6},{6,5},{7,8},{8,7},{9,10},{10,... | collective-permute-start | bytes 245768 | tf_op jit(solution)/shard_map/ppermute | solution.py:32
  16.7 4.3 %collective-permute-start.1 = (f32[4,40,128]{2,1,0:T(8,128)S(1)}, f32[4,40,128]{2,1,0:T(8,128)S(1)}, u32[]{:S(2)}, u32[]{:S(2)}) collective-permute-start(f32[4,40,128]{2,1,0:T(8,128)S(1)} %shard_map.105), channel_id=1, source_target_pairs={{0,128},{1,129},{2,130},{3,131},{4,132},{5,133},{6,134},{7,135},{8... | collective-permute-start | bytes 245768 | tf_op jit(solution)/shard_map/ppermute | solution.py:32
  20.2 1.3 %collective-permute-start.4 = (f32[4,40,128]{2,1,0:T(8,128)S(1)}, f32[4,40,128]{2,1,0:T(8,128)S(1)}, u32[]{:S(2)}, u32[]{:S(2)}) collective-permute-start(f32[4,40,128]{2,1,0:T(8,128)S(1)} %shard_map.106), channel_id=1, source_target_pairs={{0,64},{1,65},{2,66},{3,67},{4,68},{5,69},{6,70},{7,71},{8,72},{9,... | collective-permute-start | bytes 245768 | tf_op jit(solution)/shard_map/ppermute | solution.py:32
  22.6 1.3 %collective-permute-start.5 = (f32[2,40,128]{2,1,0:T(8,128)S(1)}, f32[2,40,128]{2,1,0:T(8,128)S(1)}, u32[]{:S(2)}, u32[]{:S(2)}) collective-permute-start(f32[2,40,128]{2,1,0:T(8,128)S(1)} %shard_map.107.first_ref.own_ref), channel_id=1, source_target_pairs={{0,64},{1,65},{2,66},{3,67},{4,68},{5,69},{6,70},{7,71},{8,72},{9,... | collective-permute-start | bytes 122888 | tf_op jit(solution)/shard_map/ppermute | solution.py:32
  23.9 8.5 %collective-permute-start.8 = (f32[4,40,128]{2,1,0:T(8,128)S(1)}, f32[4,40,128]{2,1,0:T(8,128)S(1)}, u32[]{:S(2)}, u32[]{:S(2)}) collective-permute-start(f32[4,40,128]{2,1,0:T(8,128)S(1)} %shard_map.108), channel_id=1, source_target_pairs={{0,1},{1,0},{2,3},{3,2},{4,5},{5,4},{6,7},{7,6},{8,9},{9,8},{10,11... | collective-permute-start | bytes 245768 | tf_op jit(solution)/shard_map/ppermute | solution.py:32
  23.9 10.8 %collective-permute-start.7 = (f32[4,40,128]{2,1,0:T(8,128)S(1)}, f32[4,40,128]{2,1,0:T(8,128)S(1)}, u32[]{:S(2)}, u32[]{:S(2)}) collective-permute-start(f32[4,40,128]{2,1,0:T(8,128)S(1)} %shard_map.108), channel_id=1, source_target_pairs={{0,63},{1,2},{2,1},{3,4},{4,3},{5,6},{6,5},{7,8},{8,7},{9,10},{10,... | collective-permute-start | bytes 245768 | tf_op jit(solution)/shard_map/ppermute | solution.py:32
  32.0 3.6 %collective-permute-start.6 = (f32[4,40,128]{2,1,0:T(8,128)S(1)}, f32[4,40,128]{2,1,0:T(8,128)S(1)}, u32[]{:S(2)}, u32[]{:S(2)}) collective-permute-start(f32[4,40,128]{2,1,0:T(8,128)S(1)} %shard_map.108), channel_id=1, source_target_pairs={{0,128},{1,129},{2,130},{3,131},{4,132},{5,133},{6,134},{7,135},{8... | collective-permute-start | bytes 245768 | tf_op jit(solution)/shard_map/ppermute | solution.py:32
  34.7 1.8 %collective-permute-start.9 = (f32[4,40,128]{2,1,0:T(8,128)S(1)}, f32[4,40,128]{2,1,0:T(8,128)S(1)}, u32[]{:S(2)}, u32[]{:S(2)}) collective-permute-start(f32[4,40,128]{2,1,0:T(8,128)S(1)} %shard_map.109), channel_id=1, source_target_pairs={{0,64},{1,65},{2,66},{3,67},{4,68},{5,69},{6,70},{7,71},{8,72},{9,... | collective-permute-start | bytes 245768 | tf_op jit(solution)/shard_map/ppermute | solution.py:32

commit v4 on v3

--- a/solution.py
+++ b/solution.py
@@ -52,24 +52,26 @@
     return inst, part - near_step(part, 1 + inst % 2)
 
 
-def join_kernel(base, first_ref, second_ref, out_ref):
+def join_kernel(base, first_ref, second_ref, *rest):
+    out_ref = rest[-1]
     insts = out_ref.shape[0] // 2
     out_ref[:insts] = first_ref[base : base + insts]
     out_ref[insts:] = second_ref[base : base + insts]
 
 
-def join(first, second, base):
+def join(first, second, base, *after):
     insts = first.shape[0] - base
     return pl.pallas_call(
         functools.partial(join_kernel, base),
         out_shape=jax.ShapeDtypeStruct((2 * insts,) + first.shape[1:], jnp.float32),
-        in_specs=[pl.BlockSpec(memory_space=pltpu.VMEM)] * 2,
+        in_specs=[pl.BlockSpec(memory_space=pltpu.VMEM)] * 2
+        + [pl.BlockSpec(memory_space=pl.ANY)] * len(after),
         out_specs=pl.BlockSpec(memory_space=pltpu.VMEM),
         cost_estimate=pl.CostEstimate(
             flops=0, bytes_accessed=8 * first.size, transcendentals=0
         ),
         compiler_params=pltpu.CompilerParams(vmem_limit_bytes=2**20),
-    )(first, second)
+    )(first, second, *after)
 
 
 def sublanes():
@@ -91,33 +93,66 @@
     return tiles[0]
 
 
-def element_term(vector_ref, blocks_ref, t):
-    unknowns = vector_ref.shape[1]
-    tiles = [vector_ref[t, 8 * g : 8 * g + 8, :] for g in range(unknowns // 8)]
-    groups = []
-    for group in range(unknowns // 8):
-        partial = []
-        for i in range(8 * group, 8 * group + 8):
-            total = blocks_ref[t, i, 0:8, :] * tiles[0]
-            for g in range(1, unknowns // 8):
-                total += blocks_ref[t, i, 8 * g : 8 * g + 8, :] * tiles[g]
-            partial.append(total)
-        groups.append(fold_rows(partial))
-    return groups
+def element_rows(vector_ref, blocks_ref, out_ref):
+    insts, unknowns, _ = out_ref.shape
+    for t in range(insts):
+        tiles = [vector_ref[t, 8 * g : 8 * g + 8, :] for g in range(unknowns // 8)]
+        for group in range(unknowns // 8):
+            partial = []
+            for i in range(8 * group, 8 * group + 8):
+                total = blocks_ref[t, i, 0:8, :] * tiles[0]
+                for g in range(1, unknowns // 8):
+                    total += blocks_ref[t, i, 8 * g : 8 * g + 8, :] * tiles[g]
+                partial.append(total)
+            out_ref[t, 8 * group : 8 * group + 8, :] = fold_rows(partial)
+
+
+def element_term(vector, blocks):
+    return pl.pallas_call(
+        element_rows,
+        out_shape=jax.ShapeDtypeStruct(blocks.shape[:2] + blocks.shape[3:], jnp.float32),
+        in_specs=[pl.BlockSpec(memory_space=pltpu.VMEM)] * 2,
+        out_specs=pl.BlockSpec(memory_space=pltpu.VMEM),
+        cost_estimate=pl.CostEstimate(
+            flops=2 * blocks.size, bytes_accessed=4 * blocks.size, transcendentals=0
+        ),
+        compiler_params=pltpu.CompilerParams(vmem_limit_bytes=4 * 2**20),
+    )(vector, blocks)
 
 
 CHUNKS = 4
 
 
+def fetch_kernel(source_ref, out_ref, sem):
+    copy = pltpu.make_async_copy(source_ref, out_ref, sem)
+    copy.start()
+    copy.wait()
+
+
+def fetch(value):
+    return pl.pallas_call(
+        fetch_kernel,
+        out_shape=pltpu.VMEM(value.shape, jnp.float32),
+        in_specs=[pl.BlockSpec(memory_space=pltpu.HBM)],
+        out_specs=pl.BlockSpec(memory_space=pltpu.VMEM),
+        scratch_shapes=[pltpu.SemaphoreType.DMA],
+        cost_estimate=pl.CostEstimate(
+            flops=0, bytes_accessed=8 * value.size, transcendentals=0
+        ),
+        compiler_params=pltpu.CompilerParams(vmem_limit_bytes=2**20),
+    )(pltpu.with_memory_space_constraint(value, pltpu.HBM))
+
+
 def stage_kernel(
-    state_ref,
     element_ref,
     faces_ref,
-    own_ref,
+    both_ref,
+    owner_ref,
     element_out_ref,
     out_ref,
+    owned_ref,
+    product_ref,
     held_ref,
-    state_sem,
     element_sem,
     face_sems,
 ):
@@ -132,10 +167,18 @@
             pltpu.make_async_copy(faces_ref.at[part], held_ref.at[part], face_sems.at[c])
         )
         copies[-1].start()
-    state_copy = pltpu.make_async_copy(state_ref, own_ref, state_sem)
-    state_copy.start()
     element_copy = pltpu.make_async_copy(element_ref, element_out_ref, element_sem)
     element_copy.start()
+
+    slot = lax.broadcasted_iota(jnp.int32, (owned_ref.shape[0], 128), 0)
+    owned = jnp.concatenate(
+        [
+            jnp.broadcast_to(owner_ref[tile : tile + 1, :], slot.shape) == slot
+            for tile in range(lane_tiles)
+        ],
+        axis=1,
+    )
+    owned_ref[...] = jnp.where(owned, 1.0, 0.0).astype(jnp.bfloat16)
 
     def one_row(i, carry):
         base = pl.multiple_of(i * columns * stride, 8)
@@ -149,25 +192,26 @@
     for c in range(CHUNKS):
         copies[c].wait()
         lax.fori_loop(c * depth, (c + 1) * depth, one_row, 0)
-    state_copy.wait()
     element_copy.wait()
-
-
-def stage(state, element_blocks, face_blocks):
-    anywhere = pl.BlockSpec(memory_space=pltpu.HBM)
+    element_rows(both_ref, element_out_ref, product_ref)
+
+
+def stage(element_blocks, face_blocks, both, owner):
+    hbm = pl.BlockSpec(memory_space=pltpu.HBM)
     vmem = pl.BlockSpec(memory_space=pltpu.VMEM)
+    insts, unknowns, _, elements = element_blocks.shape
     return pl.pallas_call(
         stage_kernel,
         out_shape=(
-            pltpu.VMEM(state.shape, jnp.float32),
             pltpu.VMEM(element_blocks.shape, jnp.float32),
             pltpu.VMEM((face_blocks.size // 128, 128), jnp.float32),
-        ),
-        in_specs=[anywhere] * 3,
-        out_specs=(vmem, vmem, vmem),
+            pltpu.VMEM((elements, owner.size), jnp.bfloat16),
+            pltpu.VMEM((insts, unknowns, elements), jnp.float32),
+        ),
+        in_specs=[hbm, hbm, vmem, vmem],
+        out_specs=(vmem, vmem, vmem, vmem),
         scratch_shapes=[
             pltpu.VMEM(face_blocks.shape, jnp.float32),
-            pltpu.SemaphoreType.DMA,
             pltpu.SemaphoreType.DMA,
             pltpu.SemaphoreType.DMA((CHUNKS,)),
         ],
@@ -176,10 +220,10 @@
         ),
         compiler_params=pltpu.CompilerParams(vmem_limit_bytes=4 * 2**20),
     )(
-        *(
-            pltpu.with_memory_space_constraint(x, pltpu.HBM)
-            for x in (state, element_blocks, face_blocks)
-        )
+        pltpu.with_memory_space_constraint(element_blocks, pltpu.HBM),
+        pltpu.with_memory_space_constraint(face_blocks, pltpu.HBM),
+        both,
+        owner,
     )
 
 
@@ -212,12 +256,12 @@
     part_total,
     keep,
     counts_ref,
-    owner_ref,
+    owned_ref,
     side_ref,
     part_ref,
     nbr_ref,
     mass_ref,
-    element_blocks_ref,
+    element_ref,
     blocks_ref,
     own_ref,
     core_ref,
@@ -244,10 +288,10 @@
         (-others, passed_ref, 0),
         (others, passed_ref, 1),
     )
-    insts, unknowns, elements = own_ref.shape
+    insts, unknowns, _ = own_ref.shape
     variables = unknowns // 8
     width = 4 * variables
-    lane_tiles = owner_ref.shape[0]
+    lane_tiles = side_ref.shape[0]
     stride = lane_tiles * insts
     row = sublanes()
     shape = (8, 128)
@@ -316,15 +360,7 @@
                     tile * 128 : tile * 128 + 128,
                 ] = jnp.where(held, moved, 0.0)
 
-    slot = lax.broadcasted_iota(jnp.int32, (elements, 128), 0)
-    owned = jnp.concatenate(
-        [
-            (jnp.broadcast_to(owner_ref[tile : tile + 1, :], slot.shape) == slot)
-            for tile in range(lane_tiles)
-        ],
-        axis=1,
-    )
-    owned = jnp.where(owned, 1.0, 0.0).astype(jnp.bfloat16)
+    owned = owned_ref[...]
     spread = spread_ref[...]
     high = spread.astype(jnp.bfloat16)
     low = (spread - high.astype(jnp.float32)).astype(jnp.bfloat16)
@@ -342,7 +378,6 @@
         (chip_ref, insts, 1, -1),
     )
     for t in range(insts):
-        element = element_term(own_ref, element_blocks_ref, t)
         for a in range(variables):
             rows = slice(8 * a, 8 * a + 8)
             summed = None
@@ -356,20 +391,20 @@
                     term = weight * ref[base + s, rows, :]
                     summed = term if summed is None else summed + term
             base = (t * variables + a) * 8
-            value = element[a] + landed[base : base + 8, :] + mass * summed
+            value = element_ref[t, rows, :] + landed[base : base + 8, :] + mass * summed
             out_ref[t, rows, :] = jnp.where(live, value, 0.0)
     if not keep:
         save.wait()
 
 
 def jacobian_rows(
-    keep, counts, owner, side, part, nbr, mass, element_blocks, blocks, own, *fields
+    keep, counts, owned, side, part, nbr, mass, element, blocks, own, *fields
 ):
     part_total = lax.axis_size("dom")
     instances = lax.axis_size("inst")
     insts, unknowns, _ = own.shape
     width = unknowns // 2
-    stride = owner.shape[0] * insts
+    stride = side.shape[0] * insts
     vmem = pl.BlockSpec(memory_space=pltpu.VMEM)
     result = jax.ShapeDtypeStruct(own.shape, jnp.float32)
     return pl.pallas_call(
@@ -380,14 +415,14 @@
         scratch_shapes=[
             pltpu.VMEM((width * stride, 128), jnp.float32),
             pltpu.VMEM(((width + 4) * 2 * stride, 128), jnp.float32),
-            pltpu.VMEM((insts * unknowns, owner.shape[0] * 128), jnp.float32),
+            pltpu.VMEM((insts * unknowns, side.shape[0] * 128), jnp.float32),
         ]
         + ([] if keep else [pltpu.SemaphoreType.DMA]),
         cost_estimate=pl.CostEstimate(
             flops=4 * blocks.size, bytes_accessed=4 * blocks.size, transcendentals=0
         ),
         compiler_params=pltpu.CompilerParams(vmem_limit_bytes=8 * 2**20),
-    )(counts, owner, side, part, nbr, mass, element_blocks, blocks, own, *fields)
+    )(counts, owned, side, part, nbr, mass, element, blocks, own, *fields)
 
 
 def on_device(
@@ -406,23 +441,30 @@
         x.reshape(tiles, 128) for x in (face_owner, face_side, face_part, face_nbr)
     )
     live_count = counts.reshape(1, 1)
-    own, element_blocks, blocks = stage(
-        state, element_jacobian_blocks, jnp.transpose(face_blocks, (1, 2, 0, 3))
-    )
-
-    def apply_jacobian(vector, core, keep):
-        both = join(vector, core, 0)
+    def exchange(both, *after):
         far = send(both, to_far)
         near = send(both, to_near)
         chip = send(both, to_chip)
-        passed = send(join(far, near, vector.shape[0]), to_core)
-        return jacobian_rows(
-            keep, live_count, owner, side, part, nbr, mass, element_blocks,
-            blocks, vector, core, chip, far, near, passed,
-        )
-
-    first = apply_jacobian(own, send(state, to_core), True)
-    second, first = apply_jacobian(first, send(first, to_core), False)
+        passed = send(join(far, near, both.shape[0] // 2, *after), to_core)
+        return chip, far, near, passed
+
+    core = send(state, to_core)
+    own = fetch(state)
+    both = join(own, core, 0)
+    element_blocks, blocks, owned, element = stage(
+        element_jacobian_blocks, jnp.transpose(face_blocks, (1, 2, 0, 3)), both, owner
+    )
+    first = jacobian_rows(
+        True, live_count, owned, side, part, nbr, mass, element, blocks, own, core,
+        *exchange(both, element),
+    )
+
+    core = send(first, to_core)
+    element = element_term(first, element_blocks)
+    second, first = jacobian_rows(
+        False, live_count, owned, side, part, nbr, mass, element, blocks, first, core,
+        *exchange(join(first, core, 0), element),
+    )
     return first, second
 
 

time: 38.2 us -> 37.2 us (0.974)
  starting transfers between devices: 23.7 us -> 20.5 us
  waiting for transfers between devices: 8.07 us -> 8.81 us
  Pallas kernels: 4.94 us -> 5.64 us
  local copies, waits for them, and re-layouts: 0.02 us -> 0.7 us
    ppermute x10, starting transfers between devices: 23.7 us -> 20.5 us  [send(): return lax.ppermute(value, ('inst', 'dom'), joint(rule))]
    pallas_call x1 -> x3, Pallas kernels: 2.25 us -> 3.3 us  [the longest x1 2.37 us: stage(): pl.pallas_call(stage_kernel, out_shape=(pltpu.VMEM(element_blocks.shape,...]
    ppermute x10, waiting for transfers between devices: 8.07 us -> 8.81 us  [send(): return lax.ppermute(value, ('inst', 'dom'), joint(rule))]
    unnamed x10, local copies, waits for them, and re-layouts: 0.02 us -> 0.7 us
  transfers between devices with their start and end apart: 10 -> 10, of which waited for: 6 -> 7; matrix products, arithmetic and copies ran while one was open for 0% -> 0% of each run, Pallas kernels for 6% -> 9%
where the time goes in v4:
time: 37.2 us; the launch traced here: 37.1 us
  starting transfers between devices  20.5 us (55%)
  waiting for transfers between devices  8.81 us (24%)
  Pallas kernels  5.64 us (15%)
  between operations  1.37 us (4%)
  local copies, waits for them, and re-layouts  0.7 us (2%)
    ppermute x10, starting transfers between devices, send(): return lax.ppermute(value, ('inst', 'dom'), joint(rule))  20.5 us
    ppermute x10, waiting for transfers between devices, send(): return lax.ppermute(value, ('inst', 'dom'), joint(rule))  8.81 us
    pallas_call x1, Pallas kernels, stage(): pl.pallas_call(stage_kernel, out_shape=(pltpu.VMEM(element_blocks.shape,...  2.37 us
    pallas_call x2, Pallas kernels, jacobian_rows(): pl.pallas_call(functools.partial(jacobian_kernel, instances, part_total,...  2.31 us
    pallas_call x1, Pallas kernels, fetch(): pl.pallas_call(fetch_kernel, out_shape=pltpu.VMEM(value.shape, jnp.float3...  0.79 us
  transfers between devices with their start and end apart: 10, of which 7 were waited for; matrix products, arithmetic and copies ran while one was open for 0% of the time, Pallas kernels for 9%

profile of v4, /device:TPU:1, one launch (start us, length us, event | category | flops | bytes accessed | tf_op | source)
XLA Modules:
  0.0 37.1 jit_solution(9918694529493193558)
XLA Ops:
  0.6 0.0 copy-start
  0.6 0.0 copy-start.1
  0.7 0.0 copy-start.2
  0.7 0.0 copy-start.3
  0.7 3.3 %collective-permute-start = (f32[2,40,128]{2,1,0:T(8,128)}, f32[2,40,128]{2,1,0:T(8,128)S(1)}, u32[]{:S(2)}, u32[]{:S(2)}) collective-permute-start(f32[2,40,128]{2,1,0:T(8,128)} %source_ref.1), channel_id=1, source_target_pairs={{0,64},{1,65},{2,66},{3,67},{4,68},{5,69},{6,70},{7,71},{8,72},{9,... | collective-permute-start | bytes 122888 | tf_op jit(solution)/shard_map/ppermute | solution.py:32
  4.0 0.8 %shard_map.104.first_ref.own_ref = f32[2,40,128]{2,1,0:T(8,128)S(1)} custom-call(f32[2,40,128]{2,1,0:T(8,128)} %source_ref.1), custom_call_target="tpu_custom_call" | custom-call | bytes 81920 | tf_op jit(solution)/shard_map/pallas_call | solution.py:133
  4.8 0.3 collective-permute-done.second_ref.core_ref
  5.1 9.1 %collective-permute-start.2 = (f32[4,40,128]{2,1,0:T(8,128)S(1)}, f32[4,40,128]{2,1,0:T(8,128)S(1)}, u32[]{:S(2)}, u32[]{:S(2)}) collective-permute-start(f32[4,40,128]{2,1,0:T(8,128)S(1)} %shard_map.105.both_ref), channel_id=1, source_target_pairs={{0,63},{1,2},{2,1},{3,4},{4,3},{5,6},{6,5},{7,8},{8,7},{9,10},{10,... | collective-permute-start | bytes 245768 | tf_op jit(solution)/shard_map/ppermute | solution.py:32
  14.2 0.0 collective-permute-start.3
  14.2 0.4 %collective-permute-start.1 = (f32[4,40,128]{2,1,0:T(8,128)S(1)}, f32[4,40,128]{2,1,0:T(8,128)S(1)}, u32[]{:S(2)}, u32[]{:S(2)}) collective-permute-start(f32[4,40,128]{2,1,0:T(8,128)S(1)} %shard_map.105.both_ref), channel_id=1, source_target_pairs={{0,128},{1,129},{2,130},{3,131},{4,132},{5,133},{6,134},{7,135},{8... | collective-permute-start | bytes 245768 | tf_op jit(solution)/shard_map/ppermute | solution.py:32
  14.6 0.7 %copy-done.4 = s32[768]{0:T(1024)S(1)} copy-done((s32[768]{0:T(1024)S(1)}, s32[768]{0:T(1024)}, u32[]{:S(2)}) %copy-start.4) | copy-done | bytes 3096
  15.3 2.4 %shard_map.106 = (f32[2,40,40,128]{3,2,1,0:T(8,128)S(1)}, f32[4800,128]{1,0:T(8,128)S(1)}, bf16[128,768]{1,0:T(8,128)(2,1)S(1)}, f32[2,40,128]{2,1,0:T(8,128)S(1)}) custom-call(f32[2,40,40,128]{3,2,1,0:T(8,128)} %element_ref.1, f32[20,20,2,768]{3,2,1,0:T(2,128)} %bitcast.15, f32[4,40,128]{2,1,0:T(8,128)S(1)} %shard_map.105.both_ref, s32[6,128]{1,0:T(8,128)S(1)} %bitcast.14), custom_call_target="tpu_custom_call" | custom-call | bytes 1638400 | tf_op jit(solution)/shard_map/pallas_call | solution.py:203
  17.7 0.0 collective-permute-done.2.first_ref.far_ref
  17.7 1.6 %collective-permute-done.3.second_ref.near_ref = f32[4,40,128]{2,1,0:T(8,128)S(1)} collective-permute-done((f32[4,40,128]{2,1,0:T(8,128)S(1)}, f32[4,40,128]{2,1,0:T(8,128)S(1)}, u32[]{:S(2)}, u32[]{:S(2)}) %collective-permute-start.3) | collective-permute-done | bytes 81952 | tf_op jit(solution)/shard_map/ppermute | solution.py:32
  19.3 0.1 collective-permute-start.4
  20.0 0.0 collective-permute-done.1.chip_ref
  20.0 0.5 %collective-permute-done.4.passed_ref = f32[4,40,128]{2,1,0:T(8,128)S(1)} collective-permute-done((f32[4,40,128]{2,1,0:T(8,128)S(1)}, f32[4,40,128]{2,1,0:T(8,128)S(1)}, u32[]{:S(2)}, u32[]{:S(2)}) %collective-permute-start.4) | collective-permute-done | bytes 81952 | tf_op jit(solution)/shard_map/ppermute | solution.py:32
  20.6 0.0 copy-done
  20.6 0.0 copy-done.1
  20.6 0.8 %shard_map.108.vector_ref.first_ref.own_ref = f32[2,40,128]{2,1,0:T(8,128)S(1)} custom-call(s32[1,1]{1,0:T(1,128)} %bitcast.6.counts_ref, bf16[128,768]{1,0:T(8,128)(2,1)S(1)} %get-tuple-element.8.owned_ref, s32[6,128]{1,0:T(8,128)S(1)} %bitcast.8, s32[6,128]{1,0:T(8,128)S(1)} %bitcast.10, s32[6,128]{1,0:T(8,128)S(1)} %bitcast.12, f32[8,128]{1,0:T(8,128)S(1)} %copy-done.3, ...), custom_call_target="tpu_custom_call" | custom-call | flops 2457600 | bytes 2457600 | tf_op jit(solution)/shard_map/pallas_call | solution.py:410
  21.4 0.2 collective-permute-start.5
  21.6 1.1 %collective-permute-done.5.second_ref.core_ref = f32[2,40,128]{2,1,0:T(8,128)S(1)} collective-permute-done((f32[2,40,128]{2,1,0:T(8,128)S(1)}, f32[2,40,128]{2,1,0:T(8,128)S(1)}, u32[]{:S(2)}, u32[]{:S(2)}) %collective-permute-start.5) | collective-permute-done | bytes 40992 | tf_op jit(solution)/shard_map/ppermute | solution.py:32
  22.7 6.4 %collective-permute-start.7 = (f32[4,40,128]{2,1,0:T(8,128)S(1)}, f32[4,40,128]{2,1,0:T(8,128)S(1)}, u32[]{:S(2)}, u32[]{:S(2)}) collective-permute-start(f32[4,40,128]{2,1,0:T(8,128)S(1)} %shard_map.110), channel_id=1, source_target_pairs={{0,63},{1,2},{2,1},{3,4},{4,3},{5,6},{6,5},{7,8},{8,7},{9,10},{10,... | collective-permute-start | bytes 245768 | tf_op jit(solution)/shard_map/ppermute | solution.py:32
  29.1 0.0 collective-permute-start.8
  29.2 0.1 shard_map.109.rest_0_.element_ref
  29.3 0.5 %collective-permute-start.6 = (f32[4,40,128]{2,1,0:T(8,128)S(1)}, f32[4,40,128]{2,1,0:T(8,128)S(1)}, u32[]{:S(2)}, u32[]{:S(2)}) collective-permute-start(f32[4,40,128]{2,1,0:T(8,128)S(1)} %shard_map.110), channel_id=1, source_target_pairs={{0,128},{1,129},{2,130},{3,131},{4,132},{5,133},{6,134},{7,135},{8... | collective-permute-start | bytes 245768 | tf_op jit(solution)/shard_map/ppermute | solution.py:32
  29.8 3.0 %collective-permute-done.7.first_ref.far_ref = f32[4,40,128]{2,1,0:T(8,128)S(1)} collective-permute-done((f32[4,40,128]{2,1,0:T(8,128)S(1)}, f32[4,40,128]{2,1,0:T(8,128)S(1)}, u32[]{:S(2)}, u32[]{:S(2)}) %collective-permute-start.7) | collective-permute-done | bytes 81952 | tf_op jit(solution)/shard_map/ppermute | solution.py:32
  32.7 1.5 %collective-permute-done.8.second_ref.near_ref = f32[4,40,128]{2,1,0:T(8,128)S(1)} collective-permute-done((f32[4,40,128]{2,1,0:T(8,128)S(1)}, f32[4,40,128]{2,1,0:T(8,128)S(1)}, u32[]{:S(2)}, u32[]{:S(2)}) %collective-permute-start.8) | collective-permute-done | bytes 81952 | tf_op jit(solution)/shard_map/ppermute | solution.py:32
  34.2 0.4 %collective-permute-start.9 = (f32[4,40,128]{2,1,0:T(8,128)S(1)}, f32[4,40,128]{2,1,0:T(8,128)S(1)}, u32[]{:S(2)}, u32[]{:S(2)}) collective-permute-start(f32[4,40,128]{2,1,0:T(8,128)S(1)} %shard_map.111), channel_id=1, source_target_pairs={{0,64},{1,65},{2,66},{3,67},{4,68},{5,69},{6,70},{7,71},{8,72},{9,... | collective-permute-start | bytes 245768 | tf_op jit(solution)/shard_map/ppermute | solution.py:32
  34.7 0.0 collective-permute-done.6.chip_ref
  34.7 0.9 %collective-permute-done.9.passed_ref = f32[4,40,128]{2,1,0:T(8,128)S(1)} collective-permute-done((f32[4,40,128]{2,1,0:T(8,128)S(1)}, f32[4,40,128]{2,1,0:T(8,128)S(1)}, u32[]{:S(2)}, u32[]{:S(2)}) %collective-permute-start.9) | collective-permute-done | bytes 81952 | tf_op jit(solution)/shard_map/ppermute | solution.py:32
  35.6 1.5 %shard_map.112 = (f32[2,40,128]{2,1,0:T(8,128)}, f32[2,40,128]{2,1,0:T(8,128)}) custom-call(s32[1,1]{1,0:T(1,128)} %bitcast.7.counts_ref, bf16[128,768]{1,0:T(8,128)(2,1)S(1)} %get-tuple-element.8.owned_ref, s32[6,128]{1,0:T(8,128)S(1)} %bitcast.9, s32[6,128]{1,0:T(8,128)S(1)} %bitcast.11, s32[6,128]{1,0:T(8,128)S(1)} %bitcast.13, f32[8,128]{1,0:T(8,128)S(1)} %copy-done.3, ...), custom_call_target="tpu_custom_call" | custom-call | flops 2457600 | bytes 2457600 | tf_op jit(solution)/shard_map/pallas_call | solution.py:410
  (7 shorter events, 0.0 us)
Async XLA Ops:
  0.6 19.9 %copy-start = (s32[768]{0:T(1024)S(1)}, s32[768]{0:T(1024)}, u32[]{:S(2)}) copy-start(s32[768]{0:T(1024)} %param.15) | copy-start | bytes 9220
  0.6 19.9 %copy-start.1 = (s32[768]{0:T(1024)S(1)}, s32[768]{0:T(1024)}, u32[]{:S(2)}) copy-start(s32[768]{0:T(1024)} %param.16) | copy-start | bytes 9220
  0.7 19.9 %copy-start.2 = (s32[768]{0:T(1024)S(1)}, s32[768]{0:T(1024)}, u32[]{:S(2)}) copy-start(s32[768]{0:T(1024)} %param.17) | copy-start | bytes 9220
  0.7 19.9 %copy-start.3 = (f32[8,128]{1,0:T(8,128)S(1)}, f32[8,128]{1,0:T(8,128)}, u32[]{:S(2)}) copy-start(f32[8,128]{1,0:T(8,128)} %mass_ref.3) | copy-start | bytes 12292
  0.7 4.4 %collective-permute-start = (f32[2,40,128]{2,1,0:T(8,128)}, f32[2,40,128]{2,1,0:T(8,128)S(1)}, u32[]{:S(2)}, u32[]{:S(2)}) collective-permute-start(f32[2,40,128]{2,1,0:T(8,128)} %source_ref.1), channel_id=1, source_target_pairs={{0,64},{1,65},{2,66},{3,67},{4,68},{5,69},{6,70},{7,71},{8,72},{9,... | collective-permute-start | bytes 122888 | tf_op jit(solution)/shard_map/ppermute | solution.py:32
  5.1 12.6 %collective-permute-start.2 = (f32[4,40,128]{2,1,0:T(8,128)S(1)}, f32[4,40,128]{2,1,0:T(8,128)S(1)}, u32[]{:S(2)}, u32[]{:S(2)}) collective-permute-start(f32[4,40,128]{2,1,0:T(8,128)S(1)} %shard_map.105.both_ref), channel_id=1, source_target_pairs={{0,63},{1,2},{2,1},{3,4},{4,3},{5,6},{6,5},{7,8},{8,7},{9,10},{10,... | collective-permute-start | bytes 245768 | tf_op jit(solution)/shard_map/ppermute | solution.py:32
  14.2 5.1 %collective-permute-start.3 = (f32[4,40,128]{2,1,0:T(8,128)S(1)}, f32[4,40,128]{2,1,0:T(8,128)S(1)}, u32[]{:S(2)}, u32[]{:S(2)}) collective-permute-start(f32[4,40,128]{2,1,0:T(8,128)S(1)} %shard_map.105.both_ref), channel_id=1, source_target_pairs={{0,1},{1,0},{2,3},{3,2},{4,5},{5,4},{6,7},{7,6},{8,9},{9,8},{10,11... | collective-permute-start | bytes 245768 | tf_op jit(solution)/shard_map/ppermute | solution.py:32
  14.2 5.8 %collective-permute-start.1 = (f32[4,40,128]{2,1,0:T(8,128)S(1)}, f32[4,40,128]{2,1,0:T(8,128)S(1)}, u32[]{:S(2)}, u32[]{:S(2)}) collective-permute-start(f32[4,40,128]{2,1,0:T(8,128)S(1)} %shard_map.105.both_ref), channel_id=1, source_target_pairs={{0,128},{1,129},{2,130},{3,131},{4,132},{5,133},{6,134},{7,135},{8... | collective-permute-start | bytes 245768 | tf_op jit(solution)/shard_map/ppermute | solution.py:32
  14.6 0.7 %copy-start.4 = (s32[768]{0:T(1024)S(1)}, s32[768]{0:T(1024)}, u32[]{:S(2)}) copy-start(s32[768]{0:T(1024)} %param.14) | copy-start | bytes 9220
  19.3 1.3 %collective-permute-start.4 = (f32[4,40,128]{2,1,0:T(8,128)S(1)}, f32[4,40,128]{2,1,0:T(8,128)S(1)}, u32[]{:S(2)}, u32[]{:S(2)}) collective-permute-start(f32[4,40,128]{2,1,0:T(8,128)S(1)} %shard_map.107), channel_id=1, source_target_pairs={{0,64},{1,65},{2,66},{3,67},{4,68},{5,69},{6,70},{7,71},{8,72},{9,... | collective-permute-start | bytes 245768 | tf_op jit(solution)/shard_map/ppermute | solution.py:32
  21.4 1.3 %collective-permute-start.5 = (f32[2,40,128]{2,1,0:T(8,128)S(1)}, f32[2,40,128]{2,1,0:T(8,128)S(1)}, u32[]{:S(2)}, u32[]{:S(2)}) collective-permute-start(f32[2,40,128]{2,1,0:T(8,128)S(1)} %shard_map.108.vector_ref.first_ref.own_ref), channel_id=1, source_target_pairs={{0,64},{1,65},{2,66},{3,67},{4,68},{5,69},{6,70},{7,71},{8,72},{9,... | collective-permute-start | bytes 122888 | tf_op jit(solution)/shard_map/ppermute | solution.py:32
  22.7 10.0 %collective-permute-start.7 = (f32[4,40,128]{2,1,0:T(8,128)S(1)}, f32[4,40,128]{2,1,0:T(8,128)S(1)}, u32[]{:S(2)}, u32[]{:S(2)}) collective-permute-start(f32[4,40,128]{2,1,0:T(8,128)S(1)} %shard_map.110), channel_id=1, source_target_pairs={{0,63},{1,2},{2,1},{3,4},{4,3},{5,6},{6,5},{7,8},{8,7},{9,10},{10,... | collective-permute-start | bytes 245768 | tf_op jit(solution)/shard_map/ppermute | solution.py:32
  29.1 5.1 %collective-permute-start.8 = (f32[4,40,128]{2,1,0:T(8,128)S(1)}, f32[4,40,128]{2,1,0:T(8,128)S(1)}, u32[]{:S(2)}, u32[]{:S(2)}) collective-permute-start(f32[4,40,128]{2,1,0:T(8,128)S(1)} %shard_map.110), channel_id=1, source_target_pairs={{0,1},{1,0},{2,3},{3,2},{4,5},{5,4},{6,7},{7,6},{8,9},{9,8},{10,11... | collective-permute-start | bytes 245768 | tf_op jit(solution)/shard_map/ppermute | solution.py:32
  29.3 5.4 %collective-permute-start.6 = (f32[4,40,128]{2,1,0:T(8,128)S(1)}, f32[4,40,128]{2,1,0:T(8,128)S(1)}, u32[]{:S(2)}, u32[]{:S(2)}) collective-permute-start(f32[4,40,128]{2,1,0:T(8,128)S(1)} %shard_map.110), channel_id=1, source_target_pairs={{0,128},{1,129},{2,130},{3,131},{4,132},{5,133},{6,134},{7,135},{8... | collective-permute-start | bytes 245768 | tf_op jit(solution)/shard_map/ppermute | solution.py:32
  34.2 1.4 %collective-permute-start.9 = (f32[4,40,128]{2,1,0:T(8,128)S(1)}, f32[4,40,128]{2,1,0:T(8,128)S(1)}, u32[]{:S(2)}, u32[]{:S(2)}) collective-permute-start(f32[4,40,128]{2,1,0:T(8,128)S(1)} %shard_map.111), channel_id=1, source_target_pairs={{0,64},{1,65},{2,66},{3,67},{4,68},{5,69},{6,70},{7,71},{8,72},{9,... | collective-permute-start | bytes 245768 | tf_op jit(solution)/shard_map/ppermute | solution.py:32

commit v5 on v4

--- a/solution.py
+++ b/solution.py
@@ -56,7 +56,7 @@
     out_ref = rest[-1]
     insts = out_ref.shape[0] // 2
     out_ref[:insts] = first_ref[base : base + insts]
-    out_ref[insts:] = second_ref[base : base + insts]
+    out_ref[insts:] = second_ref[...]
 
 
 def join(first, second, base, *after):
@@ -72,6 +72,24 @@
         ),
         compiler_params=pltpu.CompilerParams(vmem_limit_bytes=2**20),
     )(first, second, *after)
+
+
+def second_half_kernel(both_ref, out_ref):
+    out_ref[...] = both_ref[out_ref.shape[0] :]
+
+
+def second_half(both):
+    insts = both.shape[0] // 2
+    return pl.pallas_call(
+        second_half_kernel,
+        out_shape=jax.ShapeDtypeStruct((insts,) + both.shape[1:], jnp.float32),
+        in_specs=[pl.BlockSpec(memory_space=pltpu.VMEM)],
+        out_specs=pl.BlockSpec(memory_space=pltpu.VMEM),
+        cost_estimate=pl.CostEstimate(
+            flops=0, bytes_accessed=4 * both.size, transcendentals=0
+        ),
+        compiler_params=pltpu.CompilerParams(vmem_limit_bytes=2**20),
+    )(both)
 
 
 def sublanes():
@@ -153,6 +171,8 @@
     owned_ref,
     product_ref,
     held_ref,
+    held_owner_ref,
+    owner_sem,
     element_sem,
     face_sems,
 ):
@@ -170,10 +190,13 @@
     element_copy = pltpu.make_async_copy(element_ref, element_out_ref, element_sem)
     element_copy.start()
 
+    owner_copy = pltpu.make_async_copy(owner_ref, held_owner_ref, owner_sem)
+    owner_copy.start()
+    owner_copy.wait()
     slot = lax.broadcasted_iota(jnp.int32, (owned_ref.shape[0], 128), 0)
     owned = jnp.concatenate(
         [
-            jnp.broadcast_to(owner_ref[tile : tile + 1, :], slot.shape) == slot
+            jnp.broadcast_to(held_owner_ref[tile : tile + 1, :], slot.shape) == slot
             for tile in range(lane_tiles)
         ],
         axis=1,
@@ -208,10 +231,12 @@
             pltpu.VMEM((elements, owner.size), jnp.bfloat16),
             pltpu.VMEM((insts, unknowns, elements), jnp.float32),
         ),
-        in_specs=[hbm, hbm, vmem, vmem],
+        in_specs=[hbm, hbm, vmem, hbm],
         out_specs=(vmem, vmem, vmem, vmem),
         scratch_shapes=[
             pltpu.VMEM(face_blocks.shape, jnp.float32),
+            pltpu.VMEM(owner.shape, jnp.int32),
+            pltpu.SemaphoreType.DMA,
             pltpu.SemaphoreType.DMA,
             pltpu.SemaphoreType.DMA((CHUNKS,)),
         ],
@@ -223,7 +248,7 @@
         pltpu.with_memory_space_constraint(element_blocks, pltpu.HBM),
         pltpu.with_memory_space_constraint(face_blocks, pltpu.HBM),
         both,
-        owner,
+        pltpu.with_memory_space_constraint(owner, pltpu.HBM),
     )
 
 
@@ -445,7 +470,7 @@
         far = send(both, to_far)
         near = send(both, to_near)
         chip = send(both, to_chip)
-        passed = send(join(far, near, both.shape[0] // 2, *after), to_core)
+        passed = send(join(far, second_half(near), both.shape[0] // 2, *after), to_core)
         return chip, far, near, passed
 
     core = send(state, to_core)

time: 37.2 us -> 36.9 us (level)
  starting transfers between devices: 20.5 us -> 25.1 us
  waiting for transfers between devices: 8.81 us -> 4.54 us
  local copies, waits for them, and re-layouts: 0.7 us -> 0.02 us
    ppermute x10, starting transfers between devices: 20.5 us -> 25.1 us  [send(): return lax.ppermute(value, ('inst', 'dom'), joint(rule))]
    ppermute x10, waiting for transfers between devices: 8.81 us -> 4.54 us  [send(): return lax.ppermute(value, ('inst', 'dom'), joint(rule))]
    unnamed x10 -> x8, local copies, waits for them, and re-layouts: 0.7 us -> 0.02 us
  transfers between devices with their start and end apart: 10 -> 10, of which waited for: 7 -> 6; matrix products, arithmetic and copies ran while one was open for 0% -> 0% of each run, Pallas kernels for 9% -> 9%
where the time goes in v5:
time: 36.9 us; the launch traced here: 36.7 us
  starting transfers between devices  25.1 us (68%)
  Pallas kernels  5.65 us (15%)
  waiting for transfers between devices  4.54 us (12%)
  between operations  1.38 us (4%)
    ppermute x10, starting transfers between devices, send(): return lax.ppermute(value, ('inst', 'dom'), joint(rule))  25.1 us
    ppermute x10, waiting for transfers between devices, send(): return lax.ppermute(value, ('inst', 'dom'), joint(rule))  4.54 us
    pallas_call x1, Pallas kernels, stage(): pl.pallas_call(stage_kernel, out_shape=(pltpu.VMEM(element_blocks.shape,...  2.38 us
    pallas_call x2, Pallas kernels, jacobian_rows(): pl.pallas_call(functools.partial(jacobian_kernel, instances, part_total,...  2.31 us
    pallas_call x1, Pallas kernels, fetch(): pl.pallas_call(fetch_kernel, out_shape=pltpu.VMEM(value.shape, jnp.float3...  0.79 us
  transfers between devices with their start and end apart: 10, of which 6 were waited for; matrix products, arithmetic and copies ran while one was open for 0% of the time, Pallas kernels for 9%

profile of v5, /device:TPU:1, one launch (start us, length us, event | category | flops | bytes accessed | tf_op | source)
XLA Modules:
  0.0 36.7 jit_solution(12799003831512302583)
XLA Ops:
  0.6 0.0 copy-start
  0.6 0.0 copy-start.1
  0.7 0.0 copy-start.2
  0.7 0.0 copy-start.3
  0.7 3.3 %collective-permute-start = (f32[2,40,128]{2,1,0:T(8,128)}, f32[2,40,128]{2,1,0:T(8,128)S(1)}, u32[]{:S(2)}, u32[]{:S(2)}) collective-permute-start(f32[2,40,128]{2,1,0:T(8,128)} %source_ref.1), channel_id=1, source_target_pairs={{0,64},{1,65},{2,66},{3,67},{4,68},{5,69},{6,70},{7,71},{8,72},{9,... | collective-permute-start | bytes 122888 | tf_op jit(solution)/shard_map/ppermute | solution.py:32
  4.0 0.8 %shard_map.104.first_ref.own_ref = f32[2,40,128]{2,1,0:T(8,128)S(1)} custom-call(f32[2,40,128]{2,1,0:T(8,128)} %source_ref.1), custom_call_target="tpu_custom_call" | custom-call | bytes 81920 | tf_op jit(solution)/shard_map/pallas_call | solution.py:151
  4.8 0.3 collective-permute-done.second_ref.core_ref
  5.1 1.3 %collective-permute-start.3 = (f32[4,40,128]{2,1,0:T(8,128)S(1)}, f32[4,40,128]{2,1,0:T(8,128)S(1)}, u32[]{:S(2)}, u32[]{:S(2)}) collective-permute-start(f32[4,40,128]{2,1,0:T(8,128)S(1)} %shard_map.105.both_ref), channel_id=1, source_target_pairs={{0,1},{1,0},{2,3},{3,2},{4,5},{5,4},{6,7},{7,6},{8,9},{9,8},{10,11... | collective-permute-start | bytes 245768 | tf_op jit(solution)/shard_map/ppermute | solution.py:32
  6.3 9.0 %collective-permute-start.2 = (f32[4,40,128]{2,1,0:T(8,128)S(1)}, f32[4,40,128]{2,1,0:T(8,128)S(1)}, u32[]{:S(2)}, u32[]{:S(2)}) collective-permute-start(f32[4,40,128]{2,1,0:T(8,128)S(1)} %shard_map.105.both_ref), channel_id=1, source_target_pairs={{0,63},{1,2},{2,1},{3,4},{4,3},{5,6},{6,5},{7,8},{8,7},{9,10},{10,... | collective-permute-start | bytes 245768 | tf_op jit(solution)/shard_map/ppermute | solution.py:32
  15.4 0.4 %collective-permute-start.1 = (f32[4,40,128]{2,1,0:T(8,128)S(1)}, f32[4,40,128]{2,1,0:T(8,128)S(1)}, u32[]{:S(2)}, u32[]{:S(2)}) collective-permute-start(f32[4,40,128]{2,1,0:T(8,128)S(1)} %shard_map.105.both_ref), channel_id=1, source_target_pairs={{0,128},{1,129},{2,130},{3,131},{4,132},{5,133},{6,134},{7,135},{8... | collective-permute-start | bytes 245768 | tf_op jit(solution)/shard_map/ppermute | solution.py:32
  15.8 2.4 %shard_map.106 = (f32[2,40,40,128]{3,2,1,0:T(8,128)S(1)}, f32[4800,128]{1,0:T(8,128)S(1)}, bf16[128,768]{1,0:T(8,128)(2,1)S(1)}, f32[2,40,128]{2,1,0:T(8,128)S(1)}) custom-call(f32[2,40,40,128]{3,2,1,0:T(8,128)} %element_ref.1, f32[20,20,2,768]{3,2,1,0:T(2,128)} %bitcast.14, f32[4,40,128]{2,1,0:T(8,128)S(1)} %shard_map.105.both_ref, s32[6,128]{1,0:T(8,128)} %bitcast.15), custom_call_target="tpu_custom_call" | custom-call | bytes 1638400 | tf_op jit(solution)/shard_map/pallas_call | solution.py:226
  18.2 0.0 collective-permute-done.3.both_ref.near_ref
  18.2 0.5 %collective-permute-done.2.first_ref.far_ref = f32[4,40,128]{2,1,0:T(8,128)S(1)} collective-permute-done((f32[4,40,128]{2,1,0:T(8,128)S(1)}, f32[4,40,128]{2,1,0:T(8,128)S(1)}, u32[]{:S(2)}, u32[]{:S(2)}) %collective-permute-start.2) | collective-permute-done | bytes 81952 | tf_op jit(solution)/shard_map/ppermute | solution.py:32
  18.7 0.4 %collective-permute-start.4 = (f32[4,40,128]{2,1,0:T(8,128)S(1)}, f32[4,40,128]{2,1,0:T(8,128)S(1)}, u32[]{:S(2)}, u32[]{:S(2)}) collective-permute-start(f32[4,40,128]{2,1,0:T(8,128)S(1)} %shard_map.108), channel_id=1, source_target_pairs={{0,64},{1,65},{2,66},{3,67},{4,68},{5,69},{6,70},{7,71},{8,72},{9,... | collective-permute-start | bytes 245768 | tf_op jit(solution)/shard_map/ppermute | solution.py:32
  19.8 0.0 collective-permute-done.1.chip_ref
  19.8 0.3 collective-permute-done.4.passed_ref
  20.0 0.0 copy-done
  20.0 0.0 copy-done.1
  20.0 0.0 copy-done.3
  20.0 0.8 %shard_map.109.vector_ref.first_ref.own_ref = f32[2,40,128]{2,1,0:T(8,128)S(1)} custom-call(s32[1,1]{1,0:T(1,128)} %bitcast.6.counts_ref, bf16[128,768]{1,0:T(8,128)(2,1)S(1)} %get-tuple-element.8.owned_ref, s32[6,128]{1,0:T(8,128)S(1)} %bitcast.8, s32[6,128]{1,0:T(8,128)S(1)} %bitcast.10, s32[6,128]{1,0:T(8,128)S(1)} %bitcast.12, f32[8,128]{1,0:T(8,128)S(1)} %copy-done.3, ...), custom_call_target="tpu_custom_call" | custom-call | flops 2457600 | bytes 2457600 | tf_op jit(solution)/shard_map/pallas_call | solution.py:435
  20.9 0.4 %collective-permute-start.5 = (f32[2,40,128]{2,1,0:T(8,128)S(1)}, f32[2,40,128]{2,1,0:T(8,128)S(1)}, u32[]{:S(2)}, u32[]{:S(2)}) collective-permute-start(f32[2,40,128]{2,1,0:T(8,128)S(1)} %shard_map.109.vector_ref.first_ref.own_ref), channel_id=1, source_target_pairs={{0,64},{1,65},{2,66},{3,67},{4,68},{5,69},{6,70},{7,71},{8,72},{9,... | collective-permute-start | bytes 122888 | tf_op jit(solution)/shard_map/ppermute | solution.py:32
  21.3 0.9 %collective-permute-done.5.second_ref.core_ref = f32[2,40,128]{2,1,0:T(8,128)S(1)} collective-permute-done((f32[2,40,128]{2,1,0:T(8,128)S(1)}, f32[2,40,128]{2,1,0:T(8,128)S(1)}, u32[]{:S(2)}, u32[]{:S(2)}) %collective-permute-start.5) | collective-permute-done | bytes 40992 | tf_op jit(solution)/shard_map/ppermute | solution.py:32
  22.2 0.0 collective-permute-start.8
  22.2 8.2 %collective-permute-start.7 = (f32[4,40,128]{2,1,0:T(8,128)S(1)}, f32[4,40,128]{2,1,0:T(8,128)S(1)}, u32[]{:S(2)}, u32[]{:S(2)}) collective-permute-start(f32[4,40,128]{2,1,0:T(8,128)S(1)} %shard_map.111), channel_id=1, source_target_pairs={{0,63},{1,2},{2,1},{3,4},{4,3},{5,6},{6,5},{7,8},{8,7},{9,10},{10,... | collective-permute-start | bytes 245768 | tf_op jit(solution)/shard_map/ppermute | solution.py:32
  30.4 0.1 shard_map.110.rest_0_.element_ref
  30.5 0.5 %collective-permute-start.6 = (f32[4,40,128]{2,1,0:T(8,128)S(1)}, f32[4,40,128]{2,1,0:T(8,128)S(1)}, u32[]{:S(2)}, u32[]{:S(2)}) collective-permute-start(f32[4,40,128]{2,1,0:T(8,128)S(1)} %shard_map.111), channel_id=1, source_target_pairs={{0,128},{1,129},{2,130},{3,131},{4,132},{5,133},{6,134},{7,135},{8... | collective-permute-start | bytes 245768 | tf_op jit(solution)/shard_map/ppermute | solution.py:32
  31.0 0.0 collective-permute-done.8.both_ref.near_ref
  31.0 1.7 %collective-permute-done.7.first_ref.far_ref = f32[4,40,128]{2,1,0:T(8,128)S(1)} collective-permute-done((f32[4,40,128]{2,1,0:T(8,128)S(1)}, f32[4,40,128]{2,1,0:T(8,128)S(1)}, u32[]{:S(2)}, u32[]{:S(2)}) %collective-permute-start.7) | collective-permute-done | bytes 81952 | tf_op jit(solution)/shard_map/ppermute | solution.py:32
  32.7 1.6 %collective-permute-start.9 = (f32[4,40,128]{2,1,0:T(8,128)S(1)}, f32[4,40,128]{2,1,0:T(8,128)S(1)}, u32[]{:S(2)}, u32[]{:S(2)}) collective-permute-start(f32[4,40,128]{2,1,0:T(8,128)S(1)} %shard_map.113), channel_id=1, source_target_pairs={{0,64},{1,65},{2,66},{3,67},{4,68},{5,69},{6,70},{7,71},{8,72},{9,... | collective-permute-start | bytes 245768 | tf_op jit(solution)/shard_map/ppermute | solution.py:32
  34.3 0.0 collective-permute-done.6.chip_ref
  34.3 0.9 %collective-permute-done.9.passed_ref = f32[4,40,128]{2,1,0:T(8,128)S(1)} collective-permute-done((f32[4,40,128]{2,1,0:T(8,128)S(1)}, f32[4,40,128]{2,1,0:T(8,128)S(1)}, u32[]{:S(2)}, u32[]{:S(2)}) %collective-permute-start.9) | collective-permute-done | bytes 81952 | tf_op jit(solution)/shard_map/ppermute | solution.py:32
  35.2 1.5 %shard_map.114 = (f32[2,40,128]{2,1,0:T(8,128)}, f32[2,40,128]{2,1,0:T(8,128)}) custom-call(s32[1,1]{1,0:T(1,128)} %bitcast.7.counts_ref, bf16[128,768]{1,0:T(8,128)(2,1)S(1)} %get-tuple-element.8.owned_ref, s32[6,128]{1,0:T(8,128)S(1)} %bitcast.9, s32[6,128]{1,0:T(8,128)S(1)} %bitcast.11, s32[6,128]{1,0:T(8,128)S(1)} %bitcast.13, f32[8,128]{1,0:T(8,128)S(1)} %copy-done.3, ...), custom_call_target="tpu_custom_call" | custom-call | flops 2457600 | bytes 2457600 | tf_op jit(solution)/shard_map/pallas_call | solution.py:435
  (7 shorter events, 0.0 us)
Async XLA Ops:
  0.6 19.4 %copy-start = (s32[768]{0:T(1024)S(1)}, s32[768]{0:T(1024)}, u32[]{:S(2)}) copy-start(s32[768]{0:T(1024)} %param.15) | copy-start | bytes 9220
  0.6 19.4 %copy-start.1 = (s32[768]{0:T(1024)S(1)}, s32[768]{0:T(1024)}, u32[]{:S(2)}) copy-start(s32[768]{0:T(1024)} %param.16) | copy-start | bytes 9220
  0.7 19.4 %copy-start.2 = (s32[768]{0:T(1024)S(1)}, s32[768]{0:T(1024)}, u32[]{:S(2)}) copy-start(s32[768]{0:T(1024)} %param.17) | copy-start | bytes 9220
  0.7 19.4 %copy-start.3 = (f32[8,128]{1,0:T(8,128)S(1)}, f32[8,128]{1,0:T(8,128)}, u32[]{:S(2)}) copy-start(f32[8,128]{1,0:T(8,128)} %mass_ref.3) | copy-start | bytes 12292
  0.7 4.4 %collective-permute-start = (f32[2,40,128]{2,1,0:T(8,128)}, f32[2,40,128]{2,1,0:T(8,128)S(1)}, u32[]{:S(2)}, u32[]{:S(2)}) collective-permute-start(f32[2,40,128]{2,1,0:T(8,128)} %source_ref.1), channel_id=1, source_target_pairs={{0,64},{1,65},{2,66},{3,67},{4,68},{5,69},{6,70},{7,71},{8,72},{9,... | collective-permute-start | bytes 122888 | tf_op jit(solution)/shard_map/ppermute | solution.py:32
  5.1 13.1 %collective-permute-start.3 = (f32[4,40,128]{2,1,0:T(8,128)S(1)}, f32[4,40,128]{2,1,0:T(8,128)S(1)}, u32[]{:S(2)}, u32[]{:S(2)}) collective-permute-start(f32[4,40,128]{2,1,0:T(8,128)S(1)} %shard_map.105.both_ref), channel_id=1, source_target_pairs={{0,1},{1,0},{2,3},{3,2},{4,5},{5,4},{6,7},{7,6},{8,9},{9,8},{10,11... | collective-permute-start | bytes 245768 | tf_op jit(solution)/shard_map/ppermute | solution.py:32
  6.3 12.3 %collective-permute-start.2 = (f32[4,40,128]{2,1,0:T(8,128)S(1)}, f32[4,40,128]{2,1,0:T(8,128)S(1)}, u32[]{:S(2)}, u32[]{:S(2)}) collective-permute-start(f32[4,40,128]{2,1,0:T(8,128)S(1)} %shard_map.105.both_ref), channel_id=1, source_target_pairs={{0,63},{1,2},{2,1},{3,4},{4,3},{5,6},{6,5},{7,8},{8,7},{9,10},{10,... | collective-permute-start | bytes 245768 | tf_op jit(solution)/shard_map/ppermute | solution.py:32
  15.4 4.4 %collective-permute-start.1 = (f32[4,40,128]{2,1,0:T(8,128)S(1)}, f32[4,40,128]{2,1,0:T(8,128)S(1)}, u32[]{:S(2)}, u32[]{:S(2)}) collective-permute-start(f32[4,40,128]{2,1,0:T(8,128)S(1)} %shard_map.105.both_ref), channel_id=1, source_target_pairs={{0,128},{1,129},{2,130},{3,131},{4,132},{5,133},{6,134},{7,135},{8... | collective-permute-start | bytes 245768 | tf_op jit(solution)/shard_map/ppermute | solution.py:32
  18.7 1.3 %collective-permute-start.4 = (f32[4,40,128]{2,1,0:T(8,128)S(1)}, f32[4,40,128]{2,1,0:T(8,128)S(1)}, u32[]{:S(2)}, u32[]{:S(2)}) collective-permute-start(f32[4,40,128]{2,1,0:T(8,128)S(1)} %shard_map.108), channel_id=1, source_target_pairs={{0,64},{1,65},{2,66},{3,67},{4,68},{5,69},{6,70},{7,71},{8,72},{9,... | collective-permute-start | bytes 245768 | tf_op jit(solution)/shard_map/ppermute | solution.py:32
  20.9 1.3 %collective-permute-start.5 = (f32[2,40,128]{2,1,0:T(8,128)S(1)}, f32[2,40,128]{2,1,0:T(8,128)S(1)}, u32[]{:S(2)}, u32[]{:S(2)}) collective-permute-start(f32[2,40,128]{2,1,0:T(8,128)S(1)} %shard_map.109.vector_ref.first_ref.own_ref), channel_id=1, source_target_pairs={{0,64},{1,65},{2,66},{3,67},{4,68},{5,69},{6,70},{7,71},{8,72},{9,... | collective-permute-start | bytes 122888 | tf_op jit(solution)/shard_map/ppermute | solution.py:32
  22.2 8.8 %collective-permute-start.8 = (f32[4,40,128]{2,1,0:T(8,128)S(1)}, f32[4,40,128]{2,1,0:T(8,128)S(1)}, u32[]{:S(2)}, u32[]{:S(2)}) collective-permute-start(f32[4,40,128]{2,1,0:T(8,128)S(1)} %shard_map.111), channel_id=1, source_target_pairs={{0,1},{1,0},{2,3},{3,2},{4,5},{5,4},{6,7},{7,6},{8,9},{9,8},{10,11... | collective-permute-start | bytes 245768 | tf_op jit(solution)/shard_map/ppermute | solution.py:32
  22.2 10.5 %collective-permute-start.7 = (f32[4,40,128]{2,1,0:T(8,128)S(1)}, f32[4,40,128]{2,1,0:T(8,128)S(1)}, u32[]{:S(2)}, u32[]{:S(2)}) collective-permute-start(f32[4,40,128]{2,1,0:T(8,128)S(1)} %shard_map.111), channel_id=1, source_target_pairs={{0,63},{1,2},{2,1},{3,4},{4,3},{5,6},{6,5},{7,8},{8,7},{9,10},{10,... | collective-permute-start | bytes 245768 | tf_op jit(solution)/shard_map/ppermute | solution.py:32
  30.5 3.8 %collective-permute-start.6 = (f32[4,40,128]{2,1,0:T(8,128)S(1)}, f32[4,40,128]{2,1,0:T(8,128)S(1)}, u32[]{:S(2)}, u32[]{:S(2)}) collective-permute-start(f32[4,40,128]{2,1,0:T(8,128)S(1)} %shard_map.111), channel_id=1, source_target_pairs={{0,128},{1,129},{2,130},{3,131},{4,132},{5,133},{6,134},{7,135},{8... | collective-permute-start | bytes 245768 | tf_op jit(solution)/shard_map/ppermute | solution.py:32
  32.7 2.5 %collective-permute-start.9 = (f32[4,40,128]{2,1,0:T(8,128)S(1)}, f32[4,40,128]{2,1,0:T(8,128)S(1)}, u32[]{:S(2)}, u32[]{:S(2)}) collective-permute-start(f32[4,40,128]{2,1,0:T(8,128)S(1)} %shard_map.113), channel_id=1, source_target_pairs={{0,64},{1,65},{2,66},{3,67},{4,68},{5,69},{6,70},{7,71},{8,72},{9,... | collective-permute-start | bytes 245768 | tf_op jit(solution)/shard_map/ppermute | solution.py:32

commit v6 on v5

--- a/solution.py
+++ b/solution.py
@@ -301,6 +301,8 @@
     if not keep:
         save = pltpu.make_async_copy(own_ref, rest[0], rest[4])
         save.start()
+        result_ref, out_ref = out_ref, rest[5]
+        copies = []
     my_part = lax.axis_index("dom")
     on_first = (lax.axis_index("inst") & 1) == 0
     step_one = jnp.where((my_part & 1) == 0, 1, -1)
@@ -418,8 +420,15 @@
             base = (t * variables + a) * 8
             value = element_ref[t, rows, :] + landed[base : base + 8, :] + mass * summed
             out_ref[t, rows, :] = jnp.where(live, value, 0.0)
+        if not keep:
+            copies.append(
+                pltpu.make_async_copy(out_ref.at[t], result_ref.at[t], rest[6].at[t])
+            )
+            copies[-1].start()
     if not keep:
         save.wait()
+        for copy in copies:
+            copy.wait()
 
 
 def jacobian_rows(
@@ -436,13 +445,21 @@
         functools.partial(jacobian_kernel, instances, part_total, keep),
         out_shape=pltpu.VMEM(own.shape, jnp.float32) if keep else (result, result),
         in_specs=[vmem] * (9 + len(fields)),
-        out_specs=vmem if keep else (vmem, pl.BlockSpec(memory_space=pl.ANY)),
+        out_specs=vmem if keep else (pl.BlockSpec(memory_space=pl.ANY),) * 2,
         scratch_shapes=[
             pltpu.VMEM((width * stride, 128), jnp.float32),
             pltpu.VMEM(((width + 4) * 2 * stride, 128), jnp.float32),
             pltpu.VMEM((insts * unknowns, side.shape[0] * 128), jnp.float32),
         ]
-        + ([] if keep else [pltpu.SemaphoreType.DMA]),
+        + (
+            []
+            if keep
+            else [
+                pltpu.SemaphoreType.DMA,
+                pltpu.VMEM(own.shape, jnp.float32),
+                pltpu.SemaphoreType.DMA((insts,)),
+            ]
+        ),
         cost_estimate=pl.CostEstimate(
             flops=4 * blocks.size, bytes_accessed=4 * blocks.size, transcendentals=0
         ),

time: 36.9 us -> 36.9 us (level)
  no operation moved by 1% of the time
where the time goes in v6:
time: 36.9 us; the launch traced here: 36.7 us
  starting transfers between devices  25.1 us (68%)
  Pallas kernels  5.65 us (15%)
  waiting for transfers between devices  4.54 us (12%)
  between operations  1.38 us (4%)
    ppermute x10, starting transfers between devices, send(): return lax.ppermute(value, ('inst', 'dom'), joint(rule))  25.1 us
    ppermute x10, waiting for transfers between devices, send(): return lax.ppermute(value, ('inst', 'dom'), joint(rule))  4.54 us
    pallas_call x1, Pallas kernels, stage(): pl.pallas_call(stage_kernel, out_shape=(pltpu.VMEM(element_blocks.shape,...  2.38 us
    pallas_call x2, Pallas kernels, jacobian_rows(): pl.pallas_call(functools.partial(jacobian_kernel, instances, part_total,...  2.3 us
    pallas_call x1, Pallas kernels, fetch(): pl.pallas_call(fetch_kernel, out_shape=pltpu.VMEM(value.shape, jnp.float3...  0.79 us
  transfers between devices with their start and end apart: 10, of which 6 were waited for; matrix products, arithmetic and copies ran while one was open for 0% of the time, Pallas kernels for 9%

profile of v6, /device:TPU:1, one launch (start us, length us, event | category | flops | bytes accessed | tf_op | source)
XLA Modules:
  0.0 36.7 jit_solution(17565126837451801934)
XLA Ops:
  0.6 0.0 copy-start
  0.6 0.0 copy-start.1
  0.7 0.0 copy-start.2
  0.7 0.0 copy-start.3
  0.7 3.3 %collective-permute-start = (f32[2,40,128]{2,1,0:T(8,128)}, f32[2,40,128]{2,1,0:T(8,128)S(1)}, u32[]{:S(2)}, u32[]{:S(2)}) collective-permute-start(f32[2,40,128]{2,1,0:T(8,128)} %source_ref.1), channel_id=1, source_target_pairs={{0,64},{1,65},{2,66},{3,67},{4,68},{5,69},{6,70},{7,71},{8,72},{9,... | collective-permute-start | bytes 122888 | tf_op jit(solution)/shard_map/ppermute | solution.py:32
  4.0 0.8 %shard_map.104.first_ref.own_ref = f32[2,40,128]{2,1,0:T(8,128)S(1)} custom-call(f32[2,40,128]{2,1,0:T(8,128)} %source_ref.1), custom_call_target="tpu_custom_call" | custom-call | bytes 81920 | tf_op jit(solution)/shard_map/pallas_call | solution.py:151
  4.8 0.3 collective-permute-done.second_ref.core_ref
  5.1 1.3 %collective-permute-start.3 = (f32[4,40,128]{2,1,0:T(8,128)S(1)}, f32[4,40,128]{2,1,0:T(8,128)S(1)}, u32[]{:S(2)}, u32[]{:S(2)}) collective-permute-start(f32[4,40,128]{2,1,0:T(8,128)S(1)} %shard_map.105.both_ref), channel_id=1, source_target_pairs={{0,1},{1,0},{2,3},{3,2},{4,5},{5,4},{6,7},{7,6},{8,9},{9,8},{10,11... | collective-permute-start | bytes 245768 | tf_op jit(solution)/shard_map/ppermute | solution.py:32
  6.3 9.0 %collective-permute-start.2 = (f32[4,40,128]{2,1,0:T(8,128)S(1)}, f32[4,40,128]{2,1,0:T(8,128)S(1)}, u32[]{:S(2)}, u32[]{:S(2)}) collective-permute-start(f32[4,40,128]{2,1,0:T(8,128)S(1)} %shard_map.105.both_ref), channel_id=1, source_target_pairs={{0,63},{1,2},{2,1},{3,4},{4,3},{5,6},{6,5},{7,8},{8,7},{9,10},{10,... | collective-permute-start | bytes 245768 | tf_op jit(solution)/shard_map/ppermute | solution.py:32
  15.4 0.4 %collective-permute-start.1 = (f32[4,40,128]{2,1,0:T(8,128)S(1)}, f32[4,40,128]{2,1,0:T(8,128)S(1)}, u32[]{:S(2)}, u32[]{:S(2)}) collective-permute-start(f32[4,40,128]{2,1,0:T(8,128)S(1)} %shard_map.105.both_ref), channel_id=1, source_target_pairs={{0,128},{1,129},{2,130},{3,131},{4,132},{5,133},{6,134},{7,135},{8... | collective-permute-start | bytes 245768 | tf_op jit(solution)/shard_map/ppermute | solution.py:32
  15.8 2.4 %shard_map.106 = (f32[2,40,40,128]{3,2,1,0:T(8,128)S(1)}, f32[4800,128]{1,0:T(8,128)S(1)}, bf16[128,768]{1,0:T(8,128)(2,1)S(1)}, f32[2,40,128]{2,1,0:T(8,128)S(1)}) custom-call(f32[2,40,40,128]{3,2,1,0:T(8,128)} %element_ref.1, f32[20,20,2,768]{3,2,1,0:T(2,128)} %bitcast.14, f32[4,40,128]{2,1,0:T(8,128)S(1)} %shard_map.105.both_ref, s32[6,128]{1,0:T(8,128)} %bitcast.15), custom_call_target="tpu_custom_call" | custom-call | bytes 1638400 | tf_op jit(solution)/shard_map/pallas_call | solution.py:226
  18.2 0.0 collective-permute-done.3.both_ref.near_ref
  18.2 0.5 %collective-permute-done.2.first_ref.far_ref = f32[4,40,128]{2,1,0:T(8,128)S(1)} collective-permute-done((f32[4,40,128]{2,1,0:T(8,128)S(1)}, f32[4,40,128]{2,1,0:T(8,128)S(1)}, u32[]{:S(2)}, u32[]{:S(2)}) %collective-permute-start.2) | collective-permute-done | bytes 81952 | tf_op jit(solution)/shard_map/ppermute | solution.py:32
  18.7 0.4 %collective-permute-start.4 = (f32[4,40,128]{2,1,0:T(8,128)S(1)}, f32[4,40,128]{2,1,0:T(8,128)S(1)}, u32[]{:S(2)}, u32[]{:S(2)}) collective-permute-start(f32[4,40,128]{2,1,0:T(8,128)S(1)} %shard_map.108), channel_id=1, source_target_pairs={{0,64},{1,65},{2,66},{3,67},{4,68},{5,69},{6,70},{7,71},{8,72},{9,... | collective-permute-start | bytes 245768 | tf_op jit(solution)/shard_map/ppermute | solution.py:32
  19.8 0.0 collective-permute-done.1.chip_ref
  19.8 0.3 collective-permute-done.4.passed_ref
  20.0 0.0 copy-done
  20.0 0.0 copy-done.1
  20.0 0.0 copy-done.3
  20.0 0.8 %shard_map.109.vector_ref.first_ref.own_ref = f32[2,40,128]{2,1,0:T(8,128)S(1)} custom-call(s32[1,1]{1,0:T(1,128)} %bitcast.6.counts_ref, bf16[128,768]{1,0:T(8,128)(2,1)S(1)} %get-tuple-element.8.owned_ref, s32[6,128]{1,0:T(8,128)S(1)} %bitcast.8, s32[6,128]{1,0:T(8,128)S(1)} %bitcast.10, s32[6,128]{1,0:T(8,128)S(1)} %bitcast.12, f32[8,128]{1,0:T(8,128)S(1)} %copy-done.3, ...), custom_call_target="tpu_custom_call" | custom-call | flops 2457600 | bytes 2457600 | tf_op jit(solution)/shard_map/pallas_call | solution.py:444
  20.9 0.4 %collective-permute-start.5 = (f32[2,40,128]{2,1,0:T(8,128)S(1)}, f32[2,40,128]{2,1,0:T(8,128)S(1)}, u32[]{:S(2)}, u32[]{:S(2)}) collective-permute-start(f32[2,40,128]{2,1,0:T(8,128)S(1)} %shard_map.109.vector_ref.first_ref.own_ref), channel_id=1, source_target_pairs={{0,64},{1,65},{2,66},{3,67},{4,68},{5,69},{6,70},{7,71},{8,72},{9,... | collective-permute-start | bytes 122888 | tf_op jit(solution)/shard_map/ppermute | solution.py:32
  21.3 0.9 %collective-permute-done.5.second_ref.core_ref = f32[2,40,128]{2,1,0:T(8,128)S(1)} collective-permute-done((f32[2,40,128]{2,1,0:T(8,128)S(1)}, f32[2,40,128]{2,1,0:T(8,128)S(1)}, u32[]{:S(2)}, u32[]{:S(2)}) %collective-permute-start.5) | collective-permute-done | bytes 40992 | tf_op jit(solution)/shard_map/ppermute | solution.py:32
  22.2 0.0 collective-permute-start.8
  22.2 8.2 %collective-permute-start.7 = (f32[4,40,128]{2,1,0:T(8,128)S(1)}, f32[4,40,128]{2,1,0:T(8,128)S(1)}, u32[]{:S(2)}, u32[]{:S(2)}) collective-permute-start(f32[4,40,128]{2,1,0:T(8,128)S(1)} %shard_map.111), channel_id=1, source_target_pairs={{0,63},{1,2},{2,1},{3,4},{4,3},{5,6},{6,5},{7,8},{8,7},{9,10},{10,... | collective-permute-start | bytes 245768 | tf_op jit(solution)/shard_map/ppermute | solution.py:32
  30.4 0.1 shard_map.110.rest_0_.element_ref
  30.5 0.5 %collective-permute-start.6 = (f32[4,40,128]{2,1,0:T(8,128)S(1)}, f32[4,40,128]{2,1,0:T(8,128)S(1)}, u32[]{:S(2)}, u32[]{:S(2)}) collective-permute-start(f32[4,40,128]{2,1,0:T(8,128)S(1)} %shard_map.111), channel_id=1, source_target_pairs={{0,128},{1,129},{2,130},{3,131},{4,132},{5,133},{6,134},{7,135},{8... | collective-permute-start | bytes 245768 | tf_op jit(solution)/shard_map/ppermute | solution.py:32
  31.0 0.0 collective-permute-done.8.both_ref.near_ref
  31.0 1.7 %collective-permute-done.7.first_ref.far_ref = f32[4,40,128]{2,1,0:T(8,128)S(1)} collective-permute-done((f32[4,40,128]{2,1,0:T(8,128)S(1)}, f32[4,40,128]{2,1,0:T(8,128)S(1)}, u32[]{:S(2)}, u32[]{:S(2)}) %collective-permute-start.7) | collective-permute-done | bytes 81952 | tf_op jit(solution)/shard_map/ppermute | solution.py:32
  32.7 1.6 %collective-permute-start.9 = (f32[4,40,128]{2,1,0:T(8,128)S(1)}, f32[4,40,128]{2,1,0:T(8,128)S(1)}, u32[]{:S(2)}, u32[]{:S(2)}) collective-permute-start(f32[4,40,128]{2,1,0:T(8,128)S(1)} %shard_map.113), channel_id=1, source_target_pairs={{0,64},{1,65},{2,66},{3,67},{4,68},{5,69},{6,70},{7,71},{8,72},{9,... | collective-permute-start | bytes 245768 | tf_op jit(solution)/shard_map/ppermute | solution.py:32
  34.3 0.0 collective-permute-done.6.chip_ref
  34.3 0.9 %collective-permute-done.9.passed_ref = f32[4,40,128]{2,1,0:T(8,128)S(1)} collective-permute-done((f32[4,40,128]{2,1,0:T(8,128)S(1)}, f32[4,40,128]{2,1,0:T(8,128)S(1)}, u32[]{:S(2)}, u32[]{:S(2)}) %collective-permute-start.9) | collective-permute-done | bytes 81952 | tf_op jit(solution)/shard_map/ppermute | solution.py:32
  35.2 1.5 %shard_map.114 = (f32[2,40,128]{2,1,0:T(8,128)}, f32[2,40,128]{2,1,0:T(8,128)}) custom-call(s32[1,1]{1,0:T(1,128)} %bitcast.7.counts_ref, bf16[128,768]{1,0:T(8,128)(2,1)S(1)} %get-tuple-element.8.owned_ref, s32[6,128]{1,0:T(8,128)S(1)} %bitcast.9, s32[6,128]{1,0:T(8,128)S(1)} %bitcast.11, s32[6,128]{1,0:T(8,128)S(1)} %bitcast.13, f32[8,128]{1,0:T(8,128)S(1)} %copy-done.3, ...), custom_call_target="tpu_custom_call" | custom-call | flops 2457600 | bytes 2457600 | tf_op jit(solution)/shard_map/pallas_call | solution.py:444
  (7 shorter events, 0.0 us)
Async XLA Ops:
  0.6 19.4 %copy-start = (s32[768]{0:T(1024)S(1)}, s32[768]{0:T(1024)}, u32[]{:S(2)}) copy-start(s32[768]{0:T(1024)} %param.15) | copy-start | bytes 9220
  0.6 19.4 %copy-start.1 = (s32[768]{0:T(1024)S(1)}, s32[768]{0:T(1024)}, u32[]{:S(2)}) copy-start(s32[768]{0:T(1024)} %param.16) | copy-start | bytes 9220
  0.7 19.4 %copy-start.2 = (s32[768]{0:T(1024)S(1)}, s32[768]{0:T(1024)}, u32[]{:S(2)}) copy-start(s32[768]{0:T(1024)} %param.17) | copy-start | bytes 9220
  0.7 19.4 %copy-start.3 = (f32[8,128]{1,0:T(8,128)S(1)}, f32[8,128]{1,0:T(8,128)}, u32[]{:S(2)}) copy-start(f32[8,128]{1,0:T(8,128)} %mass_ref.3) | copy-start | bytes 12292
  0.7 4.4 %collective-permute-start = (f32[2,40,128]{2,1,0:T(8,128)}, f32[2,40,128]{2,1,0:T(8,128)S(1)}, u32[]{:S(2)}, u32[]{:S(2)}) collective-permute-start(f32[2,40,128]{2,1,0:T(8,128)} %source_ref.1), channel_id=1, source_target_pairs={{0,64},{1,65},{2,66},{3,67},{4,68},{5,69},{6,70},{7,71},{8,72},{9,... | collective-permute-start | bytes 122888 | tf_op jit(solution)/shard_map/ppermute | solution.py:32
  5.1 13.1 %collective-permute-start.3 = (f32[4,40,128]{2,1,0:T(8,128)S(1)}, f32[4,40,128]{2,1,0:T(8,128)S(1)}, u32[]{:S(2)}, u32[]{:S(2)}) collective-permute-start(f32[4,40,128]{2,1,0:T(8,128)S(1)} %shard_map.105.both_ref), channel_id=1, source_target_pairs={{0,1},{1,0},{2,3},{3,2},{4,5},{5,4},{6,7},{7,6},{8,9},{9,8},{10,11... | collective-permute-start | bytes 245768 | tf_op jit(solution)/shard_map/ppermute | solution.py:32
  6.3 12.3 %collective-permute-start.2 = (f32[4,40,128]{2,1,0:T(8,128)S(1)}, f32[4,40,128]{2,1,0:T(8,128)S(1)}, u32[]{:S(2)}, u32[]{:S(2)}) collective-permute-start(f32[4,40,128]{2,1,0:T(8,128)S(1)} %shard_map.105.both_ref), channel_id=1, source_target_pairs={{0,63},{1,2},{2,1},{3,4},{4,3},{5,6},{6,5},{7,8},{8,7},{9,10},{10,... | collective-permute-start | bytes 245768 | tf_op jit(solution)/shard_map/ppermute | solution.py:32
  15.4 4.4 %collective-permute-start.1 = (f32[4,40,128]{2,1,0:T(8,128)S(1)}, f32[4,40,128]{2,1,0:T(8,128)S(1)}, u32[]{:S(2)}, u32[]{:S(2)}) collective-permute-start(f32[4,40,128]{2,1,0:T(8,128)S(1)} %shard_map.105.both_ref), channel_id=1, source_target_pairs={{0,128},{1,129},{2,130},{3,131},{4,132},{5,133},{6,134},{7,135},{8... | collective-permute-start | bytes 245768 | tf_op jit(solution)/shard_map/ppermute | solution.py:32
  18.7 1.3 %collective-permute-start.4 = (f32[4,40,128]{2,1,0:T(8,128)S(1)}, f32[4,40,128]{2,1,0:T(8,128)S(1)}, u32[]{:S(2)}, u32[]{:S(2)}) collective-permute-start(f32[4,40,128]{2,1,0:T(8,128)S(1)} %shard_map.108), channel_id=1, source_target_pairs={{0,64},{1,65},{2,66},{3,67},{4,68},{5,69},{6,70},{7,71},{8,72},{9,... | collective-permute-start | bytes 245768 | tf_op jit(solution)/shard_map/ppermute | solution.py:32
  20.9 1.3 %collective-permute-start.5 = (f32[2,40,128]{2,1,0:T(8,128)S(1)}, f32[2,40,128]{2,1,0:T(8,128)S(1)}, u32[]{:S(2)}, u32[]{:S(2)}) collective-permute-start(f32[2,40,128]{2,1,0:T(8,128)S(1)} %shard_map.109.vector_ref.first_ref.own_ref), channel_id=1, source_target_pairs={{0,64},{1,65},{2,66},{3,67},{4,68},{5,69},{6,70},{7,71},{8,72},{9,... | collective-permute-start | bytes 122888 | tf_op jit(solution)/shard_map/ppermute | solution.py:32
  22.2 8.8 %collective-permute-start.8 = (f32[4,40,128]{2,1,0:T(8,128)S(1)}, f32[4,40,128]{2,1,0:T(8,128)S(1)}, u32[]{:S(2)}, u32[]{:S(2)}) collective-permute-start(f32[4,40,128]{2,1,0:T(8,128)S(1)} %shard_map.111), channel_id=1, source_target_pairs={{0,1},{1,0},{2,3},{3,2},{4,5},{5,4},{6,7},{7,6},{8,9},{9,8},{10,11... | collective-permute-start | bytes 245768 | tf_op jit(solution)/shard_map/ppermute | solution.py:32
  22.2 10.5 %collective-permute-start.7 = (f32[4,40,128]{2,1,0:T(8,128)S(1)}, f32[4,40,128]{2,1,0:T(8,128)S(1)}, u32[]{:S(2)}, u32[]{:S(2)}) collective-permute-start(f32[4,40,128]{2,1,0:T(8,128)S(1)} %shard_map.111), channel_id=1, source_target_pairs={{0,63},{1,2},{2,1},{3,4},{4,3},{5,6},{6,5},{7,8},{8,7},{9,10},{10,... | collective-permute-start | bytes 245768 | tf_op jit(solution)/shard_map/ppermute | solution.py:32
  30.5 3.8 %collective-permute-start.6 = (f32[4,40,128]{2,1,0:T(8,128)S(1)}, f32[4,40,128]{2,1,0:T(8,128)S(1)}, u32[]{:S(2)}, u32[]{:S(2)}) collective-permute-start(f32[4,40,128]{2,1,0:T(8,128)S(1)} %shard_map.111), channel_id=1, source_target_pairs={{0,128},{1,129},{2,130},{3,131},{4,132},{5,133},{6,134},{7,135},{8... | collective-permute-start | bytes 245768 | tf_op jit(solution)/shard_map/ppermute | solution.py:32
  32.7 2.5 %collective-permute-start.9 = (f32[4,40,128]{2,1,0:T(8,128)S(1)}, f32[4,40,128]{2,1,0:T(8,128)S(1)}, u32[]{:S(2)}, u32[]{:S(2)}) collective-permute-start(f32[4,40,128]{2,1,0:T(8,128)S(1)} %shard_map.113), channel_id=1, source_target_pairs={{0,64},{1,65},{2,66},{3,67},{4,68},{5,69},{6,70},{7,71},{8,72},{9,... | collective-permute-start | bytes 245768 | tf_op jit(solution)/shard_map/ppermute | solution.py:32
